TPU v7x, 32 devices: a whole 2x2x4 slice. The times are simulated.
32 devices in a mesh: grp: 8 (over z, core), shard: 4 (over y, x).
Axes of the slice: x: 2, y: 2, z: 4, core: 2. Of those that a mesh axis runs over, the one named last changes fastest.
Arguments:
- tokens: bfloat16 [64, 128, 2048], P(('grp', 'shard')), may hold values from -6 to 6
- cotangent: bfloat16 [64, 128, 2048], P(('grp', 'shard')), may hold values from -6 to 6
- lengths: int32 [64, 4], P('grp'), may hold values from 0 to 128, as said below
- dealing: int32 [64], P('grp'), may hold values from 0 to 63, as said below
- first_gain: bfloat16 [2048], P(('grp', 'shard')), may hold values from 0.5 to 1.5
- first_shift: bfloat16 [2048], P(('grp', 'shard')), may hold values from -3 to 3
- query_weight: bfloat16 [2048, 2048], P(('grp', 'shard')), may hold values from -0.125 to 0.125
- query_bias: bfloat16 [2048], P(('grp', 'shard')), may hold values from -3 to 3
- keyval_weight: bfloat16 [2048, 256], P(('grp', 'shard')), may hold values from -0.125 to 0.125
- value_bias: bfloat16 [128], P(('grp', 'shard')), may hold values from -3 to 3
- out_weight: bfloat16 [2048, 2048], P(('grp', 'shard')), may hold values from -0.375 to 0.375
- out_bias: bfloat16 [2048], P(('grp', 'shard')), may hold values from -3 to 3
- second_gain: bfloat16 [2048], P(('grp', 'shard')), may hold values from 0.5 to 1.5
- second_shift: bfloat16 [2048], P(('grp', 'shard')), may hold values from -3 to 3
- up_weight: bfloat16 [2048, 8192], P(('grp', 'shard')), may hold values from -0.125 to 0.125
- up_bias: bfloat16 [8192], P(('grp', 'shard')), may hold values from -3 to 3
- down_weight: bfloat16 [8192, 2048], P(('grp', 'shard')), may hold values from -0.0625 to 0.0625
- down_bias: bfloat16 [2048], P(('grp', 'shard')), may hold values from -3 to 3
Outputs:
- block_output: bfloat16 [64, 128, 2048], P(('grp', 'shard'))
- input_grad: bfloat16 [64, 128, 2048], P(('grp', 'shard'))
- first_gain_grad: float32 [2048], P('shard')
- first_shift_grad: float32 [2048], P('shard')
- query_weight_grad: float32 [2048, 2048], P('shard')
- query_bias_grad: float32 [2048], P('shard')
- keyval_weight_grad: float32 [2048, 256], P('shard')
- value_bias_grad: float32 [128], P('shard')
- out_weight_grad: float32 [2048, 2048], P('shard')
- out_bias_grad: float32 [2048], P('shard')
- second_gain_grad: float32 [2048], P('shard')
- second_shift_grad: float32 [2048], P('shard')
- up_weight_grad: float32 [2048, 8192], P('shard')
- up_bias_grad: float32 [8192], P('shard')
- down_weight_grad: float32 [8192, 2048], P('shard')
- down_bias_grad: float32 [2048], P('shard')
Inputs may be any that keep to these rules, and one draw needn't show every extreme that they name: The 4 lengths of a row sum to 102 or more and to 128 at most; positions after that sum are padding; a length may be 0; in every draw some row holds a single document of 128 tokens. dealing is a permutation of the rows, and dealing[j] lies in the same group of 8 rows as j (rows g * 8 to (g + 1) * 8 - 1).
All inputs are finite; a program needn't handle non-finite values.
Results may differ from a plain program's by a relative error of at most 0.019.
Values may be sent and summed in bfloat16 or wider, within the bound.
A program may use at most 448 MiB of HBM per device.

v0:
```python
from functools import partial

import jax
import jax.numpy as jnp
from jax import lax
from jax.sharding import PartitionSpec as P

HEADS = 16
HD = 128


EPS = 1e-05
NEGATIVE = -1e30


def layer_norm(values, gain, shift):
    centre = jnp.mean(values, axis=-1, keepdims=True)
    offset = values - centre
    spread = jnp.mean(offset * offset, axis=-1, keepdims=True)
    return offset * lax.rsqrt(spread + EPS) * gain + shift


def row_masks(lengths_row, length):
    doc_ends = jnp.cumsum(lengths_row)
    places = jnp.arange(length, dtype=jnp.int32)
    segment = jnp.sum((places[:, None] >= doc_ends[None, :]).astype(jnp.int32), axis=1)
    live_mask = (places < doc_ends[-1]).astype(jnp.float32)
    allowed = (segment[:, None] == segment[None, :]) & (places[None, :] <= places[:, None])
    return (live_mask, allowed)


def matmul_plain(left, right):
    return jnp.dot(left, right, preferred_element_type=jnp.float32)


def product_tn(left, right):
    return lax.dot_general(
        left, right, (((0,), (0,)), ((), ())), preferred_element_type=jnp.float32
    )


def product_nt(left, right):
    return lax.dot_general(
        left, right, (((1,), (1,)), ((), ())), preferred_element_type=jnp.float32
    )


def column_sum(values):
    return jnp.sum(values.astype(jnp.float32), axis=0)


def shards(
    tokens,
    cotangent,
    lengths,
    dealing,
    first_gain,
    first_shift,
    query_weight,
    query_bias,
    keyval_weight,
    value_bias,
    out_weight,
    out_bias,
    second_gain,
    second_shift,
    up_weight,
    up_bias,
    down_weight,
    down_bias,
):
    micro_count = tokens.shape[0]
    length = tokens.shape[1]
    width = tokens.shape[2]
    group_rows = dealing.shape[0]
    local_deal = dealing - lax.axis_index("grp") * group_rows
    own_rows = lax.axis_index("shard") * micro_count + jnp.arange(micro_count, dtype=jnp.int32)
    taken = jnp.take(local_deal, own_rows, axis=0)
    pooled = lax.all_gather(tokens, "shard", axis=0, tiled=True)
    dealt_tokens = jnp.take(pooled, taken, axis=0)
    dealt_lengths = jnp.take(lengths, taken, axis=0)
    gathered = (
        lax.all_gather(first_gain, ("grp", "shard"), axis=0, tiled=True),
        lax.all_gather(first_shift, ("grp", "shard"), axis=0, tiled=True),
        lax.all_gather(query_weight, ("grp", "shard"), axis=0, tiled=True),
        lax.all_gather(query_bias, ("grp", "shard"), axis=0, tiled=True),
        lax.all_gather(keyval_weight, ("grp", "shard"), axis=0, tiled=True),
        lax.all_gather(value_bias, ("grp", "shard"), axis=0, tiled=True),
        lax.all_gather(out_weight, ("grp", "shard"), axis=0, tiled=True),
        lax.all_gather(out_bias, ("grp", "shard"), axis=0, tiled=True),
        lax.all_gather(second_gain, ("grp", "shard"), axis=0, tiled=True),
        lax.all_gather(second_shift, ("grp", "shard"), axis=0, tiled=True),
        lax.all_gather(up_weight, ("grp", "shard"), axis=0, tiled=True),
        lax.all_gather(up_bias, ("grp", "shard"), axis=0, tiled=True),
        lax.all_gather(down_weight, ("grp", "shard"), axis=0, tiled=True),
        lax.all_gather(down_bias, ("grp", "shard"), axis=0, tiled=True),
    )
    accum = tuple((jnp.zeros(item.shape, jnp.float32) for item in gathered))
    scale = HD ** (-0.5)
    gelu_tanh = partial(jax.nn.gelu, approximate=True)
    outputs = []
    back_rows = []
    for micro in range(micro_count):
        (
            gain_one,
            shift_one,
            weight_query,
            bias_query,
            weight_keyval,
            bias_value,
            weight_out,
            bias_out,
            gain_two,
            shift_two,
            weight_up,
            bias_up,
            weight_down,
            bias_down,
        ) = gathered
        gain_one32 = gain_one.astype(jnp.float32)
        shift_one32 = shift_one.astype(jnp.float32)
        gain_two32 = gain_two.astype(jnp.float32)
        shift_two32 = shift_two.astype(jnp.float32)
        value_pad = jnp.concatenate([jnp.zeros((HD,), jnp.float32), bias_value.astype(jnp.float32)])
        live_mask, allowed = row_masks(dealt_lengths[micro], length)
        head_mask = jnp.repeat(allowed, HEADS, axis=0)
        inputs32 = dealt_tokens[micro].astype(jnp.float32)
        normed_low = layer_norm(inputs32, gain_one32, shift_one32).astype(jnp.bfloat16)
        queries = (matmul_plain(normed_low, weight_query) + bias_query.astype(jnp.float32)).astype(
            jnp.bfloat16
        )
        keyvals = (matmul_plain(normed_low, weight_keyval) + value_pad).astype(jnp.bfloat16)
        key_rows = keyvals[:, :HD]
        value_rows = keyvals[:, HD:]
        query_rows = queries.reshape(length * HEADS, HD)
        scores = jnp.where(head_mask, product_nt(query_rows, key_rows) * scale, NEGATIVE)
        top_score = jnp.max(scores, axis=1, keepdims=True)
        exp_scores = jnp.exp(scores - top_score)
        totals = jnp.sum(exp_scores, axis=1, keepdims=True)
        log_total = top_score + jnp.log(totals)
        probs_low = (exp_scores / totals).astype(jnp.bfloat16)
        attended = matmul_plain(probs_low, value_rows).reshape(length, width).astype(jnp.bfloat16)
        middle = inputs32 + matmul_plain(attended, weight_out) + bias_out.astype(jnp.float32)
        normed_two = layer_norm(middle, gain_two32, shift_two32).astype(jnp.bfloat16)
        hidden_pre = matmul_plain(normed_two, weight_up) + bias_up.astype(jnp.float32)
        activated = gelu_tanh(hidden_pre).astype(jnp.bfloat16)
        result = (
            middle + matmul_plain(activated, weight_down) + bias_down.astype(jnp.float32)
        ) * live_mask[:, None]
        outputs.append(result.astype(jnp.bfloat16))
        grad_out = cotangent[micro].astype(jnp.float32) * live_mask[:, None]
        grad_down = grad_out.astype(jnp.bfloat16)
        grad_act = product_nt(grad_down, weight_down)
        gelu_value, gelu_pull = jax.vjp(gelu_tanh, hidden_pre)
        grad_hidden = gelu_pull(grad_act)[0].astype(jnp.bfloat16)
        grad_normed_two = product_nt(grad_hidden, weight_up)
        norm_value, second_pull = jax.vjp(layer_norm, middle, gain_two32, shift_two32)
        grad_middle, grad_gain_two, grad_shift_two = second_pull(grad_normed_two)
        grad_middle = grad_middle + grad_out
        grad_branch = grad_middle.astype(jnp.bfloat16)
        grad_attended = (
            product_nt(grad_branch, weight_out).astype(jnp.bfloat16).reshape(length * HEADS, HD)
        )
        again = jnp.where(head_mask, product_nt(query_rows, key_rows) * scale, NEGATIVE)
        probs = jnp.exp(again - log_total)
        grad_probs = product_nt(grad_attended, value_rows)
        centre = jnp.sum(probs * grad_probs, axis=1, keepdims=True)
        grad_scores = (probs * (grad_probs - centre)).astype(jnp.bfloat16)
        grad_queries = (
            (matmul_plain(grad_scores, key_rows) * scale)
            .reshape(length, width)
            .astype(jnp.bfloat16)
        )
        grad_keys = product_tn(grad_scores, query_rows) * scale
        grad_values = product_tn(probs_low, grad_attended)
        grad_keyvals = jnp.concatenate([grad_keys, grad_values], axis=1).astype(jnp.bfloat16)
        grad_normed_one = product_nt(grad_queries, weight_query) + product_nt(
            grad_keyvals, weight_keyval
        )
        first_value, first_pull = jax.vjp(layer_norm, inputs32, gain_one32, shift_one32)
        grad_inputs, grad_gain_one, grad_shift_one = first_pull(grad_normed_one)
        back_rows.append((grad_inputs + grad_middle).astype(jnp.bfloat16))
        terms = (
            grad_gain_one,
            grad_shift_one,
            product_tn(normed_low, grad_queries),
            column_sum(grad_queries),
            product_tn(normed_low, grad_keyvals),
            column_sum(grad_keyvals[:, HD:]),
            product_tn(attended, grad_branch),
            column_sum(grad_branch),
            grad_gain_two,
            grad_shift_two,
            product_tn(normed_two, grad_hidden),
            column_sum(grad_hidden),
            product_tn(activated, grad_down),
            column_sum(grad_down),
        )
        accum = tuple((older + newer for older, newer in zip(accum, terms)))
    dealt_back = jnp.stack(back_rows)
    pooled_back = lax.all_gather(dealt_back, "shard", axis=0, tiled=True)
    matches = local_deal[:, None] == own_rows[None, :]
    source = jnp.sum(
        jnp.where(matches, jnp.arange(group_rows, dtype=jnp.int32)[:, None], 0), axis=0
    )
    grad_tokens = jnp.take(pooled_back, source, axis=0)
    slices = (
        lax.psum_scatter(
            accum[0].astype(jnp.bfloat16), "shard", scatter_dimension=0, tiled=True
        ).astype(jnp.float32),
        lax.psum_scatter(
            accum[1].astype(jnp.bfloat16), "shard", scatter_dimension=0, tiled=True
        ).astype(jnp.float32),
        lax.psum_scatter(
            accum[2].astype(jnp.bfloat16), "shard", scatter_dimension=0, tiled=True
        ).astype(jnp.float32),
        lax.psum_scatter(
            accum[3].astype(jnp.bfloat16), "shard", scatter_dimension=0, tiled=True
        ).astype(jnp.float32),
        lax.psum_scatter(
            accum[4].astype(jnp.bfloat16), "shard", scatter_dimension=0, tiled=True
        ).astype(jnp.float32),
        lax.psum_scatter(
            accum[5].astype(jnp.bfloat16), "shard", scatter_dimension=0, tiled=True
        ).astype(jnp.float32),
        lax.psum_scatter(
            accum[6].astype(jnp.bfloat16), "shard", scatter_dimension=0, tiled=True
        ).astype(jnp.float32),
        lax.psum_scatter(
            accum[7].astype(jnp.bfloat16), "shard", scatter_dimension=0, tiled=True
        ).astype(jnp.float32),
        lax.psum_scatter(
            accum[8].astype(jnp.bfloat16), "shard", scatter_dimension=0, tiled=True
        ).astype(jnp.float32),
        lax.psum_scatter(
            accum[9].astype(jnp.bfloat16), "shard", scatter_dimension=0, tiled=True
        ).astype(jnp.float32),
        lax.psum_scatter(
            accum[10].astype(jnp.bfloat16), "shard", scatter_dimension=0, tiled=True
        ).astype(jnp.float32),
        lax.psum_scatter(
            accum[11].astype(jnp.bfloat16), "shard", scatter_dimension=0, tiled=True
        ).astype(jnp.float32),
        lax.psum_scatter(
            accum[12].astype(jnp.bfloat16), "shard", scatter_dimension=0, tiled=True
        ).astype(jnp.float32),
        lax.psum_scatter(
            accum[13].astype(jnp.bfloat16), "shard", scatter_dimension=0, tiled=True
        ).astype(jnp.float32),
    )
    total = (
        lax.psum(slices[0].astype(jnp.bfloat16), "grp").astype(jnp.float32),
        lax.psum(slices[1].astype(jnp.bfloat16), "grp").astype(jnp.float32),
        lax.psum(slices[2].astype(jnp.bfloat16), "grp").astype(jnp.float32),
        lax.psum(slices[3].astype(jnp.bfloat16), "grp").astype(jnp.float32),
        lax.psum(slices[4].astype(jnp.bfloat16), "grp").astype(jnp.float32),
        lax.psum(slices[5].astype(jnp.bfloat16), "grp").astype(jnp.float32),
        lax.psum(slices[6].astype(jnp.bfloat16), "grp").astype(jnp.float32),
        lax.psum(slices[7].astype(jnp.bfloat16), "grp").astype(jnp.float32),
        lax.psum(slices[8].astype(jnp.bfloat16), "grp").astype(jnp.float32),
        lax.psum(slices[9].astype(jnp.bfloat16), "grp").astype(jnp.float32),
        lax.psum(slices[10].astype(jnp.bfloat16), "grp").astype(jnp.float32),
        lax.psum(slices[11].astype(jnp.bfloat16), "grp").astype(jnp.float32),
        lax.psum(slices[12].astype(jnp.bfloat16), "grp").astype(jnp.float32),
        lax.psum(slices[13].astype(jnp.bfloat16), "grp").astype(jnp.float32),
    )
    return (
        jnp.stack(outputs),
        grad_tokens,
        total[0],
        total[1],
        total[2],
        total[3],
        total[4],
        total[5],
        total[6],
        total[7],
        total[8],
        total[9],
        total[10],
        total[11],
        total[12],
        total[13],
    )


def solution(mesh):
    return jax.shard_map(
        shards,
        mesh=mesh,
        in_specs=(
            P(("grp", "shard"), None, None),
            P(("grp", "shard"), None, None),
            P("grp", None),
            P("grp"),
            P(("grp", "shard")),
            P(("grp", "shard")),
            P(("grp", "shard"), None),
            P(("grp", "shard")),
            P(("grp", "shard"), None),
            P(("grp", "shard")),
            P(("grp", "shard"), None),
            P(("grp", "shard")),
            P(("grp", "shard")),
            P(("grp", "shard")),
            P(("grp", "shard"), None),
            P(("grp", "shard")),
            P(("grp", "shard"), None),
            P(("grp", "shard")),
        ),
        out_specs=(
            P(("grp", "shard"), None, None),
            P(("grp", "shard"), None, None),
            P("shard"),
            P("shard"),
            P("shard", None),
            P("shard"),
            P("shard", None),
            P("shard"),
            P("shard", None),
            P("shard"),
            P("shard"),
            P("shard"),
            P("shard", None),
            P("shard"),
            P("shard", None),
            P("shard"),
        ),
        check_vma=False,
    )
```

profile of v0, /device:TPU:0, one launch (start us, length us, event | category | flops | bytes accessed | tf_op | source)
XLA Modules:
  0.0 2092.2 jit_solution(9293613585932900098)
XLA Ops:
  18.2 43.0 %all-reduce.20 = (bf16[2048]{0:T(1024)(128)(2,1)S(1)}, bf16[2048]{0:T(1024)(128)(2,1)S(1)}, bf16[2048]{0:T(1024)(128)(2,1)S(1)}, bf16[128]{0:T(256)(128)(2,1)S(1...) all-reduce(bf16[2048]{0:T(1024)(128)(2,1)S(1)} %dynamic-update-slic, ...), channel_id=1, replica_groups=mesh['grp'=8,'shard'=4] {'grp','shard'}, use_global_device_ids=true, to_apply=%add.3 | all-reduce | flops 14464 | bytes 57856
  61.2 66.1 %all-gather = bf16[32,1,256]{2,1,0:T(2,128)(2,1)S(1)} all-gather(bf16[1,1,256]{2,1,0:T(2,128)(2,1)S(1)} %reshape.422), channel_id=1, replica_groups=mesh['grp'=8,'shard'=4] {'grp','shard'}, dimensions={0}, use_global_device_ids=true | all-gather | bytes 16896 | tf_op jit(solution)/shard_map/all_gather | solution.py:94
  130.0 2.8 gather_fusion.2
  134.1 1.7 fusion.45
  135.8 1.6 fusion.46
  137.4 65.7 %all-gather.11.cloned.1.call-done = bf16[2048,2048]{1,0:T(8,128)(2,1)} async-done(((bf16[64,2048]{1,0:T(8,128)(2,1)}), bf16[2048,2048]{1,0:T(8,128)(2,1)}) %all-gather.11.cloned.1.call-update) | async-done | bytes 8388624 | tf_op jit(solution)/shard_map/all_gather | solution.py:85
  203.2 4.7 fusion.24
  208.1 4.9 fusion.23
  215.9 1.0 convert_element_type.349
  219.8 62.2 %all-gather.15.cloned.1.call-done = bf16[2048,2048]{1,0:T(8,128)(2,1)} async-done(((bf16[64,2048]{1,0:T(8,128)(2,1)}), bf16[2048,2048]{1,0:T(8,128)(2,1)}) %all-gather.15.cloned.1.call-update) | async-done | bytes 8388624 | tf_op jit(solution)/shard_map/all_gather | solution.py:89
  282.1 4.9 fusion.141
  287.9 1.5 fusion.143
  289.7 188.5 %all-gather.17.cloned.1.call-done = bf16[2048,8192]{1,0:T(8,128)(2,1)} async-done(((bf16[64,8192]{1,0:T(8,128)(2,1)}), bf16[2048,8192]{1,0:T(8,128)(2,1)}) %all-gather.17.cloned.1.call-update) | async-done | bytes 33554448 | tf_op jit(solution)/shard_map/all_gather | solution.py:93
  478.2 18.4 convolution_add_fusion.1
  496.6 17.3 convolution_add_fusion
  513.9 160.0 %all-gather.19.cloned.1.call-done = bf16[8192,2048]{1,0:T(8,128)(2,1)} async-done(((bf16[256,2048]{1,0:T(8,128)(2,1)}), bf16[8192,2048]{1,0:T(8,128)(2,1)}) %all-gather.19.cloned.1.call-update) | async-done | bytes 33554448 | tf_op jit(solution)/shard_map/all_gather | solution.py:95
  673.9 19.9 convert_reduce_fusion
  693.8 17.3 fusion.145
  711.1 19.7 convert_reduce_fusion.1
  730.8 20.3 multiply_reduce_fusion.1
  751.1 2.2 fusion.139
  753.5 2.0 convert_reduce_fusion.6
  756.3 7.1 convolution_convert_fusion.1
  763.4 2.1 reshape.368
  765.5 2.1 convert_reduce_fusion.11
  767.6 7.3 convolution_convert_fusion
  774.9 2.1 reshape.369
  777.0 2.3 convert_reduce_fusion.10
  779.3 1.7 multiply_reduce_fusion.2
  783.2 1.6 fusion.14
  785.3 9.8 fusion.147
  795.1 11.5 add_convert_fusion.2
  806.7 2.2 fusion.26
  808.9 2.0 copy.64
  810.9 2.1 convert_element_type.390
  813.0 2.2 fusion.25
  815.2 2.0 copy.61
  817.2 2.1 convert_element_type.380
  819.3 9.7 fusion.80
  829.0 12.2 add_convert_fusion.3
  841.5 27.6 %fusion.116 = f32[8192,2048]{1,0:T(8,128)} fusion(f32[128]{0:T(128)S(1)} %compare_convert_fusion.1, bf16[2,128,2048]{2,1,0:T(8,128)(2,1)} %param.21, f32[128,8192]{1,0:T(8,128)} %convolution_add_fusion.1), kind=kOutput, calls=%fused_computation.255 | convolution fusion | flops 4305190912 | bytes 71827968 | tf_op jit(solution)/shard_map/dot_general | solution.py:37
  869.1 37.4 %add_convert_fusion = bf16[8192,2048]{1,0:T(8,128)(2,1)} fusion(f32[8192,2048]{1,0:T(8,128)} %fusion.116, f32[128]{0:T(128)S(1)} %compare_convert_fusion, bf16[2,128,2048]{2,1,0:T(8,128)(2,1)} %param.21, f32[128,8192]{1,0:T(8,128)} %convolution_add_fusion), kind=kOutput, calls=%fused_computation.4 | convolution fusion | flops 4338745344 | bytes 105382400 | tf_op jit(solution)/shard_map/dot_general | solution.py:37
  907.2 26.4 %fusion.129 = f32[2048,8192]{1,0:T(8,128)} fusion(bf16[128,8192]{1,0:T(8,128)(2,1)} %get-tuple-element.109, f32[128,2048]{1,0:T(8,128)S(1)} %get-tuple-element.97, f32[2048]{0:T(1024)S(1)} %copy-done.33, f32[2048]{0:T(1024)S(1)} %convert_element_type.351, f32[128]{0:T(128)S(1)} %fusion.109, f32[128]{0:T(128)S(1)} %broadcast_multiply_fusion.2), kind=kOutput, calls=%fused_computation.260 | convolution fusion | flops 4296278016 | bytes 70272000 | tf_op jit(solution)/shard_map/dot_general | solution.py:37
  933.6 35.4 %add_convert_fusion.1 = bf16[2048,8192]{1,0:T(8,128)(2,1)} fusion(f32[2048,8192]{1,0:T(8,128)} %fusion.129, bf16[128,8192]{1,0:T(8,128)(2,1)} %get-tuple-element.111, f32[128,2048]{1,0:T(8,128)S(1)} %get-tuple-element.93, f32[128]{0:T(128)S(1)} %fusion.111, f32[128]{0:T(128)S(1)} %broadcast_multiply_fusion, f32[2048]{0:T(1024)S(1)} %copy-done.33, ...), kind=kOutput, calls=%fused_computation.5 | convolution fusion | flops 4329832448 | bytes 103826432 | tf_op jit(solution)/shard_map/dot_general | solution.py:37
  969.3 6.8 fusion.146
  976.7 6.5 fusion.144
  986.6 1.1 pad_maximum_fusion.1
  987.8 2.9 reduce-scatter.10.cloned.1.call-done
  990.7 291.9 %reduce-scatter.18.cloned.1.call-done = bf16[2048,2048]{1,0:T(8,128)(2,1)} async-done(((bf16[8192,2048]{1,0:T(8,128)(2,1)}), bf16[2048,2048]{1,0:T(8,128)(2,1)}) %reduce-scatter.18.cloned.1.call-update) | async-done | bytes 8388624
  1282.6 291.8 %reduce-scatter.16.cloned.1.call-done = bf16[512,8192]{1,0:T(8,128)(2,1)} async-done(((bf16[2048,8192]{1,0:T(8,128)(2,1)}), bf16[512,8192]{1,0:T(8,128)(2,1)}) %reduce-scatter.16.cloned.1.call-update) | async-done | bytes 8388624
  1577.9 1.1 convert_reduce_fusion.9
  1579.3 16.6 all-reduce.23
  1596.5 26.1 %all-reduce.21 = (bf16[512]{0:T(512)(128)(2,1)S(1)}, bf16[512]{0:T(512)(128)(2,1)S(1)}, bf16[512]{0:T(512)(128)(2,1)S(1)}, bf16[32]{0:T(256)(128)(2,1)S(1)}, bf1...) all-reduce(bf16[512]{0:T(512)(128)(2,1)S(1)} %dynamic-slice.1, ...), channel_id=1, replica_groups=mesh['grp'=8,'shard'=4] {'grp'}, use_global_device_ids=true, to_apply=%region_30.32 | all-reduce | flops 5664 | bytes 22656 | tf_op jit(solution)/shard_map/psum | solution.py:252
  1627.8 17.7 fusion.30
  1645.5 17.3 fusion.29
  1662.8 1.1 pad_maximum_fusion
  1663.9 2.9 gather_fusion.3
  1666.8 1.1 broadcast_select_fusion
  1667.9 385.0 %all-reduce.26.cloned.1.call-done = (bf16[512,2048]{1,0:T(8,128)(2,1)}, bf16[512,256]{1,0:T(8,128)(2,1)}, bf16[512,2048]{1,0:T(8,128)(2,1)}, bf16[512,8192]{1,0:T(8,128)(2,1)}, bf16[2048,2048]{1,0:T(8,128)(2,1)}) async-done(((bf16[512,2048]{1,0:T(8,128)(2,1)}, bf16[512,256]{1,0:T(8,128)(2,1)}, bf16[512,2048]{1,0:T(8,128)(2,1)}, bf16[512,8192]{1,0:T(8,128)(2,1)}, bf16[2048,2048]{1,0:T(8,128)(2,1)}), ...) | async-done | bytes 21233680 | tf_op jit(solution)/shard_map/psum | solution.py:254
  2052.9 1.9 convert_element_type.407
  2054.8 4.1 convert_element_type.401
  2058.9 2.5 convert_element_type.413
  2061.5 12.0 convert_element_type.423
  2073.5 11.7 convert_element_type.429
  (301 shorter events, 37.6 us)
Async XLA Ops:
  7.2 9.0 copy-start.61
  7.2 9.2 copy-start.62
  7.2 9.5 copy-start.63
  7.2 9.7 copy-start.64
  7.2 10.0 copy-start.65
  7.2 10.2 copy-start.66
  7.2 10.5 copy-start.67
  7.3 10.7 copy-start.68
  7.3 122.7 %all-gather.9.cloned.1.call-start = ((), (), s32[]{:S(2)}) async-start(), calls=%async_computation.5 | async-start | bytes 5242880 | tf_op jit(solution)/shard_map/all_gather | solution.py:79
  8.0 126.1 %all-gather.13.cloned.1.call-start = ((), (), s32[]{:S(2)}) async-start(), calls=%async_computation.7 | async-start | bytes 1081344 | tf_op jit(solution)/shard_map/all_gather | solution.py:87
  8.7 194.4 %all-gather.11.cloned.1.call-start = ((), (), s32[]{:S(2)}) async-start(), calls=%async_computation.6 | async-start | bytes 8650752 | tf_op jit(solution)/shard_map/all_gather | solution.py:85
  9.5 272.6 %all-gather.15.cloned.1.call-start = ((), (), s32[]{:S(2)}) async-start(), calls=%async_computation.8 | async-start | bytes 8650752 | tf_op jit(solution)/shard_map/all_gather | solution.py:89
  10.1 468.1 %all-gather.17.cloned.1.call-start = ((), (), s32[]{:S(2)}) async-start(), calls=%async_computation.9 | async-start | bytes 34603008 | tf_op jit(solution)/shard_map/all_gather | solution.py:93
  10.6 663.3 %all-gather.19.cloned.1.call-start = ((), (), s32[]{:S(2)}) async-start(), calls=%async_computation.10 | async-start | bytes 34603008 | tf_op jit(solution)/shard_map/all_gather | solution.py:95
  11.2 976.5 %reduce-scatter.12.cloned.1.call-start = ((), (), s32[]{:S(2)}) async-start(), calls=%async_computation.13 | async-start | bytes 1310720 | tf_op jit(solution)/shard_map/reduce_scatter | solution.py:220
  13.4 120.2 %copy-start = (s32[8]{0:T(128)}, s32[8]{0:T(128)S(1)}, u32[]{:S(2)}) copy-start(s32[8]{0:T(128)S(1)} %broadcast_subtract_fusion) | copy-start | bytes 100
  61.2 435.4 %copy-start.32 = (f32[2048]{0:T(1024)}, f32[2048]{0:T(1024)S(1)}, u32[]{:S(2)}) copy-start(f32[2048]{0:T(1024)S(1)} %convert_element_type.352) | copy-start | bytes 24580
  133.6 74.2 %copy-start.55 = (f32[128]{0:T(128)}, f32[128]{0:T(128)S(1)}, u32[]{:S(2)}) copy-start(f32[128]{0:T(128)S(1)} %get-tuple-element.36) | copy-start | bytes 1540
  208.1 8.8 copy-start.21
  213.3 4.0 copy-start.19
  219.8 67.2 %copy-start.17 = (bf16[128,2048]{1,0:T(8,128)(2,1)}, bf16[128,2048]{1,0:T(8,128)(2,1)S(1)}, u32[]{:S(2)}) copy-start(bf16[128,2048]{1,0:T(8,128)(2,1)S(1)} %convert_element_type.367) | copy-start | bytes 1572868
  282.1 5.8 copy-start.2
  282.1 5.8 copy-start.16
  751.1 2.3 copy-start.7
  753.4 2.1 copy-start.9
  753.4 2.1 copy-start.11
  753.4 10.0 copy-start.51
  753.4 9.9 copy-start.53
  767.6 15.0 copy-start.34
  777.0 4.0 copy-start.6
  777.0 4.3 copy-start.22
  777.0 4.6 copy-start.4
  777.0 4.7 copy-start.29
  779.3 3.9 copy-start.36
  781.3 1.9 copy-start.25
  784.8 203.0 %reduce-scatter.14.cloned.1.call-start = ((), (), s32[]{:S(2)}) async-start(), calls=%async_computation.14 | async-start | bytes 10485760 | tf_op jit(solution)/shard_map/reduce_scatter | solution.py:226
  785.3 9.8 copy-start.18
  785.3 9.8 copy-start.27
  806.7 184.1 %reduce-scatter.10.cloned.1.call-start = ((), (), s32[]{:S(2)}) async-start(), calls=%async_computation.12 | async-start | bytes 10485760 | tf_op jit(solution)/shard_map/reduce_scatter | solution.py:214
  819.3 9.8 copy-start.13
  841.2 441.4 %reduce-scatter.18.cloned.1.call-start = ((), (), s32[]{:S(2)}) async-start(), calls=%async_computation.16 | async-start | bytes 41943040
  906.5 667.8 %reduce-scatter.16.cloned.1.call-start = ((), (), s32[]{:S(2)}) async-start(), calls=%async_computation.15 | async-start | bytes 41943040
  969.0 7.1 copy-start.37
  969.0 7.1 copy-start.39
  969.0 694.8 %all-gather.21.cloned.1.call-start = ((), (), s32[]{:S(2)}) async-start(), calls=%async_computation.11 | async-start | bytes 5242880 | tf_op jit(solution)/shard_map/all_gather | solution.py:201
  969.3 6.9 copy-start.30
  969.3 7.3 copy-start.15
  976.7 6.5 copy-start.35
  976.7 6.5 copy-start.41
  987.7 1065.2 %all-reduce.26.cloned.1.call-start = ((), (), s32[]{:S(2)}) async-start(), calls=%async_computation.17 | async-start | bytes 42467328 | tf_op jit(solution)/shard_map/psum | solution.py:254
  1574.4 3.2 copy-start.50
  1574.4 3.2 copy-start.1
  1574.4 3.4 copy-start.14
  1574.4 4.7 copy-start.59
  1574.4 4.7 copy-start.60
  1574.4 4.7 copy-start.44
  1574.4 4.7 copy-start.45
  1574.4 4.7 copy-start.42
  1574.4 4.7 copy-start.43
  1574.4 4.7 copy-start.46
  1574.4 4.7 copy-start.47
  1574.4 4.8 copy-start.48
  1574.5 4.8 copy-start.49
  2052.9 6.1 copy-start.31
  (19 other events, 22.0 us)
Sparse Core Ops, SparseCore 0:
  9.9 56.8 all-gather.8
  69.9 53.7 all-gather.12
  126.5 76.5 all-gather.10
  205.9 76.1 all-gather.14
  284.8 193.3 all-gather.16
  480.9 192.9 all-gather.18
  784.9 25.8 reduce-scatter.11
  814.2 86.4 reduce-scatter.13
  904.3 86.3 reduce-scatter.9
  993.9 288.6 reduce-scatter.17
  1285.7 288.6 reduce-scatter.15
  1576.8 53.0 all-gather.20
  1633.4 419.4 all-reduce.25
where the time goes:
time: 2100 us; the launch traced here: 2090 us
  waiting for transfers between devices  1450 us (69%)
  matrix products  381 us (18%)
  blocking collectives  152 us (7%)
  other arithmetic  54.1 us (3%)
  local copies, waits for them, and re-layouts  34 us (2%)
    unnamed x15, waiting for transfers between devices  587 us
    psum x1, waiting for transfers between devices, shards(): lax.psum(slices[2].astype(jnp.bfloat16), 'grp').astype(jnp.float32)  385 us
    all_gather x1, waiting for transfers between devices, shards(): lax.all_gather(up_weight, ('grp', 'shard'), axis=0, tiled=True)  188 us
    dot_general x14, matrix products, product_tn(): lax.dot_general(left, right, (((0,), (0,)), ((), ())), preferred_element_...  177 us
    all_gather x1, waiting for transfers between devices, shards(): lax.all_gather(down_weight, ('grp', 'shard'), axis=0, tiled=True)  160 us
    dot_general x14, matrix products, product_nt(): lax.dot_general(left, right, (((1,), (1,)), ((), ())), preferred_element_...  109 us
    dot_general x14, matrix products, matmul_plain(): return jnp.dot(left, right, preferred_element_type=jnp.float32)  95 us
    all_gather x1, blocking collectives, shards(): lax.all_gather(up_bias, ('grp', 'shard'), axis=0, tiled=True)  66.1 us
  transfers between devices with their start and end apart: 13, of which 8 were waited for; matrix products, arithmetic and copies ran while one was open for 15% of the time, Pallas kernels for 0%

commit v1 on v0

v1 whole, which is shorter than its diff:
```python
from functools import partial

import jax
import jax.numpy as jnp
from jax import lax
from jax.sharding import PartitionSpec as P

HEADS = 16
HD = 128
EPS = 1e-05
NEGATIVE = -1e30
BF = jnp.bfloat16
F32 = jnp.float32


def mm(left, right):
    return jnp.dot(left, right, preferred_element_type=F32)


def mm_tn(left, right):
    return lax.dot_general(left, right, (((0,), (0,)), ((), ())), preferred_element_type=F32)


def mm_nt(left, right):
    return lax.dot_general(left, right, (((1,), (1,)), ((), ())), preferred_element_type=F32)


def normalize(values):
    centre = jnp.mean(values, axis=-1, keepdims=True)
    offset = values - centre
    spread = jnp.mean(offset * offset, axis=-1, keepdims=True)
    rate = lax.rsqrt(spread + EPS)
    return offset * rate, rate


def norm_back(grad, unit, rate, gain):
    e = grad * gain
    back = rate * (
        e - jnp.mean(e, axis=-1, keepdims=True) - unit * jnp.mean(e * unit, axis=-1, keepdims=True)
    )
    return back, jnp.sum(grad * unit, axis=0), jnp.sum(grad, axis=0)


def row_ends(lengths_row):
    docs = lengths_row.shape[0]
    at = jnp.arange(docs, dtype=jnp.int32)
    return jnp.sum(jnp.where(at[None, :] <= at[:, None], lengths_row[None, :], 0), axis=1)


def live(lengths_row, length):
    places = jnp.arange(length, dtype=jnp.int32)
    return (places < jnp.sum(lengths_row)).astype(F32)


def allowed_pairs(lengths_row, length):
    ends = row_ends(lengths_row)
    places = jnp.arange(length, dtype=jnp.int32)
    segment = jnp.sum((places[:, None] >= ends[None, :]).astype(jnp.int32), axis=1)
    return (segment[:, None] == segment[None, :]) & (places[None, :] <= places[:, None])


def flips(count, mask):
    return [(i, i ^ mask) for i in range(count)]


def cube_orders(count):
    order = list(range(count.bit_length() - 1))
    return order, order[::-1]


def cube_gather(halves, count, axis):
    orders = cube_orders(count)
    held = [{0: half} for half in halves]
    for step in range(len(orders[0])):
        for k in range(2):
            mask = 1 << orders[k][step]
            keys = sorted(held[k])
            pack = jnp.stack([held[k][q] for q in keys])
            got = lax.ppermute(pack, axis, flips(count, mask))
            for i, q in enumerate(keys):
                held[k][q ^ mask] = got[i]
    return held


def cube_scatter(blocks, count, axis):
    orders = cube_orders(count)
    held = [dict(b) for b in blocks]
    for step in range(len(orders[0])):
        for k in range(2):
            mask = 1 << orders[k][step]
            away = [q for q in sorted(held[k]) if q & mask]
            pack = jnp.stack([held[k].pop(q) for q in away])
            got = lax.ppermute(pack, axis, flips(count, mask))
            for i, q in enumerate(away):
                held[k][q ^ mask] = held[k][q ^ mask] + got[i]
    return held[0][0], held[1][0]


def line_stages(groups):
    chips = groups // 2
    both = lambda pairs: [(2 * a + c, 2 * b + c) for a, b in pairs for c in range(2)]
    stages = []
    for hop in range(1, chips // 2):
        stages.append(("in", both([(hop - 1, hop), (chips - hop, chips - 1 - hop)]), None))
    low, high = chips // 2 - 1, chips // 2
    stages.append(("in", both([(low, high), (high, low)]), None))
    for hop in range(1, chips // 2):
        a, b = low + 1 - hop, high - 1 + hop
        stages.append(("out", both([(a, a - 1), (b, b + 1)]), (a - 1, b + 1)))
    return stages


def line_sum(chunks, groups, axis):
    stages = line_stages(groups)
    place = lax.axis_index(axis) // 2
    state = [None] * len(chunks)
    last = ()
    for turn in range(len(chunks) + len(stages) - 1):
        work = [k for k in range(len(chunks)) if 0 <= turn - k < len(stages)]
        sends = [chunks[k] if turn == k else state[k] for k in work]
        if last:
            tied = lax.optimization_barrier(tuple(sends) + last)
            sends = tied[: len(sends)]
        got = []
        for k, send in zip(work, sends):
            kind, pairs, ends = stages[turn - k]
            arrived = lax.ppermute(send, axis, pairs)
            got.append(arrived)
            if kind == "in":
                state[k] = send + arrived
            else:
                state[k] = jnp.where((place == ends[0]) | (place == ends[1]), arrived, send)
        last = tuple(got)
    return state


def shards(
    groups,
    count,
    tokens,
    cotangent,
    lengths,
    dealing,
    first_gain,
    first_shift,
    query_weight,
    query_bias,
    keyval_weight,
    value_bias,
    out_weight,
    out_bias,
    second_gain,
    second_shift,
    up_weight,
    up_bias,
    down_weight,
    down_bias,
):
    both = ("grp", "shard")
    micro, length, width = tokens.shape
    group_rows = dealing.shape[0]
    group = lax.axis_index("grp")
    me = lax.axis_index("shard")
    core = group % 2
    half = micro // 2
    block = down_weight.shape[0]
    hidden = block * groups
    rows = micro * length

    local_deal = dealing - group * group_rows
    steps = jnp.arange(group_rows, dtype=jnp.int32)
    inverse = jnp.sum(jnp.where(local_deal[:, None] == steps[None, :], steps[:, None], 0), axis=0)
    pick = lambda table, at: lax.dynamic_index_in_dim(table, at, 0, keepdims=False)

    small = (
        first_gain, first_shift, query_bias, value_bias, out_bias,
        second_gain, second_shift, up_bias, down_bias,
    )
    packed = lax.all_gather(jnp.concatenate(small), both, axis=0)
    wide = []
    at = 0
    for item in small:
        wide.append(packed[:, at : at + item.shape[0]].astype(F32))
        at += item.shape[0]
    up_part = pick(wide[7].reshape(groups, count, block).swapaxes(0, 1), me).reshape(hidden)
    gain_one, shift_one, bias_query, bias_value, bias_out, gain_two, shift_two, _, bias_down = [
        item.reshape(-1) for item in wide
    ]

    weight_query = lax.all_gather(query_weight, both, axis=0, tiled=True)
    weight_keyval = lax.all_gather(keyval_weight, both, axis=0, tiled=True)
    weight_out = lax.all_gather(out_weight, both, axis=0, tiled=True)
    up_rows = up_weight.shape[0]
    up_cut = up_weight.reshape(up_rows, groups, count, block).transpose(2, 0, 1, 3)
    up_cut = lax.all_to_all(up_cut.reshape(count, up_rows, hidden), "shard", 0, 0)
    weight_up = lax.all_gather(up_cut.reshape(count * up_rows, hidden), "grp", axis=0, tiled=True)
    weight_down = lax.all_gather(down_weight, "grp", axis=0, tiled=True)

    def gather_rows(values, place_of):
        held = cube_gather((values[:half], values[half:]), count, "shard")
        out = jnp.zeros((group_rows, length, width), values.dtype)
        for q in range(count):
            for k in range(2):
                for i in range(half):
                    row = (me ^ q) * micro + k * half + i
                    out = lax.dynamic_update_slice(out, held[k][q][i][None], (place_of(row), 0, 0))
        return out.reshape(group_rows * length, width)

    def scatter_rows(values, place_of):
        blocks = []
        for k in range(2):
            terms = {}
            for q in range(count):
                terms[q] = jnp.stack(
                    [pick(values, place_of((me ^ q) * micro + k * half + i)) for i in range(half)]
                )
            blocks.append(terms)
        return jnp.concatenate(cube_scatter(blocks, count, "shard"))

    dealt_place = lambda row: pick(inverse, row)
    same_place = lambda row: row

    cot_rows = gather_rows(cotangent, same_place).reshape(group_rows, length, width)
    dealt_live = jnp.stack([live(pick(lengths, local_deal[j]), length) for j in range(group_rows)])
    grad_down = (cot_rows.astype(F32) * dealt_live[:, :, None]).astype(BF)
    own_live = jnp.stack([pick(dealt_live, me * micro + m) for m in range(micro)])

    scale = HD**-0.5
    own_lengths = [pick(lengths, me * micro + m) for m in range(micro)]
    inputs = tokens.astype(F32).reshape(rows, width)
    unit_one, rate_one = normalize(inputs)
    normed_one = (unit_one * gain_one + shift_one).astype(BF)
    queries = (mm(normed_one, weight_query) + bias_query).astype(BF)
    value_pad = jnp.concatenate([jnp.zeros((HD,), F32), bias_value])
    keyvals = (mm(normed_one, weight_keyval) + value_pad).astype(BF)
    kept = []
    attended = []
    for m in range(micro):
        mask = jnp.repeat(allowed_pairs(own_lengths[m], length), HEADS, axis=0)
        query_rows = queries[m * length : (m + 1) * length].reshape(length * HEADS, HD)
        key_rows = keyvals[m * length : (m + 1) * length, :HD]
        value_rows = keyvals[m * length : (m + 1) * length, HD:]
        scores = jnp.where(mask, mm_nt(query_rows, key_rows) * scale, NEGATIVE)
        top = jnp.max(scores, axis=1, keepdims=True)
        powers = jnp.exp(scores - top)
        totals = jnp.sum(powers, axis=1, keepdims=True)
        probs = powers / totals
        probs_low = probs.astype(BF)
        attended.append(mm(probs_low, value_rows).reshape(length, width).astype(BF))
        kept.append((mask, query_rows, key_rows, value_rows, top + jnp.log(totals), probs_low))
    attended = jnp.concatenate(attended)
    middle = inputs + mm(attended, weight_out) + bias_out
    unit_two, rate_two = normalize(middle)
    normed_two_own = (unit_two * gain_two + shift_two).astype(BF)

    normed_two = gather_rows(normed_two_own.reshape(micro, length, width), dealt_place)
    hidden_pre = mm(normed_two, weight_up) + up_part
    gelu_tanh = partial(jax.nn.gelu, approximate=True)
    activated_wide, gelu_pull = jax.vjp(gelu_tanh, hidden_pre)
    activated = activated_wide.astype(BF)
    grad_down = grad_down.reshape(group_rows * length, width)
    grad_hidden = gelu_pull(mm_nt(grad_down, weight_down))[0].astype(BF)
    grad_two = mm_nt(grad_hidden, weight_up).astype(BF).reshape(group_rows, length, width)
    grad_normed_two = scatter_rows(grad_two, dealt_place).astype(F32).reshape(rows, width)
    down_grad = mm_tn(activated, grad_down).astype(BF)
    up_grad = mm_tn(normed_two, grad_hidden).astype(BF)

    result = mm(activated, weight_down).astype(BF).reshape(group_rows, length, width)
    middle_rows = middle.reshape(micro, length, width)
    for m in range(micro):
        at = dealt_place(me * micro + m)
        row = (pick(result, at).astype(F32) + middle_rows[m]).astype(BF)
        result = lax.dynamic_update_slice(result, row[None], (at, 0, 0))
    result = scatter_rows(result, same_place).astype(F32)
    block_output = ((result + bias_down) * own_live[:, :, None]).astype(BF)

    pairs = flips(groups, 1)

    def pair_sum(values):
        mine = lax.dynamic_index_in_dim(values, core, 1, keepdims=False)
        other = lax.dynamic_index_in_dim(values, 1 - core, 1, keepdims=False)
        return mine + lax.ppermute(other, "grp", pairs)

    slab = hidden // count
    down_half = pair_sum(down_grad.reshape(count, 2, slab // 2, width))
    down_half = lax.all_to_all(down_half, "shard", 0, 0)
    up_half = pair_sum(up_grad.reshape(count, 2, width // count // 2, hidden))
    up_half = lax.all_to_all(up_half, "shard", 0, 0)

    own_cot = jnp.stack([pick(cot_rows, dealt_place(me * micro + m)) for m in range(micro)])
    given_live = jnp.stack([live(own_lengths[m], length) for m in range(micro)])
    grad_out = (own_cot.astype(F32) * given_live[:, :, None]).reshape(rows, width)
    down_bias_grad = jnp.sum(grad_out.astype(BF).astype(F32), axis=0)
    back_two, gain_two_grad, shift_two_grad = norm_back(grad_normed_two, unit_two, rate_two, gain_two)
    grad_middle = back_two + grad_out
    grad_branch = grad_middle.astype(BF)
    out_bias_grad = jnp.sum(grad_branch.astype(F32), axis=0)
    out_grad = mm_tn(attended, grad_branch).astype(BF)
    grad_attended = mm_nt(grad_branch, weight_out).astype(BF)
    grad_queries = []
    grad_keyvals = []
    for m in range(micro):
        mask, query_rows, key_rows, value_rows, log_total, probs_low = kept[m]
        grad_rows = grad_attended[m * length : (m + 1) * length].reshape(length * HEADS, HD)
        again = jnp.where(mask, mm_nt(query_rows, key_rows) * scale, NEGATIVE)
        probs = jnp.exp(again - log_total)
        grad_probs = mm_nt(grad_rows, value_rows)
        centre = jnp.sum(probs * grad_probs, axis=1, keepdims=True)
        grad_scores = (probs * (grad_probs - centre)).astype(BF)
        grad_queries.append((mm(grad_scores, key_rows) * scale).reshape(length, width).astype(BF))
        grad_keys = mm_tn(grad_scores, query_rows) * scale
        grad_values = mm_tn(probs_low, grad_rows)
        grad_keyvals.append(jnp.concatenate([grad_keys, grad_values], axis=1).astype(BF))
    grad_queries = jnp.concatenate(grad_queries)
    grad_keyvals = jnp.concatenate(grad_keyvals)
    query_grad = mm_tn(normed_one, grad_queries).astype(BF)
    keyval_grad = mm_tn(normed_one, grad_keyvals).astype(BF)
    grad_normed_one = mm_nt(grad_queries, weight_query) + mm_nt(grad_keyvals, weight_keyval)
    back_one, gain_one_grad, shift_one_grad = norm_back(grad_normed_one, unit_one, rate_one, gain_one)
    input_grad = (back_one + grad_middle).astype(BF).reshape(micro, length, width)

    def slices(values):
        part = lax.psum_scatter(values, "shard", scatter_dimension=0, tiled=True)
        return pair_sum(part.reshape(1, 2, part.shape[0] // 2, part.shape[1]))[0]

    out_half, query_half, keyval_half = slices(out_grad), slices(query_grad), slices(keyval_grad)

    chunks = [down_half[q] for q in range(count)] + [up_half[q] for q in range(count)]
    chunks = chunks + [out_half, query_half, keyval_half]
    chunks = line_sum(chunks, groups, "grp")

    def whole(halves):
        other = lax.ppermute(halves, "grp", pairs)
        first = jnp.where(core == 0, halves, other)
        second = jnp.where(core == 0, other, halves)
        return jnp.stack([first, second]).astype(F32)

    down_full = whole(jnp.stack(chunks[:count]))
    per = groups // count
    down_full = down_full.transpose(1, 0, 2, 3).reshape(count, per, block, width)
    down_full = down_full.transpose(1, 0, 2, 3).reshape(per * count * block, width)
    up_full = whole(jnp.stack(chunks[count : 2 * count]))
    up_full = up_full.reshape(2, count, width // count // 2, groups, block)
    up_full = up_full.transpose(0, 2, 3, 1, 4).reshape(width // count, groups * count * block)
    tail = chunks[2 * count :]
    out_full, query_full, keyval_full = [
        whole(item).reshape(2 * item.shape[0], item.shape[1]) for item in tail
    ]

    up_bias_part = jnp.sum(grad_hidden.astype(F32), axis=0).reshape(groups, 1, block)
    value_bias_grad = jnp.sum(grad_keyvals[:, HD:].astype(F32), axis=0)
    query_bias_grad = jnp.sum(grad_queries.astype(F32), axis=0)
    spot = (jnp.arange(count, dtype=jnp.int32) == me)[None, :, None]
    up_bias_grad = jnp.where(spot, up_bias_part, 0.0).reshape(-1)
    vectors = (
        gain_one_grad, shift_one_grad, query_bias_grad, value_bias_grad, out_bias_grad,
        gain_two_grad, shift_two_grad, up_bias_grad, down_bias_grad,
    )
    summed = lax.psum(jnp.concatenate(vectors), both)
    parts = []
    at = 0
    for item in vectors:
        size = item.shape[0] // count
        parts.append(lax.dynamic_slice(summed, (at + me * size,), (size,)))
        at += item.shape[0]

    return (
        block_output, input_grad, parts[0], parts[1], query_full, parts[2], keyval_full, parts[3],
        out_full, parts[4], parts[5], parts[6], up_full, parts[7], down_full, parts[8],
    )


def solution(mesh):
    rows = P(("grp", "shard"), None, None)
    flat = P(("grp", "shard"))
    tall = P(("grp", "shard"), None)
    vector, matrix = P("shard"), P("shard", None)
    return jax.shard_map(
        partial(shards, mesh.shape["grp"], mesh.shape["shard"]),
        mesh=mesh,
        in_specs=(
            rows, rows, P("grp", None), P("grp"), flat, flat, tall, flat, tall, flat,
            tall, flat, flat, flat, tall, flat, tall, flat,
        ),
        out_specs=(
            rows, rows, vector, vector, matrix, vector, matrix, vector,
            matrix, vector, vector, vector, matrix, vector, matrix, vector,
        ),
        check_vma=False,
    )
```

time: 2100 us -> 1120 us (0.53)
  waiting for transfers between devices: 1450 us -> 490 us
  matrix products: 381 us -> 140 us
  starting transfers between devices: 1.31 us -> 117 us
  blocking collectives: 152 us -> 60.5 us
  other arithmetic: 54.1 us -> 140 us
  local copies, waits for them, and re-layouts: 34 us -> 115 us
  between operations: 17.7 us -> 47.4 us
    unnamed x15 -> x9, waiting for transfers between devices: 587 us -> 2.16 us
    psum x1, waiting for transfers between devices: 385 us -> 0.01 us  [shards(): summed = lax.psum(jnp.concatenate(vectors), both)]
    all_gather x7 -> x5, waiting for transfers between devices: 476 us -> 152 us  [the longest x1 67.6 us: shards(): weight_down = lax.all_gather(down_weight, 'grp', axis=0, tiled=True)]
    ppermute x0 -> x59, waiting for transfers between devices: none -> 280 us  [the longest x33 152 us: line_sum(): arrived = lax.ppermute(send, axis, pairs)]
    dot_general x42 -> x27, matrix products: 381 us -> 140 us  [the longest x9 47.3 us: mm(): return jnp.dot(left, right, preferred_element_type=F32)]
    ppermute x0 -> x59, starting transfers between devices: none -> 106 us  [the longest x33 75 us: line_sum(): arrived = lax.ppermute(send, axis, pairs)]
    all_gather x1 -> x0, blocking collectives: 66.1 us -> none  [shards(): lax.all_gather(up_bias, ('grp', 'shard'), axis=0, tiled=True)]
    add x3 -> x31, other arithmetic: 0.02 us -> 50.5 us  [the longest x22 33.4 us: line_sum(): state[k] = send + arrived]
  transfers between devices with their start and end apart: 13 -> 70, of which waited for: 8 -> 33; matrix products, arithmetic and copies ran while one was open for 15% -> 26% of each run, Pallas kernels for 0% -> 0%
where the time goes in v1:
time: 1120 us; the launch traced here: 1110 us
  waiting for transfers between devices  490 us (44%)
  other arithmetic  140 us (12%)
  matrix products  140 us (12%)
  starting transfers between devices  117 us (10%)
  local copies, waits for them, and re-layouts  115 us (10%)
  blocking collectives  60.5 us (5%)
  between operations  47.4 us (4%)
    ppermute x33, waiting for transfers between devices, line_sum(): arrived = lax.ppermute(send, axis, pairs)  152 us
    ppermute x33, starting transfers between devices, line_sum(): arrived = lax.ppermute(send, axis, pairs)  75 us
    ppermute x8, waiting for transfers between devices, cube_scatter(): got = lax.ppermute(pack, axis, flips(count, mask))  73 us
    all_gather x1, waiting for transfers between devices, shards(): weight_down = lax.all_gather(down_weight, 'grp', axis=0, tiled=True)  67.6 us
    all_gather x1, waiting for transfers between devices, shards(): weight_out = lax.all_gather(out_weight, both, axis=0, tiled=True)  58.7 us
    ppermute x8, waiting for transfers between devices, cube_gather(): got = lax.ppermute(pack, axis, flips(count, mask))  54.7 us
    dot_general x9, matrix products, mm(): return jnp.dot(left, right, preferred_element_type=F32)  47.3 us
    dot_general x9, matrix products, mm_tn(): lax.dot_general(left, right, (((0,), (0,)), ((), ())), preferred_element_...  46.9 us
  transfers between devices with their start and end apart: 70, of which 33 were waited for; matrix products, arithmetic and copies ran while one was open for 26% of the time, Pallas kernels for 0%

profile of v1, /device:TPU:0, one launch (start us, length us, event | category | flops | bytes accessed | tf_op | source)
XLA Modules:
  0.0 1110.3 jit_solution(17751939054827005021)
XLA Ops:
  12.0 19.6 %all_to_all.15 = bf16[4,64,2048]{2,1,0:T(8,128)(2,1)} all-to-all(bf16[4,64,2048]{2,1,0:T(8,128)(2,1)S(1)} %reshape.406), channel_id=1, replica_groups=mesh['grp'=8,'shard'=4] {'shard'}, dimensions={0} | all-to-all | bytes 2097152 | tf_op jit(solution)/shard_map/all_to_all | solution.py:195
  49.4 40.9 %all-reduce.1 = bf16[22656]{0:T(1024)(128)(2,1)S(1)} all-reduce(bf16[22656]{0:T(1024)(128)(2,1)S(1)} %dynamic-update-slice), channel_id=2, replica_groups=mesh['grp'=8,'shard'=4] {'grp','shard'}, use_global_device_ids=true, to_apply=%add.1 | all-reduce | flops 22656 | bytes 90624
  132.3 25.0 %collective-permute-done.10 = bf16[2,1,128,2048]{3,2,1,0:T(8,128)(2,1)} collective-permute-done((bf16[2,1,128,2048]{3,2,1,0:T(8,128)(2,1)S(1)}, bf16[2,1,128,2048]{3,2,1,0:T(8,128)(2,1)}, u32[]{:S(2)}, u32[]{:S(2)}) %collective-permute-start.10) | collective-permute-done | bytes 1048608 | tf_op jit(solution)/shard_map/ppermute | solution.py:79
  165.3 5.7 fusion.8
  182.3 58.7 %all-gather.11.cloned.1.call-done = bf16[2048,2048]{1,0:T(8,128)(2,1)} async-done(((bf16[64,2048]{1,0:T(8,128)(2,1)}), bf16[2048,2048]{1,0:T(8,128)(2,1)}) %all-gather.11.cloned.1.call-update) | async-done | bytes 8388624 | tf_op jit(solution)/shard_map/all_gather | solution.py:192
  241.1 6.4 fusion.100
  250.0 6.1 multiply_convert_fusion
  264.2 6.6 collective-permute-done
  273.3 19.2 %collective-permute-done.2 = bf16[2,1,128,2048]{3,2,1,0:T(8,128)(2,1)S(1)} collective-permute-done((bf16[2,1,128,2048]{3,2,1,0:T(8,128)(2,1)S(1)}, bf16[2,1,128,2048]{3,2,1,0:T(8,128)(2,1)S(1)}, u32[]{:S(2)}, u32[]{:S(2)}) %collective-permute-start.2) | collective-permute-done | bytes 1048608 | tf_op jit(solution)/shard_map/ppermute | solution.py:79
  297.8 25.3 %all-gather.13.cloned.1.call-done = bf16[2048,2048]{1,0:T(8,128)(2,1)} async-done(((bf16[256,2048]{1,0:T(8,128)(2,1)}), bf16[2048,2048]{1,0:T(8,128)(2,1)}) %all-gather.13.cloned.1.call-update) | async-done | bytes 8388624 | tf_op jit(solution)/shard_map/all_gather | solution.py:196
  323.2 14.5 %fusion.101 = f32[1024,2048]{1,0:T(8,128)} fusion(bf16[1024,2048]{1,0:T(8,128)(2,1)} %bitcast.23, bf16[2048,2048]{1,0:T(8,128)(2,1)} %all-gather.13.cloned.1.call-done), kind=kOutput, calls=%fused_computation.330 | convolution fusion | flops 8589934592 | bytes 20971520 | tf_op jit(solution)/shard_map/dot_general | solution.py:17
  337.7 67.6 %all-gather.15.cloned.1.call-done = bf16[2048,2048]{1,0:T(8,128)(2,1)} async-done(((bf16[256,2048]{1,0:T(8,128)(2,1)}), bf16[2048,2048]{1,0:T(8,128)(2,1)}) %all-gather.15.cloned.1.call-update) | async-done | bytes 8388624 | tf_op jit(solution)/shard_map/all_gather | solution.py:197
  405.3 18.8 %convert_reduce_fusion = (f32[2048]{0:T(1024)S(1)}, bf16[1024,2048]{1,0:T(8,128)(2,1)S(1)}) fusion(f32[1024,2048]{1,0:T(8,128)} %fusion.101, f32[2048]{0:T(1024)S(1)} %bitcast.401, bf16[1024,2048]{1,0:T(8,128)(2,1)} %bitcast.389, bf16[2048,2048]{1,0:T(8,128)(2,1)} %all-gather.15.cloned.1.call-done), kind=kOutput, calls=%fused_computation.12 | convolution fusion | flops 8638167040 | bytes 25182208 | tf_op jit(solution)/shard_map/dot_general | solution.py:25
  424.0 9.3 convolution_convert_fusion.4
  435.2 23.8 %collective-permute-done.12 = bf16[2,1,128,2048]{3,2,1,0:T(8,128)(2,1)S(1)} collective-permute-done((bf16[2,1,128,2048]{3,2,1,0:T(8,128)(2,1)S(1)}, bf16[2,1,128,2048]{3,2,1,0:T(8,128)(2,1)S(1)}, u32[]{:S(2)}, u32[]{:S(2)}) %collective-permute-start.12) | collective-permute-done | bytes 1048608 | tf_op jit(solution)/shard_map/ppermute | solution.py:93
  463.8 31.2 %collective-permute-done.13 = bf16[1,1,128,2048]{3,2,1,0:T(8,128)(2,1)S(1)} collective-permute-done((bf16[1,1,128,2048]{3,2,1,0:T(8,128)(2,1)S(1)}, bf16[1,1,128,2048]{3,2,1,0:T(8,128)(2,1)S(1)}, u32[]{:S(2)}, u32[]{:S(2)}) %collective-permute-start.13) | collective-permute-done | bytes 524320 | tf_op jit(solution)/shard_map/ppermute | solution.py:93
  497.0 10.6 collective-permute-done.15
  529.1 7.6 convolution_convert_fusion.1
  538.3 14.3 %convolution_convert_fusion.3 = bf16[2048,2048]{1,0:T(8,128)(2,1)S(1)} fusion(bf16[1024,2048]{1,0:T(8,128)(2,1)} %bitcast.390, f32[1024,2048]{1,0:T(8,128)} %fusion.101, f32[2048]{0:T(1024)S(1)} %bitcast.402), kind=kOutput, calls=%fused_computation.18 | convolution fusion | flops 8615100416 | bytes 20979712 | tf_op jit(solution)/shard_map/dot_general | solution.py:21
  564.4 6.6 fusion.102
  575.0 7.3 convolution_convert_fusion
  582.4 12.2 %convolution_convert_fusion.2 = bf16[2048,2048]{1,0:T(8,128)(2,1)S(1)} fusion(bf16[1024,2048]{1,0:T(8,128)(2,1)} %bitcast.23, bf16[1024,2048]{1,0:T(8,128)(2,1)} %copy-done.79), kind=kOutput, calls=%fused_computation.17 | convolution fusion | flops 8594128896 | bytes 16777216 | tf_op jit(solution)/shard_map/dot_general | solution.py:21
  599.5 6.2 bitcast_add_fusion.1
  605.6 5.0 all-to-all-start.1
  610.7 16.1 %convolution_convert_fusion.5 = bf16[1024,2048]{1,0:T(8,128)(2,1)} fusion(bf16[2048,2048]{1,0:T(8,128)(2,1)} %all-gather.15.cloned.1.call-done, f32[1024,2048]{1,0:T(8,128)} %fusion.101, f32[2048]{0:T(1024)S(1)} %bitcast.403), kind=kOutput, calls=%fused_computation.30 | convolution fusion | flops 8613003264 | bytes 20979712 | tf_op jit(solution)/shard_map/dot_general | solution.py:17
  630.7 42.6 %all-to-all-done.1 = bf16[4,256,2048]{2,1,0:T(8,128)(2,1)} async-done(((bf16[4,256,2048]{2,1,0:T(8,128)(2,1)}), bf16[4,256,2048]{2,1,0:T(8,128)(2,1)}, u32[]{:S(2)}, u32[]{:S(2)}) %all-to-all-start.1) | async-done | bytes 4194336 | tf_op jit(solution)/shard_map/all_to_all | solution.py:286
  673.3 4.0 slice_bitcast_fusion.4
  683.5 5.9 bitcast_add_fusion
  689.4 4.9 all-to-all-start.2
  694.3 5.9 collective-permute-done.17
  702.6 7.2 collective-permute-start.19
  712.9 16.2 %collective-permute-done.19 = bf16[256,2048]{1,0:T(8,128)(2,1)S(1)} collective-permute-done((bf16[256,2048]{1,0:T(8,128)(2,1)S(1)}, bf16[256,2048]{1,0:T(8,128)(2,1)S(1)}, u32[]{:S(2)}, u32[]{:S(2)}) %collective-permute-start.19) | collective-permute-done | bytes 1048608 | tf_op jit(solution)/shard_map/ppermute | solution.py:127
  731.3 6.6 collective-permute-start.21
  745.7 10.7 collective-permute-done.21
  766.9 7.4 collective-permute-done.5
  777.0 12.4 %collective-permute-start.7 = (bf16[1,1,128,2048]{3,2,1,0:T(8,128)(2,1)}, bf16[1,1,128,2048]{3,2,1,0:T(8,128)(2,1)}, u32[]{:S(2)}, u32[]{:S(2)}) collective-permute-start(bf16[1,1,128,2048]{3,2,1,0:T(8,128)(2,1)} %get-tuple-element.126), channel_id=1, source_target_pairs={{0,1},{1,0},{2,3},{3,2},{4,5},{5,4},{6,7},{7,6},{8,9},{9,8},{10,11... | collective-permute-start | bytes 1572872 | tf_op jit(solution)/shard_map/ppermute | solution.py:93
  789.4 4.1 slice_bitcast_fusion
  797.6 3.1 collective-permute-start.28
  805.3 17.9 %collective-permute-done.28 = bf16[256,2048]{1,0:T(8,128)(2,1)S(1)} collective-permute-done((bf16[256,2048]{1,0:T(8,128)(2,1)S(1)}, bf16[256,2048]{1,0:T(8,128)(2,1)S(1)}, u32[]{:S(2)}, u32[]{:S(2)}) %collective-permute-start.28) | collective-permute-done | bytes 1048608 | tf_op jit(solution)/shard_map/ppermute | solution.py:127
  823.6 3.8 collective-permute-done.29
  835.5 16.7 %collective-permute-done.31 = bf16[256,2048]{1,0:T(8,128)(2,1)S(1)} collective-permute-done((bf16[256,2048]{1,0:T(8,128)(2,1)S(1)}, bf16[256,2048]{1,0:T(8,128)(2,1)S(1)}, u32[]{:S(2)}, u32[]{:S(2)}) %collective-permute-start.31) | collective-permute-done | bytes 1048608 | tf_op jit(solution)/shard_map/ppermute | solution.py:127
  857.8 4.4 collective-permute-start.34
  873.8 7.3 collective-permute-done.34
  883.0 3.1 collective-permute-done.35
  887.8 4.1 collective-permute-start.37
  904.9 5.1 collective-permute-done.37
  910.0 3.1 add.601
  913.1 14.5 %reduce-scatter.6.cloned.1.call-done = bf16[512,2048]{1,0:T(8,128)(2,1)} async-done(((bf16[2048,2048]{1,0:T(8,128)(2,1)}), bf16[512,2048]{1,0:T(8,128)(2,1)}) %reduce-scatter.6.cloned.1.call-update) | async-done | bytes 2097168 | tf_op jit(solution)/shard_map/reduce_scatter | solution.py:323
  931.6 6.1 collective-permute-start.41
  946.7 13.7 %collective-permute-done.41 = bf16[256,2048]{1,0:T(8,128)(2,1)S(1)} collective-permute-done((bf16[256,2048]{1,0:T(8,128)(2,1)S(1)}, bf16[256,2048]{1,0:T(8,128)(2,1)S(1)}, u32[]{:S(2)}, u32[]{:S(2)}) %collective-permute-start.41) | collective-permute-done | bytes 1048608 | tf_op jit(solution)/shard_map/ppermute | solution.py:127
  966.4 3.8 collective-permute-start.45
  971.5 4.1 select_bitcast_fusion.1
  975.7 6.3 pad_maximum_fusion
  983.9 7.4 collective-permute-done.45
  993.3 3.2 collective-permute-done.47
  998.5 11.7 %bitcast_convert_fusion = f32[2048,2048]{1,0:T(8,128)} fusion(bf16[2,4,256,2048]{3,2,1,0:T(8,128)(2,1)} %pad_maximum_fusion), kind=kLoop, calls=%fused_computation.11 | loop fusion | flops 4194304 | bytes 25165824 | tf_op jit(solution)/shard_map/convert_element_type | solution.py:336
  1010.2 4.6 collective-permute-start.49
  1017.7 4.5 collective-permute-done.50
  1026.9 19.4 %collective-permute-done.51 = bf16[256,2048]{1,0:T(8,128)(2,1)S(1)} collective-permute-done((bf16[256,2048]{1,0:T(8,128)(2,1)S(1)}, bf16[256,2048]{1,0:T(8,128)(2,1)S(1)}, u32[]{:S(2)}, u32[]{:S(2)}) %collective-permute-start.51) | collective-permute-done | bytes 1048608 | tf_op jit(solution)/shard_map/ppermute | solution.py:127
  1048.2 6.1 collective-permute-done.54
  1063.7 5.4 copy.55
  1070.6 5.6 copy.54
  1076.1 6.9 convert_bitcast_fusion
  1083.0 20.6 %reshape.438 = f32[512,8192]{1,0:T(8,128)} reshape(f32[2,256,8,4,256]{4,3,2,1,0:T(4,128)} %convert_bitcast_fusion) | data formatting | bytes 33554432 | tf_op jit(solution)/shard_map/reshape | solution.py:344
  (491 shorter events, 258.0 us)
Async XLA Ops:
  7.2 156.4 %all-gather.9.cloned.1.call-start = ((), (), s32[]{:S(2)}) async-start(), calls=%async_computation.7 | async-start | bytes 1081344 | tf_op jit(solution)/shard_map/all_gather | solution.py:191
  7.9 157.4 %all-gather.7.cloned.1.call-start = ((), (), s32[]{:S(2)}) async-start(), calls=%async_computation.6 | async-start | bytes 8650752 | tf_op jit(solution)/shard_map/all_gather | solution.py:190
  8.7 232.4 %all-gather.11.cloned.1.call-start = ((), (), s32[]{:S(2)}) async-start(), calls=%async_computation.8 | async-start | bytes 8650752 | tf_op jit(solution)/shard_map/all_gather | solution.py:192
  9.4 313.8 %all-gather.13.cloned.1.call-start = ((), (), s32[]{:S(2)}) async-start(), calls=%async_computation.9 | async-start | bytes 9437184 | tf_op jit(solution)/shard_map/all_gather | solution.py:196
  31.6 373.7 %all-gather.15.cloned.1.call-start = ((), (), s32[]{:S(2)}) async-start(), calls=%async_computation.10 | async-start | bytes 9437184 | tf_op jit(solution)/shard_map/all_gather | solution.py:197
  36.3 92.4 %collective-permute-start.8 = (bf16[1,1,128,2048]{3,2,1,0:T(8,128)(2,1)}, bf16[1,1,128,2048]{3,2,1,0:T(8,128)(2,1)S(1)}, u32[]{:S(2)}, u32[]{:S(2)}) collective-permute-start(bf16[1,1,128,2048]{3,2,1,0:T(8,128)(2,1)} %get-tuple-element.139), channel_id=1, source_target_pairs={{0,1},{1,0},{2,3},{3,2},{4,5},{5,4},{6,7},{7,6},{8,9},{9,8},{10,11... | collective-permute-start | bytes 1572872 | tf_op jit(solution)/shard_map/ppermute | solution.py:79
  37.3 80.2 %collective-permute-start.9 = (bf16[1,1,128,2048]{3,2,1,0:T(8,128)(2,1)}, bf16[1,1,128,2048]{3,2,1,0:T(8,128)(2,1)S(1)}, u32[]{:S(2)}, u32[]{:S(2)}) collective-permute-start(bf16[1,1,128,2048]{3,2,1,0:T(8,128)(2,1)} %get-tuple-element.138), channel_id=1, source_target_pairs={{0,2},{1,3},{2,0},{3,1},{4,6},{5,7},{6,4},{7,5},{8,10},{9,11},{10,... | collective-permute-start | bytes 1572872 | tf_op jit(solution)/shard_map/ppermute | solution.py:79
  37.8 831.8 %reduce-scatter.8.cloned.1.call-start = ((), (), s32[]{:S(2)}) async-start(), calls=%async_computation.14 | async-start | bytes 1310720 | tf_op jit(solution)/shard_map/reduce_scatter | solution.py:323
  118.8 38.5 %collective-permute-start.10 = (bf16[2,1,128,2048]{3,2,1,0:T(8,128)(2,1)S(1)}, bf16[2,1,128,2048]{3,2,1,0:T(8,128)(2,1)}, u32[]{:S(2)}, u32[]{:S(2)}) collective-permute-start(bf16[2,1,128,2048]{3,2,1,0:T(8,128)(2,1)S(1)} %pad_maximum_fusion.9), channel_id=1, source_target_pairs={{0,1},{1,0},{2,3},{3,2},{4,5},{5,4},{6,7},{7,6},{8,9},{9,8},{10,11... | collective-permute-start | bytes 3145736 | tf_op jit(solution)/shard_map/ppermute | solution.py:79
  129.9 29.4 %collective-permute-start.11 = (bf16[2,1,128,2048]{3,2,1,0:T(8,128)(2,1)S(1)}, bf16[2,1,128,2048]{3,2,1,0:T(8,128)(2,1)S(1)}, u32[]{:S(2)}, u32[]{:S(2)}) collective-permute-start(bf16[2,1,128,2048]{3,2,1,0:T(8,128)(2,1)S(1)} %pad_maximum_fusion.10), channel_id=1, source_target_pairs={{0,2},{1,3},{2,0},{3,1},{4,6},{5,7},{6,4},{7,5},{8,10},{9,11},{10,... | collective-permute-start | bytes 3145736 | tf_op jit(solution)/shard_map/ppermute | solution.py:79
  248.4 14.2 %collective-permute-start.1 = (bf16[1,1,128,2048]{3,2,1,0:T(8,128)(2,1)S(1)}, bf16[1,1,128,2048]{3,2,1,0:T(8,128)(2,1)S(1)}, u32[]{:S(2)}, u32[]{:S(2)}) collective-permute-start(bf16[1,1,128,2048]{3,2,1,0:T(8,128)(2,1)S(1)} %get-tuple-element.141), channel_id=1, source_target_pairs={{0,2},{1,3},{2,0},{3,1},{4,6},{5,7},{6,4},{7,5},{8,10},{9,11},{10,... | collective-permute-start | bytes 1572872 | tf_op jit(solution)/shard_map/ppermute | solution.py:79
  256.0 14.8 %collective-permute-start = (bf16[1,1,128,2048]{3,2,1,0:T(8,128)(2,1)S(1)}, bf16[1,1,128,2048]{3,2,1,0:T(8,128)(2,1)S(1)}, u32[]{:S(2)}, u32[]{:S(2)}) collective-permute-start(bf16[1,1,128,2048]{3,2,1,0:T(8,128)(2,1)S(1)} %get-tuple-element.142), channel_id=1, source_target_pairs={{0,1},{1,0},{2,3},{3,2},{4,5},{5,4},{6,7},{7,6},{8,9},{9,8},{10,11... | collective-permute-start | bytes 1572872 | tf_op jit(solution)/shard_map/ppermute | solution.py:79
  262.7 29.7 %collective-permute-start.2 = (bf16[2,1,128,2048]{3,2,1,0:T(8,128)(2,1)S(1)}, bf16[2,1,128,2048]{3,2,1,0:T(8,128)(2,1)S(1)}, u32[]{:S(2)}, u32[]{:S(2)}) collective-permute-start(bf16[2,1,128,2048]{3,2,1,0:T(8,128)(2,1)S(1)} %pad_maximum_fusion.5), channel_id=1, source_target_pairs={{0,1},{1,0},{2,3},{3,2},{4,5},{5,4},{6,7},{7,6},{8,9},{9,8},{10,11... | collective-permute-start | bytes 3145736 | tf_op jit(solution)/shard_map/ppermute | solution.py:79
  270.9 23.6 %collective-permute-start.3 = (bf16[2,1,128,2048]{3,2,1,0:T(8,128)(2,1)S(1)}, bf16[2,1,128,2048]{3,2,1,0:T(8,128)(2,1)S(1)}, u32[]{:S(2)}, u32[]{:S(2)}) collective-permute-start(bf16[2,1,128,2048]{3,2,1,0:T(8,128)(2,1)S(1)} %pad_maximum_fusion.6), channel_id=1, source_target_pairs={{0,2},{1,3},{2,0},{3,1},{4,6},{5,7},{6,4},{7,5},{8,10},{9,11},{10,... | collective-permute-start | bytes 3145736 | tf_op jit(solution)/shard_map/ppermute | solution.py:79
  433.6 25.4 %collective-permute-start.12 = (bf16[2,1,128,2048]{3,2,1,0:T(8,128)(2,1)S(1)}, bf16[2,1,128,2048]{3,2,1,0:T(8,128)(2,1)S(1)}, u32[]{:S(2)}, u32[]{:S(2)}) collective-permute-start(bf16[2,1,128,2048]{3,2,1,0:T(8,128)(2,1)S(1)} %pad_maximum_fusion.11), channel_id=1, source_target_pairs={{0,1},{1,0},{2,3},{3,2},{4,5},{5,4},{6,7},{7,6},{8,9},{9,8},{10,11... | collective-permute-start | bytes 3145736 | tf_op jit(solution)/shard_map/ppermute | solution.py:93
  459.2 35.8 %collective-permute-start.14 = (bf16[2,1,128,2048]{3,2,1,0:T(8,128)(2,1)S(1)}, bf16[2,1,128,2048]{3,2,1,0:T(8,128)(2,1)S(1)}, u32[]{:S(2)}, u32[]{:S(2)}) collective-permute-start(bf16[2,1,128,2048]{3,2,1,0:T(8,128)(2,1)S(1)} %pad_maximum_fusion.12), channel_id=1, source_target_pairs={{0,2},{1,3},{2,0},{3,1},{4,6},{5,7},{6,4},{7,5},{8,10},{9,11},{10,... | collective-permute-start | bytes 3145736 | tf_op jit(solution)/shard_map/ppermute | solution.py:93
  460.8 34.2 %collective-permute-start.13 = (bf16[1,1,128,2048]{3,2,1,0:T(8,128)(2,1)S(1)}, bf16[1,1,128,2048]{3,2,1,0:T(8,128)(2,1)S(1)}, u32[]{:S(2)}, u32[]{:S(2)}) collective-permute-start(bf16[1,1,128,2048]{3,2,1,0:T(8,128)(2,1)S(1)} %get-tuple-element.118), channel_id=1, source_target_pairs={{0,2},{1,3},{2,0},{3,1},{4,6},{5,7},{6,4},{7,5},{8,10},{9,11},{10,... | collective-permute-start | bytes 1572872 | tf_op jit(solution)/shard_map/ppermute | solution.py:93
  495.2 12.4 %collective-permute-start.15 = (bf16[1,1,128,2048]{3,2,1,0:T(8,128)(2,1)S(1)}, bf16[1,1,128,2048]{3,2,1,0:T(8,128)(2,1)S(1)}, u32[]{:S(2)}, u32[]{:S(2)}) collective-permute-start(bf16[1,1,128,2048]{3,2,1,0:T(8,128)(2,1)S(1)} %get-tuple-element.117), channel_id=1, source_target_pairs={{0,1},{1,0},{2,3},{3,2},{4,5},{5,4},{6,7},{7,6},{8,9},{9,8},{10,11... | collective-permute-start | bytes 1572872 | tf_op jit(solution)/shard_map/ppermute | solution.py:93
  529.0 362.9 %reduce-scatter.4.cloned.1.call-start = ((), (), s32[]{:S(2)}) async-start(), calls=%async_computation.12 | async-start | bytes 10485760 | tf_op jit(solution)/shard_map/reduce_scatter | solution.py:323
  536.7 359.8 %all-reduce.4.cloned.1.call-start = ((), (), s32[]{:S(2)}) async-start(), calls=%async_computation.11 | async-start | bytes 188416 | tf_op jit(solution)/shard_map/psum | solution.py:359
  557.1 42.3 %collective-permute-start.16 = (bf16[4,256,2048]{2,1,0:T(8,128)(2,1)}, bf16[4,256,2048]{2,1,0:T(8,128)(2,1)}, u32[]{:S(2)}, u32[]{:S(2)}) collective-permute-start(bf16[4,256,2048]{2,1,0:T(8,128)(2,1)} %dynamic-slice_bitcast_fusion.1), channel_id=1, source_target_pairs={{0,4},{4,0},{8,12},{12,8},{16,20},{20,16},{24,28},{28,24},{1,5},{5... | collective-permute-start | bytes 12582920 | tf_op jit(solution)/shard_map/ppermute | solution.py:282
  574.6 353.0 %reduce-scatter.6.cloned.1.call-start = ((), (), s32[]{:S(2)}) async-start(), calls=%async_computation.13 | async-start | bytes 10485760 | tf_op jit(solution)/shard_map/reduce_scatter | solution.py:323
  599.2 84.3 %collective-permute-start.25 = (bf16[4,256,2048]{2,1,0:T(8,128)(2,1)}, bf16[4,256,2048]{2,1,0:T(8,128)(2,1)}, u32[]{:S(2)}, u32[]{:S(2)}) collective-permute-start(bf16[4,256,2048]{2,1,0:T(8,128)(2,1)} %dynamic-slice_bitcast_fusion), channel_id=1, source_target_pairs={{0,4},{4,0},{8,12},{12,8},{16,20},{20,16},{24,28},{28,24},{1,5},{5... | collective-permute-start | bytes 12582920 | tf_op jit(solution)/shard_map/ppermute | solution.py:282
  605.6 67.7 %all-to-all-start.1 = ((bf16[4,256,2048]{2,1,0:T(8,128)(2,1)}), bf16[4,256,2048]{2,1,0:T(8,128)(2,1)}, u32[]{:S(2)}, u32[]{:S(2)}) async-start(bf16[4,256,2048]{2,1,0:T(8,128)(2,1)} %bitcast_add_fusion.1), calls=%async_computation.1 | async-start | bytes 8388608 | tf_op jit(solution)/shard_map/all_to_all | solution.py:286
  677.3 22.9 %collective-permute-start.17 = (bf16[256,2048]{1,0:T(8,128)(2,1)}, bf16[256,2048]{1,0:T(8,128)(2,1)}, u32[]{:S(2)}, u32[]{:S(2)}) collective-permute-start(bf16[256,2048]{1,0:T(8,128)(2,1)} %get-tuple-element.115), channel_id=1, source_target_pairs={{0,8},{4,12},{24,16},{28,20},{1,9},{5,13},{25,17},{29,21},{2,10},{... | collective-permute-start | bytes 3145736 | tf_op jit(solution)/shard_map/ppermute | solution.py:127
  682.1 27.7 %collective-permute-start.4 = (bf16[2,1,128,2048]{3,2,1,0:T(8,128)(2,1)}, bf16[2,1,128,2048]{3,2,1,0:T(8,128)(2,1)S(1)}, u32[]{:S(2)}, u32[]{:S(2)}) collective-permute-start(bf16[2,1,128,2048]{3,2,1,0:T(8,128)(2,1)} %pad_maximum_fusion.7), channel_id=1, source_target_pairs={{0,1},{1,0},{2,3},{3,2},{4,5},{5,4},{6,7},{7,6},{8,9},{9,8},{10,11... | collective-permute-start | bytes 3145736 | tf_op jit(solution)/shard_map/ppermute | solution.py:93
  689.4 100.0 %all-to-all-start.2 = ((bf16[4,256,2048]{2,1,0:T(8,128)(2,1)}), bf16[4,256,2048]{2,1,0:T(8,128)(2,1)}, u32[]{:S(2)}, u32[]{:S(2)}) async-start(bf16[4,256,2048]{2,1,0:T(8,128)(2,1)} %bitcast_add_fusion), calls=%async_computation.2 | async-start | bytes 8388608 | tf_op jit(solution)/shard_map/all_to_all | solution.py:288
  701.8 10.6 collective-permute-start.18
  702.6 26.6 %collective-permute-start.19 = (bf16[256,2048]{1,0:T(8,128)(2,1)S(1)}, bf16[256,2048]{1,0:T(8,128)(2,1)S(1)}, u32[]{:S(2)}, u32[]{:S(2)}) collective-permute-start(bf16[256,2048]{1,0:T(8,128)(2,1)S(1)} %get-tuple-element.49), channel_id=1, source_target_pairs={{0,8},{4,12},{24,16},{28,20},{1,9},{5,13},{25,17},{29,21},{2,10},{... | collective-permute-start | bytes 3145736 | tf_op jit(solution)/shard_map/ppermute | solution.py:127
  729.6 13.5 %collective-permute-start.20 = (bf16[256,2048]{1,0:T(8,128)(2,1)S(1)}, bf16[256,2048]{1,0:T(8,128)(2,1)}, u32[]{:S(2)}, u32[]{:S(2)}) collective-permute-start(bf16[256,2048]{1,0:T(8,128)(2,1)S(1)} %add.588), channel_id=1, source_target_pairs={{8,16},{12,20},{16,8},{20,12},{9,17},{13,21},{17,9},{21,13},{10,18... | collective-permute-start | bytes 3145736 | tf_op jit(solution)/shard_map/ppermute | solution.py:127
  731.3 25.2 %collective-permute-start.21 = (bf16[256,2048]{1,0:T(8,128)(2,1)}, bf16[256,2048]{1,0:T(8,128)(2,1)}, u32[]{:S(2)}, u32[]{:S(2)}) collective-permute-start(bf16[256,2048]{1,0:T(8,128)(2,1)} %get-tuple-element.51), channel_id=1, source_target_pairs={{0,8},{4,12},{24,16},{28,20},{1,9},{5,13},{25,17},{29,21},{2,10},{... | collective-permute-start | bytes 3145736 | tf_op jit(solution)/shard_map/ppermute | solution.py:127
  737.9 23.4 %collective-permute-start.22 = (bf16[256,2048]{1,0:T(8,128)(2,1)S(1)}, bf16[256,2048]{1,0:T(8,128)(2,1)}, u32[]{:S(2)}, u32[]{:S(2)}) collective-permute-start(bf16[256,2048]{1,0:T(8,128)(2,1)S(1)} %add.587), channel_id=1, source_target_pairs={{8,0},{12,4},{16,24},{20,28},{9,1},{13,5},{17,25},{21,29},{10,2},{... | collective-permute-start | bytes 3145736 | tf_op jit(solution)/shard_map/ppermute | solution.py:127
  740.2 34.1 %collective-permute-start.6 = (bf16[2,1,128,2048]{3,2,1,0:T(8,128)(2,1)}, bf16[2,1,128,2048]{3,2,1,0:T(8,128)(2,1)}, u32[]{:S(2)}, u32[]{:S(2)}) collective-permute-start(bf16[2,1,128,2048]{3,2,1,0:T(8,128)(2,1)} %pad_maximum_fusion.8), channel_id=1, source_target_pairs={{0,2},{1,3},{2,0},{3,1},{4,6},{5,7},{6,4},{7,5},{8,10},{9,11},{10,... | collective-permute-start | bytes 3145736 | tf_op jit(solution)/shard_map/ppermute | solution.py:93
  741.8 32.6 %collective-permute-start.5 = (bf16[1,1,128,2048]{3,2,1,0:T(8,128)(2,1)}, bf16[1,1,128,2048]{3,2,1,0:T(8,128)(2,1)}, u32[]{:S(2)}, u32[]{:S(2)}) collective-permute-start(bf16[1,1,128,2048]{3,2,1,0:T(8,128)(2,1)} %get-tuple-element.127), channel_id=1, source_target_pairs={{0,2},{1,3},{2,0},{3,1},{4,6},{5,7},{6,4},{7,5},{8,10},{9,11},{10,... | collective-permute-start | bytes 1572872 | tf_op jit(solution)/shard_map/ppermute | solution.py:93
  761.3 32.2 %collective-permute-start.23 = (bf16[256,2048]{1,0:T(8,128)(2,1)S(1)}, bf16[256,2048]{1,0:T(8,128)(2,1)}, u32[]{:S(2)}, u32[]{:S(2)}) collective-permute-start(bf16[256,2048]{1,0:T(8,128)(2,1)S(1)} %add.590), channel_id=1, source_target_pairs={{8,16},{12,20},{16,8},{20,12},{9,17},{13,21},{17,9},{21,13},{10,18... | collective-permute-start | bytes 3145736 | tf_op jit(solution)/shard_map/ppermute | solution.py:127
  763.0 32.3 %collective-permute-start.24 = (bf16[256,2048]{1,0:T(8,128)(2,1)}, bf16[256,2048]{1,0:T(8,128)(2,1)S(1)}, u32[]{:S(2)}, u32[]{:S(2)}) collective-permute-start(bf16[256,2048]{1,0:T(8,128)(2,1)} %get-tuple-element.54), channel_id=1, source_target_pairs={{0,8},{4,12},{24,16},{28,20},{1,9},{5,13},{25,17},{29,21},{2,10},{... | collective-permute-start | bytes 3145736 | tf_op jit(solution)/shard_map/ppermute | solution.py:127
  765.6 31.2 %collective-permute-start.26 = (bf16[256,2048]{1,0:T(8,128)(2,1)}, bf16[256,2048]{1,0:T(8,128)(2,1)}, u32[]{:S(2)}, u32[]{:S(2)}) collective-permute-start(bf16[256,2048]{1,0:T(8,128)(2,1)} %add.589), channel_id=1, source_target_pairs={{8,0},{12,4},{16,24},{20,28},{9,1},{13,5},{17,25},{21,29},{10,2},{... | collective-permute-start | bytes 3145736 | tf_op jit(solution)/shard_map/ppermute | solution.py:127
  777.0 25.0 %collective-permute-start.7 = (bf16[1,1,128,2048]{3,2,1,0:T(8,128)(2,1)}, bf16[1,1,128,2048]{3,2,1,0:T(8,128)(2,1)}, u32[]{:S(2)}, u32[]{:S(2)}) collective-permute-start(bf16[1,1,128,2048]{3,2,1,0:T(8,128)(2,1)} %get-tuple-element.126), channel_id=1, source_target_pairs={{0,1},{1,0},{2,3},{3,2},{4,5},{5,4},{6,7},{7,6},{8,9},{9,8},{10,11... | collective-permute-start | bytes 1572872 | tf_op jit(solution)/shard_map/ppermute | solution.py:93
  797.6 25.6 %collective-permute-start.28 = (bf16[256,2048]{1,0:T(8,128)(2,1)S(1)}, bf16[256,2048]{1,0:T(8,128)(2,1)S(1)}, u32[]{:S(2)}, u32[]{:S(2)}) collective-permute-start(bf16[256,2048]{1,0:T(8,128)(2,1)S(1)} %get-tuple-element.57), channel_id=1, source_target_pairs={{0,8},{4,12},{24,16},{28,20},{1,9},{5,13},{25,17},{29,21},{2,10},{... | collective-permute-start | bytes 3145736 | tf_op jit(solution)/shard_map/ppermute | solution.py:127
  800.7 26.6 %collective-permute-start.29 = (bf16[256,2048]{1,0:T(8,128)(2,1)S(1)}, bf16[256,2048]{1,0:T(8,128)(2,1)S(1)}, u32[]{:S(2)}, u32[]{:S(2)}) collective-permute-start(bf16[256,2048]{1,0:T(8,128)(2,1)S(1)} %add.591), channel_id=1, source_target_pairs={{8,0},{12,4},{16,24},{20,28},{9,1},{13,5},{17,25},{21,29},{10,2},{... | collective-permute-start | bytes 3145736 | tf_op jit(solution)/shard_map/ppermute | solution.py:127
  828.1 24.0 %collective-permute-start.31 = (bf16[256,2048]{1,0:T(8,128)(2,1)S(1)}, bf16[256,2048]{1,0:T(8,128)(2,1)S(1)}, u32[]{:S(2)}, u32[]{:S(2)}) collective-permute-start(bf16[256,2048]{1,0:T(8,128)(2,1)S(1)} %get-tuple-element.60), channel_id=1, source_target_pairs={{0,8},{4,12},{24,16},{28,20},{1,9},{5,13},{25,17},{29,21},{2,10},{... | collective-permute-start | bytes 3145736 | tf_op jit(solution)/shard_map/ppermute | solution.py:127
  831.2 25.0 %collective-permute-start.32 = (bf16[256,2048]{1,0:T(8,128)(2,1)S(1)}, bf16[256,2048]{1,0:T(8,128)(2,1)S(1)}, u32[]{:S(2)}, u32[]{:S(2)}) collective-permute-start(bf16[256,2048]{1,0:T(8,128)(2,1)S(1)} %add.594), channel_id=1, source_target_pairs={{8,0},{12,4},{16,24},{20,28},{9,1},{13,5},{17,25},{21,29},{10,2},{... | collective-permute-start | bytes 3145736 | tf_op jit(solution)/shard_map/ppermute | solution.py:127
  856.2 14.5 %collective-permute-start.33 = (bf16[256,2048]{1,0:T(8,128)(2,1)}, bf16[256,2048]{1,0:T(8,128)(2,1)}, u32[]{:S(2)}, u32[]{:S(2)}) collective-permute-start(bf16[256,2048]{1,0:T(8,128)(2,1)} %add.597), channel_id=1, source_target_pairs={{8,16},{12,20},{16,8},{20,12},{9,17},{13,21},{17,9},{21,13},{10,18... | collective-permute-start | bytes 3145736 | tf_op jit(solution)/shard_map/ppermute | solution.py:127
  857.8 23.2 %collective-permute-start.34 = (bf16[256,2048]{1,0:T(8,128)(2,1)}, bf16[256,2048]{1,0:T(8,128)(2,1)}, u32[]{:S(2)}, u32[]{:S(2)}) collective-permute-start(bf16[256,2048]{1,0:T(8,128)(2,1)} %get-tuple-element.63), channel_id=1, source_target_pairs={{0,8},{4,12},{24,16},{28,20},{1,9},{5,13},{25,17},{29,21},{2,10},{... | collective-permute-start | bytes 3145736 | tf_op jit(solution)/shard_map/ppermute | solution.py:127
  862.2 24.0 %collective-permute-start.35 = (bf16[256,2048]{1,0:T(8,128)(2,1)}, bf16[256,2048]{1,0:T(8,128)(2,1)}, u32[]{:S(2)}, u32[]{:S(2)}) collective-permute-start(bf16[256,2048]{1,0:T(8,128)(2,1)} %add.596), channel_id=1, source_target_pairs={{8,0},{12,4},{16,24},{20,28},{9,1},{13,5},{17,25},{21,29},{10,2},{... | collective-permute-start | bytes 3145736 | tf_op jit(solution)/shard_map/ppermute | solution.py:127
  866.4 105.1 %collective-permute-start.58 = (bf16[4,256,2048]{2,1,0:T(8,128)(2,1)}, bf16[4,256,2048]{2,1,0:T(8,128)(2,1)}, u32[]{:S(2)}, u32[]{:S(2)}) collective-permute-start(bf16[4,256,2048]{2,1,0:T(8,128)(2,1)} %pad_maximum_fusion.2), channel_id=1, source_target_pairs={{0,4},{4,0},{8,12},{12,8},{16,20},{20,16},{24,28},{28,24},{1,5},{5... | collective-permute-start | bytes 12582920 | tf_op jit(solution)/shard_map/ppermute | solution.py:333
  870.6 28.6 %collective-permute-start.46 = (bf16[1,256,256]{2,1,0:T(8,128)(2,1)S(1)}, bf16[1,256,256]{2,1,0:T(8,128)(2,1)S(1)}, u32[]{:S(2)}, u32[]{:S(2)}) collective-permute-start(bf16[1,256,256]{2,1,0:T(8,128)(2,1)S(1)} %dynamic-slice_bitcast_fusion.12), channel_id=1, source_target_pairs={{0,4},{4,0},{8,12},{12,8},{16,20},{20,16},{24,28},{28,24},{1,5},{5... | collective-permute-start | bytes 393224 | tf_op jit(solution)/shard_map/ppermute | solution.py:282
  886.2 16.1 %collective-permute-start.36 = (bf16[256,2048]{1,0:T(8,128)(2,1)S(1)}, bf16[256,2048]{1,0:T(8,128)(2,1)}, u32[]{:S(2)}, u32[]{:S(2)}) collective-permute-start(bf16[256,2048]{1,0:T(8,128)(2,1)S(1)} %add.599), channel_id=1, source_target_pairs={{8,16},{12,20},{16,8},{20,12},{9,17},{13,21},{17,9},{21,13},{10,18... | collective-permute-start | bytes 3145736 | tf_op jit(solution)/shard_map/ppermute | solution.py:127
  887.8 22.2 %collective-permute-start.37 = (bf16[256,2048]{1,0:T(8,128)(2,1)}, bf16[256,2048]{1,0:T(8,128)(2,1)}, u32[]{:S(2)}, u32[]{:S(2)}) collective-permute-start(bf16[256,2048]{1,0:T(8,128)(2,1)} %get-tuple-element.66), channel_id=1, source_target_pairs={{0,8},{4,12},{24,16},{28,20},{1,9},{5,13},{25,17},{29,21},{2,10},{... | collective-permute-start | bytes 3145736 | tf_op jit(solution)/shard_map/ppermute | solution.py:127
  894.2 34.8 %collective-permute-start.38 = (bf16[1,256,2048]{2,1,0:T(8,128)(2,1)}, bf16[1,256,2048]{2,1,0:T(8,128)(2,1)}, u32[]{:S(2)}, u32[]{:S(2)}) collective-permute-start(bf16[1,256,2048]{2,1,0:T(8,128)(2,1)} %dynamic-slice_bitcast_fusion.3), channel_id=1, source_target_pairs={{0,4},{4,0},{8,12},{12,8},{16,20},{20,16},{24,28},{28,24},{1,5},{5... | collective-permute-start | bytes 3145736 | tf_op jit(solution)/shard_map/ppermute | solution.py:282
  899.2 31.7 %collective-permute-start.39 = (bf16[256,2048]{1,0:T(8,128)(2,1)}, bf16[256,2048]{1,0:T(8,128)(2,1)}, u32[]{:S(2)}, u32[]{:S(2)}) collective-permute-start(bf16[256,2048]{1,0:T(8,128)(2,1)} %add.598), channel_id=1, source_target_pairs={{8,0},{12,4},{16,24},{20,28},{9,1},{13,5},{17,25},{21,29},{10,2},{... | collective-permute-start | bytes 3145736 | tf_op jit(solution)/shard_map/ppermute | solution.py:127
  929.0 13.7 %collective-permute-start.42 = (bf16[1,256,2048]{2,1,0:T(8,128)(2,1)S(1)}, bf16[1,256,2048]{2,1,0:T(8,128)(2,1)S(1)}, u32[]{:S(2)}, u32[]{:S(2)}) collective-permute-start(bf16[1,256,2048]{2,1,0:T(8,128)(2,1)S(1)} %dynamic-slice_bitcast_fusion.2), channel_id=1, source_target_pairs={{0,4},{4,0},{8,12},{12,8},{16,20},{20,16},{24,28},{28,24},{1,5},{5... | collective-permute-start | bytes 3145736 | tf_op jit(solution)/shard_map/ppermute | solution.py:282
  930.9 12.9 %collective-permute-start.40 = (bf16[256,2048]{1,0:T(8,128)(2,1)}, bf16[256,2048]{1,0:T(8,128)(2,1)S(1)}, u32[]{:S(2)}, u32[]{:S(2)}) collective-permute-start(bf16[256,2048]{1,0:T(8,128)(2,1)} %add.601), channel_id=1, source_target_pairs={{8,16},{12,20},{16,8},{20,12},{9,17},{13,21},{17,9},{21,13},{10,18... | collective-permute-start | bytes 3145736 | tf_op jit(solution)/shard_map/ppermute | solution.py:127
  931.6 28.7 %collective-permute-start.41 = (bf16[256,2048]{1,0:T(8,128)(2,1)S(1)}, bf16[256,2048]{1,0:T(8,128)(2,1)S(1)}, u32[]{:S(2)}, u32[]{:S(2)}) collective-permute-start(bf16[256,2048]{1,0:T(8,128)(2,1)S(1)} %fusion.30), channel_id=1, source_target_pairs={{0,8},{4,12},{24,16},{28,20},{1,9},{5,13},{25,17},{29,21},{2,10},{... | collective-permute-start | bytes 3145736 | tf_op jit(solution)/shard_map/ppermute | solution.py:127
  937.8 27.0 %collective-permute-start.43 = (bf16[256,2048]{1,0:T(8,128)(2,1)}, bf16[256,2048]{1,0:T(8,128)(2,1)S(1)}, u32[]{:S(2)}, u32[]{:S(2)}) collective-permute-start(bf16[256,2048]{1,0:T(8,128)(2,1)} %add.600), channel_id=1, source_target_pairs={{8,0},{12,4},{16,24},{20,28},{9,1},{13,5},{17,25},{21,29},{10,2},{... | collective-permute-start | bytes 3145736 | tf_op jit(solution)/shard_map/ppermute | solution.py:127
  964.7 17.3 %collective-permute-start.44 = (bf16[256,2048]{1,0:T(8,128)(2,1)}, bf16[256,2048]{1,0:T(8,128)(2,1)}, u32[]{:S(2)}, u32[]{:S(2)}) collective-permute-start(bf16[256,2048]{1,0:T(8,128)(2,1)} %add.604), channel_id=1, source_target_pairs={{8,16},{12,20},{16,8},{20,12},{9,17},{13,21},{17,9},{21,13},{10,18... | collective-permute-start | bytes 3145736 | tf_op jit(solution)/shard_map/ppermute | solution.py:127
  966.4 24.9 %collective-permute-start.45 = (bf16[256,2048]{1,0:T(8,128)(2,1)}, bf16[256,2048]{1,0:T(8,128)(2,1)}, u32[]{:S(2)}, u32[]{:S(2)}) collective-permute-start(bf16[256,2048]{1,0:T(8,128)(2,1)} %fusion.29), channel_id=1, source_target_pairs={{0,8},{4,12},{24,16},{28,20},{1,9},{5,13},{25,17},{29,21},{2,10},{... | collective-permute-start | bytes 3145736 | tf_op jit(solution)/shard_map/ppermute | solution.py:127
  970.2 26.3 %collective-permute-start.47 = (bf16[256,2048]{1,0:T(8,128)(2,1)}, bf16[256,2048]{1,0:T(8,128)(2,1)}, u32[]{:S(2)}, u32[]{:S(2)}) collective-permute-start(bf16[256,2048]{1,0:T(8,128)(2,1)} %add.603), channel_id=1, source_target_pairs={{8,0},{12,4},{16,24},{20,28},{9,1},{13,5},{17,25},{21,29},{10,2},{... | collective-permute-start | bytes 3145736 | tf_op jit(solution)/shard_map/ppermute | solution.py:127
  996.5 20.9 %collective-permute-start.48 = (bf16[256,2048]{1,0:T(8,128)(2,1)S(1)}, bf16[256,2048]{1,0:T(8,128)(2,1)S(1)}, u32[]{:S(2)}, u32[]{:S(2)}) collective-permute-start(bf16[256,2048]{1,0:T(8,128)(2,1)S(1)} %add.607), channel_id=1, source_target_pairs={{8,16},{12,20},{16,8},{20,12},{9,17},{13,21},{17,9},{21,13},{10,18... | collective-permute-start | bytes 3145736 | tf_op jit(solution)/shard_map/ppermute | solution.py:127
  997.2 25.0 %collective-permute-start.50 = (bf16[256,2048]{1,0:T(8,128)(2,1)S(1)}, bf16[256,2048]{1,0:T(8,128)(2,1)S(1)}, u32[]{:S(2)}, u32[]{:S(2)}) collective-permute-start(bf16[256,2048]{1,0:T(8,128)(2,1)S(1)} %add.606), channel_id=1, source_target_pairs={{8,0},{12,4},{16,24},{20,28},{9,1},{13,5},{17,25},{21,29},{10,2},{... | collective-permute-start | bytes 3145736 | tf_op jit(solution)/shard_map/ppermute | solution.py:127
  1022.2 24.1 %collective-permute-start.51 = (bf16[256,2048]{1,0:T(8,128)(2,1)S(1)}, bf16[256,2048]{1,0:T(8,128)(2,1)S(1)}, u32[]{:S(2)}, u32[]{:S(2)}) collective-permute-start(bf16[256,2048]{1,0:T(8,128)(2,1)S(1)} %add.609), channel_id=1, source_target_pairs={{8,0},{12,4},{16,24},{20,28},{9,1},{13,5},{17,25},{21,29},{10,2},{... | collective-permute-start | bytes 3145736 | tf_op jit(solution)/shard_map/ppermute | solution.py:127
  1023.6 24.2 %collective-permute-start.56 = (bf16[256,2048]{1,0:T(8,128)(2,1)S(1)}, bf16[256,2048]{1,0:T(8,128)(2,1)S(1)}, u32[]{:S(2)}, u32[]{:S(2)}) collective-permute-start(bf16[256,2048]{1,0:T(8,128)(2,1)S(1)} %broadcast_select_fusion.2), channel_id=1, source_target_pairs={{0,4},{4,0},{8,12},{12,8},{16,20},{20,16},{24,28},{28,24},{1,5},{5... | collective-permute-start | bytes 3145736 | tf_op jit(solution)/shard_map/ppermute | solution.py:333
  1026.3 34.7 %collective-permute-start.57 = (bf16[4,256,2048]{2,1,0:T(8,128)(2,1)S(1)}, bf16[4,256,2048]{2,1,0:T(8,128)(2,1)S(1)}, u32[]{:S(2)}, u32[]{:S(2)}) collective-permute-start(bf16[4,256,2048]{2,1,0:T(8,128)(2,1)S(1)} %pad_maximum_fusion.1), channel_id=1, source_target_pairs={{0,4},{4,0},{8,12},{12,8},{16,20},{20,16},{24,28},{28,24},{1,5},{5... | collective-permute-start | bytes 12582920 | tf_op jit(solution)/shard_map/ppermute | solution.py:333
  1046.4 11.5 %collective-permute-start.52 = (bf16[256,2048]{1,0:T(8,128)(2,1)S(1)}, bf16[256,2048]{1,0:T(8,128)(2,1)S(1)}, u32[]{:S(2)}, u32[]{:S(2)}) collective-permute-start(bf16[256,2048]{1,0:T(8,128)(2,1)S(1)} %broadcast_select_fusion.3), channel_id=1, source_target_pairs={{0,4},{4,0},{8,12},{12,8},{16,20},{20,16},{24,28},{28,24},{1,5},{5... | collective-permute-start | bytes 3145736 | tf_op jit(solution)/shard_map/ppermute | solution.py:333
  (88 other events, 1405.8 us)
Sparse Core Ops, SparseCore 0:
  11.0 57.1 all-gather.8
  71.1 89.3 all-gather.6
  163.3 77.7 all-gather.10
  242.5 80.6 all-gather.12
  324.6 80.5 all-gather.14
  529.1 26.2 reduce-scatter.7
  558.8 123.8 reduce-scatter.3
  688.2 148.2 all-reduce.3
  840.1 87.4 reduce-scatter.5

commit v2 on v1

--- a/solution.py
+++ b/solution.py
@@ -1,8 +1,11 @@
+import functools
 from functools import partial
 
 import jax
 import jax.numpy as jnp
 from jax import lax
+from jax.experimental import pallas as pl
+from jax.experimental.pallas import tpu as pltpu
 from jax.sharding import PartitionSpec as P
 
 HEADS = 16
@@ -11,6 +14,9 @@
 NEGATIVE = -1e30
 BF = jnp.bfloat16
 F32 = jnp.float32
+MESH = pl.DeviceIdType.MESH
+LAG_MID = 2
+LAG_OUT = 4
 
 
 def mm(left, right):
@@ -96,42 +102,446 @@
     return held[0][0], held[1][0]
 
 
-def line_stages(groups):
+def near_first(count):
+    return sorted(range(1, count), key=lambda q: (bin(q).count("1"), q))
+
+
+def cube_tree(count, parity, q):
+    order = list(range(count.bit_length() - 1))
+    if parity:
+        order = order[::-1]
+    at = max([i for i, d in enumerate(order) if q >> d & 1], default=-1)
+    return [1 << d for d in order[at + 1 :]]
+
+
+def near_first(count):
+    return sorted(range(1, count), key=lambda q: (bin(q).count("1"), q))
+
+
+def gather_kernel(
+    groups, count, wq, wo, kvs, upc, q_all, o_all, kvs_all, up_all,
+    zs, zr, ps, pr, bs, br, us, ur, loc,
+):
     chips = groups // 2
-    both = lambda pairs: [(2 * a + c, 2 * b + c) for a, b in pairs for c in range(2)]
-    stages = []
-    for hop in range(1, chips // 2):
-        stages.append(("in", both([(hop - 1, hop), (chips - hop, chips - 1 - hop)]), None))
-    low, high = chips // 2 - 1, chips // 2
-    stages.append(("in", both([(low, high), (high, low)]), None))
-    for hop in range(1, chips // 2):
-        a, b = low + 1 - hop, high - 1 + hop
-        stages.append(("out", both([(a, a - 1), (b, b + 1)]), (a - 1, b + 1)))
-    return stages
-
-
-def line_sum(chunks, groups, axis):
-    stages = line_stages(groups)
-    place = lax.axis_index(axis) // 2
-    state = [None] * len(chunks)
-    last = ()
-    for turn in range(len(chunks) + len(stages) - 1):
-        work = [k for k in range(len(chunks)) if 0 <= turn - k < len(stages)]
-        sends = [chunks[k] if turn == k else state[k] for k in work]
-        if last:
-            tied = lax.optimization_barrier(tuple(sends) + last)
-            sends = tied[: len(sends)]
-        got = []
-        for k, send in zip(work, sends):
-            kind, pairs, ends = stages[turn - k]
-            arrived = lax.ppermute(send, axis, pairs)
-            got.append(arrived)
-            if kind == "in":
-                state[k] = send + arrived
-            else:
-                state[k] = jnp.where((place == ends[0]) | (place == ends[1]), arrived, send)
-        last = tuple(got)
-    return state
+    g, me = lax.axis_index("grp"), lax.axis_index("shard")
+    p, c = lax.div(g, 2), lax.rem(g, 2)
+
+    barrier = pltpu.get_barrier_semaphore()
+
+    def greet(target):
+        pl.semaphore_signal(barrier, inc=1, device_id=target, device_id_type=MESH)
+
+    greet((g + 1 - 2 * c, me))
+    for q in range(1, count):
+        greet((g, lax.bitwise_xor(me, q)))
+
+    @pl.when(p < chips - 1)
+    def _():
+        greet((g + 2, me))
+
+    @pl.when(p > 0)
+    def _():
+        greet((g - 2, me))
+
+    ends = (p == 0).astype(jnp.int32) + (p == chips - 1).astype(jnp.int32)
+    pl.semaphore_wait(barrier, count + 2 - ends)
+
+    def send(src, dst, send_sem, recv_sem, target):
+        pltpu.make_async_remote_copy(
+            src_ref=src, dst_ref=dst, send_sem=send_sem, recv_sem=recv_sem,
+            device_id=target, device_id_type=MESH,
+        ).start()
+
+    def wait(ref, sem):
+        pltpu.make_async_copy(ref, ref, sem).wait()
+
+    own = (wq, wo, kvs)
+    whole = (q_all, o_all, kvs_all)
+    parity = (0, 1, 0)
+    size = wq.shape[0]
+    up_size = upc.shape[1]
+    up_half = up_size * count // 2
+
+    def spot(a, z, col):
+        if a < 3:
+            at = ((z * 2 + c) * count + col) * size
+            return whole[a].at[pl.ds(pl.multiple_of(at, 16), size)]
+        at = (z * 2 + c) * up_half * 2 + (a - 3) * up_half
+        return up_all.at[pl.ds(pl.multiple_of(at, 16), up_half)]
+
+    def along(a, way, hop, src, z):
+        step = 1 - 2 * way
+        send(src, spot(a, z, me), zs.at[a, way, hop], zr.at[a, way, hop], (g + 2 * step, me))
+
+    def across(a, src, z, q):
+        for m in cube_tree(count, parity[a], q):
+            send(
+                src, spot(a, z, lax.bitwise_xor(me, q)), ps.at[a], pr.at[a, z, q ^ m],
+                (g, lax.bitwise_xor(me, m)),
+            )
+
+    def aside(a, src, z, q):
+        send(src, spot(a, z, lax.bitwise_xor(me, q)), bs.at[a], br.at[a], (g + 1 - 2 * c, me))
+
+    def may_send(way, hop):
+        if way == 0:
+            return (p >= hop - 1) & (p < chips - 1)
+        return (p + hop - 1 <= chips - 1) & (p > 0)
+
+    def may_take(way, hop):
+        return p >= hop if way == 0 else p + hop <= chips - 1
+
+    up_rows = lambda col: up_all.at[pl.ds(pl.multiple_of((g * count + col) * up_size, 16), up_size)]
+    for q in near_first(count):
+        to = lax.bitwise_xor(me, q)
+        send(upc.at[to], up_rows(me), us, ur.at[q], (g, to))
+    mine = [pltpu.make_async_copy(upc.at[me], up_rows(me), loc.at[3])]
+    for a in range(3):
+        mine.append(pltpu.make_async_copy(own[a], spot(a, p, me), loc.at[a]))
+    for copy in mine:
+        copy.start()
+
+    def first(a, src):
+        for way in range(2):
+            pl.when(may_send(way, 1))(functools.partial(along, a, way, 1, src, p))
+        aside(a, src, p, 0)
+
+    for a in range(3):
+        first(a, own[a])
+        across(a, own[a], p, 0)
+    mine[0].wait()
+    for q in near_first(count):
+        wait(up_rows(me), ur.at[q])
+    for a in (3, 4):
+        first(a, spot(a, p, me))
+
+    def plane(z):
+        for q in near_first(count):
+            for a in range(3):
+                ref = spot(a, z, lax.bitwise_xor(me, q))
+                wait(ref, pr.at[a, z, q])
+                across(a, ref, z, q)
+                aside(a, ref, z, q)
+
+    def planes(hop):
+        if hop == 0:
+            plane(p)
+            return
+        for way in range(2):
+            z = p - hop if way == 0 else p + hop
+            pl.when(may_take(way, hop))(functools.partial(plane, z))
+
+    def arrive(a, hop):
+        for way in range(2):
+
+            @pl.when(may_take(way, hop))
+            def _():
+                z = p - hop if way == 0 else p + hop
+                ref = spot(a, z, me)
+                wait(ref, zr.at[a, way, hop])
+                if hop + 1 < chips:
+                    pl.when(may_send(way, hop + 1))(
+                        functools.partial(along, a, way, hop + 1, ref, z)
+                    )
+                if a < 3:
+                    across(a, ref, z, 0)
+                aside(a, ref, z, 0)
+
+    for hop in range(1, chips):
+        for a in range(3):
+            arrive(a, hop)
+        planes(hop - 1)
+        for a in (3, 4):
+            arrive(a, hop)
+    planes(chips - 1)
+
+    for copy in mine[1:]:
+        copy.wait()
+    for a in range(5):
+        for way in range(2):
+            for hop in range(1, chips):
+                pl.when(may_send(way, hop))(
+                    functools.partial(wait, spot(a, p, me), zs.at[a, way, hop])
+                )
+    for a in range(3):
+        wait(whole[a].at[pl.ds(0, chips * (count - 1) * size)], ps.at[a])
+        wait(whole[a].at[pl.ds(0, chips * count * size)], bs.at[a])
+        wait(whole[a].at[pl.ds(0, chips * count * size)], br.at[a])
+    for a in (3, 4):
+        wait(up_all.at[pl.ds(0, chips * up_half)], bs.at[a])
+        wait(up_all.at[pl.ds(0, chips * up_half)], br.at[a])
+    wait(up_all.at[pl.ds(0, (count - 1) * up_size)], us)
+
+
+def gather_all(groups, count, wq, wo, kvs, upc):
+    chips = groups // 2
+    n = groups * count
+    any_ = pl.BlockSpec(memory_space=pl.ANY)
+    dma = pltpu.SemaphoreType.DMA
+    tall = lambda x: jax.ShapeDtypeStruct((n * x.shape[0], x.shape[1]), x.dtype)
+    return pl.pallas_call(
+        functools.partial(gather_kernel, groups, count),
+        out_shape=(
+            tall(wq), tall(wo), tall(kvs),
+            jax.ShapeDtypeStruct((n * upc.shape[1], upc.shape[2]), upc.dtype),
+        ),
+        in_specs=[any_] * 4,
+        out_specs=(any_,) * 4,
+        scratch_shapes=[
+            dma((5, 2, chips)), dma((5, 2, chips)), dma((3,)), dma((3, chips, count)),
+            dma((5,)), dma((5,)), dma, dma((count,)), dma((4,)),
+        ],
+        compiler_params=pltpu.CompilerParams(collective_id=1, has_side_effects=True),
+        cost_estimate=pl.CostEstimate(flops=0, bytes_accessed=100_000_000, transcendentals=0),
+        name="gather_all",
+    )(wq, wo, kvs, upc)
+
+
+def reduce_kernel(groups, count, subs, plain, *refs):
+    n = len(subs)
+    take = iter(refs)
+    many = lambda: [next(take) for _ in range(n)]
+    terms, final, land = many(), many(), many()
+    part, held, outer, mid, load = many(), many(), many(), many(), many()
+    sib, ld, sent, came, zs, z_in, z_mid, os, z_fin, xs, xr, loc, ss = take
+    chips = groups // 2
+    g, me = lax.axis_index("grp"), lax.axis_index("shard")
+    p, c = lax.div(g, 2), lax.rem(g, 2)
+    low = p < chips // 2
+    inn = jnp.where(low, g + 2, g - 2)
+    out = jnp.where(low, g - 2, g + 2)
+    end = (p == 0) | (p == chips - 1)
+    middle = (p == chips // 2 - 1) | (p == chips // 2)
+    other = g + 1 - 2 * c
+
+    barrier = pltpu.get_barrier_semaphore()
+
+    def greet(target):
+        pl.semaphore_signal(barrier, inc=1, device_id=target, device_id_type=MESH)
+
+    greet((other, me))
+    greet((inn, me))
+    for q in range(1, count):
+        greet((g, lax.bitwise_xor(me, q)))
+
+    @pl.when(jnp.logical_not(end))
+    def _():
+        greet((out, me))
+
+    pl.semaphore_wait(barrier, count + 2 - end.astype(jnp.int32))
+
+    def send(src, dst, send_sem, recv_sem, target):
+        pltpu.make_async_remote_copy(
+            src_ref=src, dst_ref=dst, send_sem=send_sem, recv_sem=recv_sem,
+            device_id=target, device_id_type=MESH,
+        ).start()
+
+    def wait(ref, sem):
+        pltpu.make_async_copy(ref, ref, sem).wait()
+
+    def add(dst, *more):
+        rows = dst.shape[0]
+
+        @pl.loop(0, rows // 16)
+        def _(i):
+            at = pl.ds(pl.multiple_of(i * 16, 16), 16)
+            total = dst[at].astype(F32)
+            for ref in more:
+                total = total + ref[at].astype(F32)
+            dst[at] = total.astype(BF)
+
+    size = [terms[m].shape[2] // subs[m] for m in range(n)]
+    cut = lambda m, j: pl.ds(j * size[m], size[m])
+
+    for m in range(n):
+        for q in near_first(count) + [0]:
+            send(
+                terms[m].at[lax.bitwise_xor(me, q), 1 - c], land[m].at[q], ss.at[m], sib.at[m, q],
+                (other, me),
+            )
+
+    pair_tasks = []
+    for m in range(n):
+        pair_tasks.append([(m, j, q) for j in range(subs[m]) for q in near_first(count) + [0]])
+    flat = [task for tasks in pair_tasks for task in tasks]
+
+    def place(m, j, q):
+        if q:
+            return part[m].at[q - 1, cut(m, j)]
+        return held[m].at[me, cut(m, j)]
+
+    def loads(k):
+        m, j, q = flat[k]
+        slot = k % 2
+        return (
+            pltpu.make_async_copy(
+                terms[m].at[lax.bitwise_xor(me, q), c, cut(m, j)], place(m, j, q), ld.at[slot, 0]
+            ),
+            pltpu.make_async_copy(land[m].at[q, cut(m, j)], load[m].at[slot], ld.at[slot, 1]),
+        )
+
+    def begin(k):
+        m, j, q = flat[k]
+        if j == 0:
+            wait(land[m].at[q], sib.at[m, q])
+        for copy in loads(k):
+            copy.start()
+
+    def pair(k):
+        m, j, q = flat[k]
+        if k == 0:
+            begin(0)
+        if k + 1 < len(flat):
+            begin(k + 1)
+        for copy in loads(k):
+            copy.wait()
+        ref = place(m, j, q)
+        add(ref, load[m].at[k % 2])
+        if q:
+            send(ref, held[m].at[me, cut(m, j)], sent.at[m], came.at[m, j, q], (g, lax.bitwise_xor(me, q)))
+
+    units = []
+    for m in range(n):
+        for j in range(subs[m]):
+            units += [(m, j, q) for q in range(count)] if plain[m] else [(m, j, 0)]
+
+    def value(u):
+        m, j, q = units[u]
+        return held[m].at[lax.bitwise_xor(me, q), cut(m, j)]
+
+    def result(u, half):
+        m, j, q = units[u]
+        return final[m].at[half, lax.bitwise_xor(me, q) if plain[m] else 0, cut(m, j)]
+
+    def inward(u):
+        m, j, q = units[u]
+        ref = value(u)
+        if plain[m]:
+            if q:
+                wait(ref, came.at[m, j, q])
+        else:
+            others = [held[m].at[lax.bitwise_xor(me, r), cut(m, j)] for r in near_first(count)]
+            for r, other_ref in zip(near_first(count), others):
+                wait(other_ref, came.at[m, j, r])
+            add(ref, *others)
+
+        @pl.when(jnp.logical_not(end))
+        def _():
+            wait(outer[m].at[q, cut(m, j)], z_in.at[u])
+            add(ref, outer[m].at[q, cut(m, j)])
+
+        @pl.when(middle)
+        def _():
+            send(ref, mid[m].at[q, cut(m, j)], zs.at[u], z_mid.at[u], (inn, me))
+
+        @pl.when(jnp.logical_not(middle))
+        def _():
+            send(ref, outer[m].at[q, cut(m, j)], zs.at[u], z_in.at[u], (inn, me))
+
+    def centre(u):
+        m, j, q = units[u]
+
+        @pl.when(middle)
+        def _():
+            ref = value(u)
+            wait(ref, zs.at[u])
+            wait(mid[m].at[q, cut(m, j)], z_mid.at[u])
+            add(ref, mid[m].at[q, cut(m, j)])
+            pl.when(jnp.logical_not(end))(
+                lambda: send(ref, result(u, c), os.at[u], z_fin.at[u], (out, me))
+            )
+            send(ref, result(u, c), xs.at[u], xr.at[u], (other, me))
+            pltpu.make_async_copy(ref, result(u, c), loc.at[u]).start()
+
+    def outward(u):
+        @pl.when(jnp.logical_not(middle))
+        def _():
+            ref = result(u, c)
+            wait(ref, z_fin.at[u])
+            pl.when(jnp.logical_not(end))(
+                lambda: send(ref, ref, os.at[u], z_fin.at[u], (out, me))
+            )
+            send(ref, ref, xs.at[u], xr.at[u], (other, me))
+
+    done = 0
+    for _ in pair_tasks[0]:
+        pair(done)
+        done += 1
+    for step in range(len(units) + LAG_OUT):
+        for _ in range(3):
+            if done < len(flat):
+                pair(done)
+                done += 1
+        if step < len(units):
+            inward(step)
+        if 0 <= step - LAG_MID < len(units):
+            centre(step - LAG_MID)
+        if 0 <= step - LAG_OUT < len(units):
+            outward(step - LAG_OUT)
+
+    for m in range(n):
+        wait(land[m], ss.at[m])
+        for q in range(count - 1):
+            wait(part[m].at[q], sent.at[m])
+    for u in range(len(units)):
+        wait(result(u, 1 - c), xr.at[u])
+        wait(result(u, c), xs.at[u])
+        pl.when(jnp.logical_not(end))(functools.partial(wait, result(u, c), os.at[u]))
+        pl.when(middle)(functools.partial(wait, result(u, c), loc.at[u]))
+        pl.when(jnp.logical_not(middle))(functools.partial(wait, value(u), zs.at[u]))
+
+
+def reduce_all(groups, count, terms, plain, subs):
+    n = len(terms)
+    any_ = pl.BlockSpec(memory_space=pl.ANY)
+    dma = pltpu.SemaphoreType.DMA
+    shape = lambda x, a, b: tuple(d for d in (a, b) if d) + x.shape[2:]
+    out = [jax.ShapeDtypeStruct(shape(x, 2, count if f else 1), BF) for x, f in zip(terms, plain)]
+    land = [jax.ShapeDtypeStruct(shape(x, count, 0), BF) for x in terms]
+    part = [pltpu.VMEM(shape(x, count - 1, 0), BF) for x in terms]
+    held = [pltpu.VMEM(shape(x, count, 0), BF) for x in terms]
+    line = [pltpu.VMEM(shape(x, count if f else 1, 0), BF) for x, f in zip(terms, plain)]
+    load = [pltpu.VMEM((2, x.shape[2] // s, x.shape[3]), BF) for x, s in zip(terms, subs)]
+    units = sum(s * (count if f else 1) for s, f in zip(subs, plain))
+    got = pl.pallas_call(
+        functools.partial(reduce_kernel, groups, count, subs, plain),
+        out_shape=tuple(out + land),
+        in_specs=[any_] * n,
+        out_specs=(any_,) * (2 * n),
+        scratch_shapes=part + held + line + line + load + [
+            dma((n, count)), dma((2, 2)), dma((n,)), dma((n, max(subs), count)),
+            dma((units,)), dma((units,)), dma((units,)), dma((units,)), dma((units,)),
+            dma((units,)), dma((units,)), dma((units,)), dma((n,)),
+        ],
+        compiler_params=pltpu.CompilerParams(
+            collective_id=2, has_side_effects=True, vmem_limit_bytes=60 * 1024 * 1024
+        ),
+        cost_estimate=pl.CostEstimate(flops=0, bytes_accessed=200_000_000, transcendentals=0),
+        name="reduce_all",
+    )(*terms)
+    return got[:n]
+
+
+def spread_kernel(block, x_ref, o_ref):
+    _, count, rows, hidden = x_ref.shape
+    for source in range(count):
+        for k in range(hidden // block):
+            o_ref[:, pl.ds((k * count + source) * block, block)] = x_ref[
+                0, source, :, pl.ds(k * block, block)
+            ].astype(F32)
+
+
+def spread(values, block):
+    _, count, rows, hidden = values.shape
+    step = rows // 4
+    return pl.pallas_call(
+        functools.partial(spread_kernel, block),
+        out_shape=jax.ShapeDtypeStruct((2 * rows, count * hidden), F32),
+        grid=(2, rows // step),
+        in_specs=[pl.BlockSpec((1, count, step, hidden), lambda h, i: (h, 0, i, 0))],
+        out_specs=pl.BlockSpec((step, count * hidden), lambda h, i: (h * (rows // step) + i, 0)),
+        name="spread",
+    )(values)
 
 
 def shards(
@@ -161,7 +571,6 @@
     group_rows = dealing.shape[0]
     group = lax.axis_index("grp")
     me = lax.axis_index("shard")
-    core = group % 2
     half = micro // 2
     block = down_weight.shape[0]
     hidden = block * groups
@@ -176,7 +585,21 @@
         first_gain, first_shift, query_bias, value_bias, out_bias,
         second_gain, second_shift, up_bias, down_bias,
     )
-    packed = lax.all_gather(jnp.concatenate(small), both, axis=0)
+    up_rows = up_weight.shape[0]
+    beside = jnp.concatenate(small)
+    beside = jnp.pad(beside, (0, up_rows * 128 - beside.shape[0])).reshape(up_rows, 128)
+    keyval_wide = jnp.concatenate([keyval_weight, beside], axis=1)
+    up_cut = up_weight.reshape(up_rows, groups, count, block).transpose(2, 0, 1, 3)
+    up_cut = up_cut.reshape(count, up_rows, hidden)
+    weight_query, weight_out, keyval_all, weight_up = gather_all(
+        groups, count, query_weight, out_weight, keyval_wide, up_cut
+    )
+    weight_query, weight_out, keyval_all, weight_up, down_weight, cotangent = lax.optimization_barrier(
+        (weight_query, weight_out, keyval_all, weight_up, down_weight, cotangent)
+    )
+    weight_down = lax.all_gather(down_weight, "grp", axis=0, tiled=True)
+    weight_keyval = keyval_all[:, : 2 * HD]
+    packed = keyval_all[:, 2 * HD :].reshape(groups * count, up_rows * 128)
     wide = []
     at = 0
     for item in small:
@@ -186,15 +609,6 @@
     gain_one, shift_one, bias_query, bias_value, bias_out, gain_two, shift_two, _, bias_down = [
         item.reshape(-1) for item in wide
     ]
-
-    weight_query = lax.all_gather(query_weight, both, axis=0, tiled=True)
-    weight_keyval = lax.all_gather(keyval_weight, both, axis=0, tiled=True)
-    weight_out = lax.all_gather(out_weight, both, axis=0, tiled=True)
-    up_rows = up_weight.shape[0]
-    up_cut = up_weight.reshape(up_rows, groups, count, block).transpose(2, 0, 1, 3)
-    up_cut = lax.all_to_all(up_cut.reshape(count, up_rows, hidden), "shard", 0, 0)
-    weight_up = lax.all_gather(up_cut.reshape(count * up_rows, hidden), "grp", axis=0, tiled=True)
-    weight_down = lax.all_gather(down_weight, "grp", axis=0, tiled=True)
 
     def gather_rows(values, place_of):
         held = cube_gather((values[:half], values[half:]), count, "shard")
@@ -273,19 +687,6 @@
         result = lax.dynamic_update_slice(result, row[None], (at, 0, 0))
     result = scatter_rows(result, same_place).astype(F32)
     block_output = ((result + bias_down) * own_live[:, :, None]).astype(BF)
-
-    pairs = flips(groups, 1)
-
-    def pair_sum(values):
-        mine = lax.dynamic_index_in_dim(values, core, 1, keepdims=False)
-        other = lax.dynamic_index_in_dim(values, 1 - core, 1, keepdims=False)
-        return mine + lax.ppermute(other, "grp", pairs)
-
-    slab = hidden // count
-    down_half = pair_sum(down_grad.reshape(count, 2, slab // 2, width))
-    down_half = lax.all_to_all(down_half, "shard", 0, 0)
-    up_half = pair_sum(up_grad.reshape(count, 2, width // count // 2, hidden))
-    up_half = lax.all_to_all(up_half, "shard", 0, 0)
 
     own_cot = jnp.stack([pick(cot_rows, dealt_place(me * micro + m)) for m in range(micro)])
     given_live = jnp.stack([live(own_lengths[m], length) for m in range(micro)])
@@ -319,34 +720,6 @@
     back_one, gain_one_grad, shift_one_grad = norm_back(grad_normed_one, unit_one, rate_one, gain_one)
     input_grad = (back_one + grad_middle).astype(BF).reshape(micro, length, width)
 
-    def slices(values):
-        part = lax.psum_scatter(values, "shard", scatter_dimension=0, tiled=True)
-        return pair_sum(part.reshape(1, 2, part.shape[0] // 2, part.shape[1]))[0]
-
-    out_half, query_half, keyval_half = slices(out_grad), slices(query_grad), slices(keyval_grad)
-
-    chunks = [down_half[q] for q in range(count)] + [up_half[q] for q in range(count)]
-    chunks = chunks + [out_half, query_half, keyval_half]
-    chunks = line_sum(chunks, groups, "grp")
-
-    def whole(halves):
-        other = lax.ppermute(halves, "grp", pairs)
-        first = jnp.where(core == 0, halves, other)
-        second = jnp.where(core == 0, other, halves)
-        return jnp.stack([first, second]).astype(F32)
-
-    down_full = whole(jnp.stack(chunks[:count]))
-    per = groups // count
-    down_full = down_full.transpose(1, 0, 2, 3).reshape(count, per, block, width)
-    down_full = down_full.transpose(1, 0, 2, 3).reshape(per * count * block, width)
-    up_full = whole(jnp.stack(chunks[count : 2 * count]))
-    up_full = up_full.reshape(2, count, width // count // 2, groups, block)
-    up_full = up_full.transpose(0, 2, 3, 1, 4).reshape(width // count, groups * count * block)
-    tail = chunks[2 * count :]
-    out_full, query_full, keyval_full = [
-        whole(item).reshape(2 * item.shape[0], item.shape[1]) for item in tail
-    ]
-
     up_bias_part = jnp.sum(grad_hidden.astype(F32), axis=0).reshape(groups, 1, block)
     value_bias_grad = jnp.sum(grad_keyvals[:, HD:].astype(F32), axis=0)
     query_bias_grad = jnp.sum(grad_queries.astype(F32), axis=0)
@@ -356,13 +729,31 @@
         gain_one_grad, shift_one_grad, query_bias_grad, value_bias_grad, out_bias_grad,
         gain_two_grad, shift_two_grad, up_bias_grad, down_bias_grad,
     )
-    summed = lax.psum(jnp.concatenate(vectors), both)
+    line = jnp.concatenate([item.reshape(count, -1) for item in vectors], axis=1).astype(BF)
+    unit = 2 * 16 * 2 * HD
+    more = -(-line.shape[1] // unit)
+    line = jnp.pad(line, ((0, 0), (0, more * unit - line.shape[1])))
+    line = line.reshape(count, 2, more * 16, 2 * HD)
+
+    cut = lambda x: x.reshape(count, 2, x.shape[0] // count // 2, x.shape[1])
+    terms = [cut(x) for x in (down_grad, up_grad, out_grad, query_grad, keyval_grad)]
+    terms[4] = jnp.concatenate([terms[4], line], axis=2)
+    down_full, up_full, out_full, query_full, last = reduce_all(
+        groups, count, terms, (True, True, False, False, False), (2, 2, 2, 2, 1)
+    )
+    down_full = down_full.reshape(-1, width).astype(F32)
+    up_full = spread(up_full, block)
+    out_full = out_full.reshape(-1, width).astype(F32)
+    query_full = query_full.reshape(-1, width).astype(F32)
+    tall = width // count // 2
+    keyval_full = last[:, 0, :tall].reshape(2 * tall, 2 * HD).astype(F32)
+    summed = last[:, 0, tall:].reshape(-1).astype(F32)
     parts = []
     at = 0
     for item in vectors:
         size = item.shape[0] // count
-        parts.append(lax.dynamic_slice(summed, (at + me * size,), (size,)))
-        at += item.shape[0]
+        parts.append(summed[at : at + size])
+        at += size
 
     return (
         block_output, input_grad, parts[0], parts[1], query_full, parts[2], keyval_full, parts[3],

time: 1120 us -> 859 us (0.77)
  Pallas kernels: 0 us -> 423 us
  waiting for transfers between devices: 490 us -> 89.4 us
  starting transfers between devices: 117 us -> 16.4 us
  other arithmetic: 140 us -> 74.7 us
  blocking collectives: 60.5 us -> 0 us
  local copies, waits for them, and re-layouts: 115 us -> 59 us
    pallas_call x0 -> x3, Pallas kernels: none -> 423 us  [the longest x1 283 us: reduce_all(): pl.pallas_call(functools.partial(reduce_kernel, groups, count, subs, plai...]
    ppermute x43 -> x0, waiting for transfers between devices: 152 us -> none  [the longest x33 152 us: line_sum(): arrived = lax.ppermute(send, axis, pairs)]
    all_gather x4 -> x0, waiting for transfers between devices: 84.1 us -> none  [the longest x1 58.7 us: shards(): weight_out = lax.all_gather(out_weight, both, axis=0, tiled=True)]
    ppermute x43 -> x0, starting transfers between devices: 76.2 us -> none  [the longest x33 75 us: line_sum(): arrived = lax.ppermute(send, axis, pairs)]
    all_gather x1, waiting for transfers between devices: 67.6 us -> 0.01 us  [shards(): weight_down = lax.all_gather(down_weight, 'grp', axis=0, tiled=True)]
    add x24 -> x0, other arithmetic: 45.4 us -> none  [the longest x22 33.4 us: line_sum(): state[k] = send + arrived]
    all_to_all x2 -> x0, waiting for transfers between devices: 42.6 us -> none  [the longest x1 42.6 us: shards(): down_half = lax.all_to_all(down_half, 'shard', 0, 0)]
    unnamed x1 -> x0, blocking collectives: 40.9 us -> none
  transfers between devices with their start and end apart: 70 -> 17, of which waited for: 33 -> 6; matrix products, arithmetic and copies ran while one was open for 26% -> 28% of each run, Pallas kernels for 0% -> 34%
where the time goes in v2:
time: 859 us; the launch traced here: 853 us
  Pallas kernels  423 us (49%)
  matrix products  144 us (17%)
  waiting for transfers between devices  89.4 us (10%)
  other arithmetic  74.7 us (9%)
  local copies, waits for them, and re-layouts  59 us (7%)
  between operations  47 us (5%)
  starting transfers between devices  16.4 us (2%)
    pallas_call x1, Pallas kernels, reduce_all(): pl.pallas_call(functools.partial(reduce_kernel, groups, count, subs, plai...  283 us
    pallas_call x1, Pallas kernels, gather_all(): pl.pallas_call(functools.partial(gather_kernel, groups, count), out_shape...  129 us
    ppermute x8, waiting for transfers between devices, cube_scatter(): got = lax.ppermute(pack, axis, flips(count, mask))  57.2 us
    dot_general x9, matrix products, mm_nt(): lax.dot_general(left, right, (((1,), (1,)), ((), ())), preferred_element_...  51.6 us
    dot_general x9, matrix products, mm_tn(): lax.dot_general(left, right, (((0,), (0,)), ((), ())), preferred_element_...  46.6 us
    dot_general x9, matrix products, mm(): return jnp.dot(left, right, preferred_element_type=F32)  45.7 us
    ppermute x8, waiting for transfers between devices, cube_gather(): got = lax.ppermute(pack, axis, flips(count, mask))  32.2 us
  transfers between devices with their start and end apart: 17, of which 6 were waited for; matrix products, arithmetic and copies ran while one was open for 28% of the time, Pallas kernels for 34%

profile of v2, /device:TPU:0, one launch (start us, length us, event | category | flops | bytes accessed | tf_op | source)
XLA Modules:
  0.0 853.4 jit_solution(4728349082030738924)
XLA Ops:
  7.2 6.1 concatenate.41
  13.3 1.8 reshape.425
  15.3 1.3 reshape.426.upc
  17.3 129.3 %gather_all.1 = (bf16[2048,2048]{1,0:T(8,128)(2,1)}, bf16[2048,2048]{1,0:T(8,128)(2,1)}, bf16[2048,384]{1,0:T(8,128)(2,1)}, bf16[2048,2048]{1,0:T(8,128)(2,1)}) custom-call(bf16[64,2048]{1,0:T(8,128)(2,1)} %wq.1, bf16[64,2048]{1,0:T(8,128)(2,1)} %wo.1, bf16[64,384]{1,0:T(8,128)(2,1)} %pad_maximum_fusion.10.kvs, bf16[4,64,2048]{2,1,0:T(8,128)(2,1)} %reshape.426.upc), custom_call_target="tpu_custom_call" | custom-call | bytes 100000000 | tf_op jit(solution)/shard_map/gather_all/pallas_call | solution.py:282
  146.6 2.5 broadcast.208.clone.1
  151.8 1.5 collective-permute-start.8
  177.4 2.1 fusion.22
  179.5 5.8 fusion.8
  189.0 1.3 convert_element_type.295
  194.6 1.3 convert_element_type.299
  196.9 6.3 fusion.105
  205.7 1.4 collective-permute-start
  210.5 1.3 iota_compare_fusion.10
  214.2 1.3 iota_compare_fusion.8
  220.2 2.0 copy-done.22
  235.8 1.3 pad_maximum_fusion.6
  237.9 1.6 pad_maximum_fusion.5
  239.5 1.3 collective-permute-start.10
  240.8 1.3 pad_maximum_fusion.2
  242.8 1.3 pad_maximum_fusion.1
  245.4 1.9 bitcast_dynamic-update-slice_fusion.1
  248.4 17.3 %collective-permute-done.10 = bf16[2,1,128,2048]{3,2,1,0:T(8,128)(2,1)S(1)} collective-permute-done((bf16[2,1,128,2048]{3,2,1,0:T(8,128)(2,1)S(1)}, bf16[2,1,128,2048]{3,2,1,0:T(8,128)(2,1)S(1)}, u32[]{:S(2)}, u32[]{:S(2)}) %collective-permute-start.10) | collective-permute-done | bytes 1048608 | tf_op jit(solution)/shard_map/ppermute | solution.py:85
  267.3 2.0 bitcast_dynamic-update-slice_fusion
  271.0 14.9 %collective-permute-done.2 = bf16[2,1,128,2048]{3,2,1,0:T(8,128)(2,1)S(1)} collective-permute-done((bf16[2,1,128,2048]{3,2,1,0:T(8,128)(2,1)S(1)}, bf16[2,1,128,2048]{3,2,1,0:T(8,128)(2,1)S(1)}, u32[]{:S(2)}, u32[]{:S(2)}) %collective-permute-start.2) | collective-permute-done | bytes 1048608 | tf_op jit(solution)/shard_map/ppermute | solution.py:85
  287.3 4.5 multiply_convert_fusion
  292.2 11.1 %fusion.106 = f32[1024,2048]{1,0:T(8,128)} fusion(bf16[1024,2048]{1,0:T(8,128)(2,1)S(1)} %bitcast.297, bf16[2048,2048]{1,0:T(8,128)(2,1)S(1)} %bitcast.316), kind=kOutput, calls=%fused_computation.279 | convolution fusion | flops 8589934592 | bytes 20971520 | tf_op jit(solution)/shard_map/dot_general | solution.py:23
  303.3 18.4 %convolution_convert_fusion.3 = bf16[2048,2048]{1,0:T(8,128)(2,1)} fusion(bf16[1024,2048]{1,0:T(8,128)(2,1)S(1)} %bitcast.301, f32[1024,2048]{1,0:T(8,128)} %fusion.106, f32[2048]{0:T(1024)S(1)} %bitcast.312), kind=kOutput, calls=%fused_computation.16 | convolution fusion | flops 8615100416 | bytes 20979712 | tf_op jit(solution)/shard_map/dot_general | solution.py:27
  321.8 15.9 %convolution_convert_fusion.5 = bf16[1024,2048]{1,0:T(8,128)(2,1)S(1)} fusion(bf16[2048,2048]{1,0:T(8,128)(2,1)} %all-gather.2.cloned.1.call-done, f32[1024,2048]{1,0:T(8,128)} %fusion.106, f32[2048]{0:T(1024)S(1)} %bitcast.313), kind=kOutput, calls=%fused_computation.18 | convolution fusion | flops 8613003264 | bytes 20979712 | tf_op jit(solution)/shard_map/dot_general | solution.py:23
  338.0 2.1 copy-done.12
  341.3 1.4 collective-permute-start.4
  342.7 20.3 %convert_reduce_fusion = (bf16[2048]{0:T(1024)(128)(2,1)S(1)}, bf16[1024,2048]{1,0:T(8,128)(2,1)}) fusion(f32[1024,2048]{1,0:T(8,128)} %fusion.106, f32[2048]{0:T(1024)S(1)} %bitcast.314, bf16[1024,2048]{1,0:T(8,128)(2,1)S(1)} %bitcast.302, bf16[2048,2048]{1,0:T(8,128)(2,1)} %all-gather.2.cloned.1.call-done), kind=kOutput, calls=%fused_computation.10 | convolution fusion | flops 8638167040 | bytes 25178112 | tf_op jit(solution)/shard_map/dot_general | solution.py:31
  363.1 10.9 %convolution_convert_fusion.4 = bf16[1024,2048]{1,0:T(8,128)(2,1)S(1)} fusion(bf16[1024,2048]{1,0:T(8,128)(2,1)} %get-tuple-element.65, bf16[2048,2048]{1,0:T(8,128)(2,1)S(1)} %bitcast.318), kind=kOutput, calls=%fused_computation.17 | convolution fusion | flops 8592031744 | bytes 16777216 | tf_op jit(solution)/shard_map/dot_general | solution.py:31
  377.5 1.6 fusion.25
  379.1 2.6 fusion.53
  384.8 13.7 %collective-permute-done.12 = bf16[2,1,128,2048]{3,2,1,0:T(8,128)(2,1)S(1)} collective-permute-done((bf16[2,1,128,2048]{3,2,1,0:T(8,128)(2,1)}, bf16[2,1,128,2048]{3,2,1,0:T(8,128)(2,1)S(1)}, u32[]{:S(2)}, u32[]{:S(2)}) %collective-permute-start.12) | collective-permute-done | bytes 1048608 | tf_op jit(solution)/shard_map/ppermute | solution.py:99
  398.5 2.7 fusion.41
  402.9 1.4 collective-permute-start.14
  404.3 11.6 %convolution_convert_fusion.2 = bf16[2048,2048]{1,0:T(8,128)(2,1)} fusion(bf16[1024,2048]{1,0:T(8,128)(2,1)S(1)} %bitcast.298, bf16[1024,2048]{1,0:T(8,128)(2,1)S(1)} %copy-done.63), kind=kOutput, calls=%fused_computation.15 | convolution fusion | flops 8594128896 | bytes 16777216 | tf_op jit(solution)/shard_map/dot_general | solution.py:27
  415.9 14.7 %collective-permute-done.13 = bf16[1,1,128,2048]{3,2,1,0:T(8,128)(2,1)} collective-permute-done((bf16[1,1,128,2048]{3,2,1,0:T(8,128)(2,1)}, bf16[1,1,128,2048]{3,2,1,0:T(8,128)(2,1)}, u32[]{:S(2)}, u32[]{:S(2)}) %collective-permute-start.13) | collective-permute-done | bytes 524320 | tf_op jit(solution)/shard_map/ppermute | solution.py:99
  430.6 18.9 %collective-permute-done.14 = bf16[2,1,128,2048]{3,2,1,0:T(8,128)(2,1)} collective-permute-done((bf16[2,1,128,2048]{3,2,1,0:T(8,128)(2,1)}, bf16[2,1,128,2048]{3,2,1,0:T(8,128)(2,1)}, u32[]{:S(2)}, u32[]{:S(2)}) %collective-permute-start.14) | collective-permute-done | bytes 1048608 | tf_op jit(solution)/shard_map/ppermute | solution.py:99
  449.5 2.2 fusion.93
  451.6 1.4 collective-permute-start.15
  453.1 2.9 fusion.55
  456.8 9.9 %collective-permute-done.15 = bf16[1,1,128,2048]{3,2,1,0:T(8,128)(2,1)} collective-permute-done((bf16[1,1,128,2048]{3,2,1,0:T(8,128)(2,1)S(1)}, bf16[1,1,128,2048]{3,2,1,0:T(8,128)(2,1)}, u32[]{:S(2)}, u32[]{:S(2)}) %collective-permute-start.15) | collective-permute-done | bytes 524320 | tf_op jit(solution)/shard_map/ppermute | solution.py:99
  466.7 1.6 fusion.91
  470.4 6.5 convolution_convert_fusion.7
  479.3 1.5 multiply_reduce_fusion.6
  482.5 1.3 reshape.439
  484.8 1.5 fusion.24
  487.6 1.5 convolution_convert_fusion.6
  489.0 5.6 convolution_convert_fusion.1
  497.1 2.0 copy.50
  499.1 2.3 convert_element_type.325
  503.5 7.2 fusion.107
  510.7 6.9 convolution_convert_fusion
  517.7 4.3 multiply_reduce_fusion
  522.3 2.3 pad_maximum_fusion.refs_4_
  524.6 283.2 %reduce_all.1 = (bf16[2,4,256,2048]{3,2,1,0:T(8,128)(2,1)}, bf16[2,4,256,2048]{3,2,1,0:T(8,128)(2,1)}, bf16[2,1,256,2048]{3,2,1,0:T(8,128)(2,1)}, bf16[2,1,256,2...) custom-call(bf16[4,2,256,2048]{3,2,1,0:T(8,128)(2,1)} %bitcast.290, ...), custom_call_target="tpu_custom_call" | custom-call | bytes 200000000 | tf_op jit(solution)/shard_map/reduce_all/pallas_call | solution.py:506
  812.2 4.1 bitcast_convert_fusion.2
  816.4 10.6 %spread.1 = f32[512,8192]{1,0:T(8,128)} custom-call(bf16[2,4,256,2048]{3,2,1,0:T(8,128)(2,1)} %get-tuple-element.44.x_ref), custom_call_target="tpu_custom_call" | custom-call | tf_op jit(solution)/shard_map/spread/pallas_call | solution.py:537
  827.0 11.8 %bitcast_convert_fusion = f32[2048,2048]{1,0:T(8,128)} fusion(bf16[2,4,256,2048]{3,2,1,0:T(8,128)(2,1)} %get-tuple-element.45), kind=kLoop, calls=%fused_computation.9 | loop fusion | flops 4194304 | bytes 25165824 | tf_op jit(solution)/shard_map/convert_element_type | solution.py:744
  838.8 1.8 add_convert_fusion
  840.6 2.7 bitcast_convert_fusion.1
  843.3 1.4 fusion.51
  (296 shorter events, 69.8 us)
Async XLA Ops:
  7.2 9.5 %copy-start.53 = (bf16[64,256]{1,0:T(8,128)(2,1)S(1)}, bf16[64,256]{1,0:T(8,128)(2,1)}, u32[]{:S(2)}) copy-start(bf16[64,256]{1,0:T(8,128)(2,1)} %param.26) | copy-start | bytes 98308
  7.2 314.6 %all-gather.2.cloned.1.call-start = ((), (), s32[]{:S(2)}) async-start(), calls=%async_computation | async-start | bytes 9437184 | tf_op jit(solution)/shard_map/all_gather | solution.py:600
  15.3 133.8 %copy-start.32 = (bf16[2,128,2048]{2,1,0:T(8,128)(2,1)S(1)}, bf16[2,128,2048]{2,1,0:T(8,128)(2,1)}, u32[]{:S(2)}) copy-start(bf16[2,128,2048]{2,1,0:T(8,128)(2,1)} %param.19) | copy-start | bytes 3145732
  146.6 6.7 copy-start.62
  146.6 20.3 %copy-start.6 = (bf16[2,128,2048]{2,1,0:T(8,128)(2,1)S(1)}, bf16[2,128,2048]{2,1,0:T(8,128)(2,1)}, u32[]{:S(2)}) copy-start(bf16[2,128,2048]{2,1,0:T(8,128)(2,1)} %param.18) | copy-start | bytes 3145732
  149.2 23.6 %copy-start.41 = (s32[8,4]{0,1:T(4,128)S(1)}, s32[8,4]{0,1:T(4,128)}, u32[]{:S(2)}) copy-start(s32[8,4]{0,1:T(4,128)} %param.20) | copy-start | bytes 388
  151.2 86.7 %collective-permute-start.9 = (bf16[1,1,128,2048]{3,2,1,0:T(8,128)(2,1)}, bf16[1,1,128,2048]{3,2,1,0:T(8,128)(2,1)}, u32[]{:S(2)}, u32[]{:S(2)}) collective-permute-start(bf16[1,1,128,2048]{3,2,1,0:T(8,128)(2,1)} %get-tuple-element.91), channel_id=1, source_target_pairs={{0,2},{1,3},{2,0},{3,1},{4,6},{5,7},{6,4},{7,5},{8,10},{9,11},{10,... | collective-permute-start | bytes 1572872 | tf_op jit(solution)/shard_map/ppermute | solution.py:85
  151.8 84.0 %collective-permute-start.8 = (bf16[1,1,128,2048]{3,2,1,0:T(8,128)(2,1)}, bf16[1,1,128,2048]{3,2,1,0:T(8,128)(2,1)}, u32[]{:S(2)}, u32[]{:S(2)}) collective-permute-start(bf16[1,1,128,2048]{3,2,1,0:T(8,128)(2,1)} %get-tuple-element.92), channel_id=1, source_target_pairs={{0,1},{1,0},{2,3},{3,2},{4,5},{5,4},{6,7},{7,6},{8,9},{9,8},{10,11... | collective-permute-start | bytes 1572872 | tf_op jit(solution)/shard_map/ppermute | solution.py:85
  166.2 13.3 %copy-start.38 = (bf16[32,8192]{1,0:T(8,128)(2,1)}, bf16[32,8192]{1,0:T(8,128)(2,1)S(1)}, u32[]{:S(2)}) copy-start(bf16[32,8192]{1,0:T(8,128)(2,1)S(1)} %reshape.427) | copy-start | bytes 1572868
  167.2 9.8 %copy-start.56 = (f32[256]{0:T(256)}, f32[256]{0:T(256)S(1)}, u32[]{:S(2)}) copy-start(f32[256]{0:T(256)S(1)} %get-tuple-element.120) | copy-start | bytes 3076
  167.6 9.3 %copy-start.58 = (f32[256]{0:T(256)}, f32[256]{0:T(256)S(1)}, u32[]{:S(2)}) copy-start(f32[256]{0:T(256)S(1)} %rsqrt_bitcast_fusion) | copy-start | bytes 3076
  177.4 7.9 copy-start.8
  179.5 13.1 %copy-start.39 = (bf16[256,256]{1,0:T(8,128)(2,1)}, bf16[256,256]{1,0:T(8,128)(2,1)S(1)}, u32[]{:S(2)}) copy-start(bf16[256,256]{1,0:T(8,128)(2,1)S(1)} %fusion.22) | copy-start | bytes 393220
  185.7 5.5 copy-start.13
  185.9 5.6 copy-start.14
  187.9 6.7 copy-start.18
  191.5 5.4 copy-start.60
  191.5 4.4 copy-start.28
  196.9 6.7 copy-start.52
  203.2 15.0 %copy-start.49 = (f32[2048]{0:T(1024)S(1)}, f32[2048]{0:T(1024)}, u32[]{:S(2)}) copy-start(f32[2048]{0:T(1024)} %copy-done.48) | copy-start | bytes 24580
  204.0 18.2 %copy-start.43 = (f32[2048]{0:T(1024)S(1)}, f32[2048]{0:T(1024)}, u32[]{:S(2)}) copy-start(f32[2048]{0:T(1024)} %copy-done.42) | copy-start | bytes 24580
  204.1 27.2 %copy-start.50 = (f32[32,64]{1,0:T(8,128)S(1)}, f32[32,64]{1,0:T(8,128)}, u32[]{:S(2)}) copy-start(f32[32,64]{1,0:T(8,128)} %get-tuple-element.102) | copy-start | bytes 24580
  205.3 37.5 %collective-permute-start.1 = (bf16[1,1,128,2048]{3,2,1,0:T(8,128)(2,1)}, bf16[1,1,128,2048]{3,2,1,0:T(8,128)(2,1)}, u32[]{:S(2)}, u32[]{:S(2)}) collective-permute-start(bf16[1,1,128,2048]{3,2,1,0:T(8,128)(2,1)} %get-tuple-element.94), channel_id=1, source_target_pairs={{0,2},{1,3},{2,0},{3,1},{4,6},{5,7},{6,4},{7,5},{8,10},{9,11},{10,... | collective-permute-start | bytes 1572872 | tf_op jit(solution)/shard_map/ppermute | solution.py:85
  205.7 35.1 %collective-permute-start = (bf16[1,1,128,2048]{3,2,1,0:T(8,128)(2,1)}, bf16[1,1,128,2048]{3,2,1,0:T(8,128)(2,1)}, u32[]{:S(2)}, u32[]{:S(2)}) collective-permute-start(bf16[1,1,128,2048]{3,2,1,0:T(8,128)(2,1)} %get-tuple-element.95), channel_id=1, source_target_pairs={{0,1},{1,0},{2,3},{3,2},{4,5},{5,4},{6,7},{7,6},{8,9},{9,8},{10,11... | collective-permute-start | bytes 1572872 | tf_op jit(solution)/shard_map/ppermute | solution.py:85
  237.1 10.1 %copy-start.23 = (bf16[8,128,2048]{2,1,0:T(8,128)(2,1)S(1)}, bf16[8,128,2048]{2,1,0:T(8,128)(2,1)}, u32[]{:S(2)}) copy-start(bf16[8,128,2048]{2,1,0:T(8,128)(2,1)} %copy-done.22) | copy-start | bytes 12582916
  237.2 29.3 %collective-permute-start.11 = (bf16[2,1,128,2048]{3,2,1,0:T(8,128)(2,1)S(1)}, bf16[2,1,128,2048]{3,2,1,0:T(8,128)(2,1)S(1)}, u32[]{:S(2)}, u32[]{:S(2)}) collective-permute-start(bf16[2,1,128,2048]{3,2,1,0:T(8,128)(2,1)S(1)} %pad_maximum_fusion.6), channel_id=1, source_target_pairs={{0,2},{1,3},{2,0},{3,1},{4,6},{5,7},{6,4},{7,5},{8,10},{9,11},{10,... | collective-permute-start | bytes 3145736 | tf_op jit(solution)/shard_map/ppermute | solution.py:85
  239.5 26.2 %collective-permute-start.10 = (bf16[2,1,128,2048]{3,2,1,0:T(8,128)(2,1)S(1)}, bf16[2,1,128,2048]{3,2,1,0:T(8,128)(2,1)S(1)}, u32[]{:S(2)}, u32[]{:S(2)}) collective-permute-start(bf16[2,1,128,2048]{3,2,1,0:T(8,128)(2,1)S(1)} %pad_maximum_fusion.5), channel_id=1, source_target_pairs={{0,1},{1,0},{2,3},{3,2},{4,5},{5,4},{6,7},{7,6},{8,9},{9,8},{10,11... | collective-permute-start | bytes 3145736 | tf_op jit(solution)/shard_map/ppermute | solution.py:85
  242.1 43.8 %collective-permute-start.3 = (bf16[2,1,128,2048]{3,2,1,0:T(8,128)(2,1)S(1)}, bf16[2,1,128,2048]{3,2,1,0:T(8,128)(2,1)S(1)}, u32[]{:S(2)}, u32[]{:S(2)}) collective-permute-start(bf16[2,1,128,2048]{3,2,1,0:T(8,128)(2,1)S(1)} %pad_maximum_fusion.2), channel_id=1, source_target_pairs={{0,2},{1,3},{2,0},{3,1},{4,6},{5,7},{6,4},{7,5},{8,10},{9,11},{10,... | collective-permute-start | bytes 3145736 | tf_op jit(solution)/shard_map/ppermute | solution.py:85
  244.1 41.8 %collective-permute-start.2 = (bf16[2,1,128,2048]{3,2,1,0:T(8,128)(2,1)S(1)}, bf16[2,1,128,2048]{3,2,1,0:T(8,128)(2,1)S(1)}, u32[]{:S(2)}, u32[]{:S(2)}) collective-permute-start(bf16[2,1,128,2048]{3,2,1,0:T(8,128)(2,1)S(1)} %pad_maximum_fusion.1), channel_id=1, source_target_pairs={{0,1},{1,0},{2,3},{3,2},{4,5},{5,4},{6,7},{7,6},{8,9},{9,8},{10,11... | collective-permute-start | bytes 3145736 | tf_op jit(solution)/shard_map/ppermute | solution.py:85
  267.3 24.4 %slice-start = ((s8[8388608]{0:T(1024)(128)(4,1)}), s8[4194304]{0:T(1024)(128)(4,1)S(1)}, s32[]{:S(2)}) async-start(s8[8388608]{0:T(1024)(128)(4,1)} %bitcast.315), calls=%async_computation.1 | async-start | bytes 8388608
  287.2 16.1 %copy-start.24 = (bf16[8,128,2048]{2,1,0:T(8,128)(2,1)}, bf16[8,128,2048]{2,1,0:T(8,128)(2,1)S(1)}, u32[]{:S(2)}) copy-start(bf16[8,128,2048]{2,1,0:T(8,128)(2,1)S(1)} %fusion.56) | copy-start | bytes 12582916
  287.3 5.0 slice-start.1
  291.8 11.6 %copy-start.26 = (bf16[8,128,2048]{2,1,0:T(8,128)(2,1)}, bf16[8,128,2048]{2,1,0:T(8,128)(2,1)S(1)}, u32[]{:S(2)}) copy-start(bf16[8,128,2048]{2,1,0:T(8,128)(2,1)S(1)} %multiply_convert_fusion) | copy-start | bytes 12582916
  337.7 5.0 copy-start.27
  340.3 22.8 %slice-start.2 = ((s8[8388608]{0:T(1024)(128)(4,1)}), s8[4194304]{0:T(1024)(128)(4,1)S(1)}, s32[]{:S(2)}) async-start(s8[8388608]{0:T(1024)(128)(4,1)} %bitcast.317), calls=%async_computation.3 | async-start | bytes 8388608
  341.3 21.7 %slice-start.3 = ((s8[8388608]{0:T(1024)(128)(4,1)}), s8[4194304]{0:T(1024)(128)(4,1)S(1)}, s32[]{:S(2)}) async-start(s8[8388608]{0:T(1024)(128)(4,1)} %bitcast.317), calls=%async_computation.4 | async-start | bytes 8388608
  341.3 37.8 %collective-permute-start.4 = (bf16[2,1,128,2048]{3,2,1,0:T(8,128)(2,1)}, bf16[2,1,128,2048]{3,2,1,0:T(8,128)(2,1)}, u32[]{:S(2)}, u32[]{:S(2)}) collective-permute-start(bf16[2,1,128,2048]{3,2,1,0:T(8,128)(2,1)} %pad_maximum_fusion.3), channel_id=1, source_target_pairs={{0,1},{1,0},{2,3},{3,2},{4,5},{5,4},{6,7},{7,6},{8,9},{9,8},{10,11... | collective-permute-start | bytes 3145736 | tf_op jit(solution)/shard_map/ppermute | solution.py:99
  374.0 5.1 copy-start.21
  375.4 23.2 %collective-permute-start.12 = (bf16[2,1,128,2048]{3,2,1,0:T(8,128)(2,1)}, bf16[2,1,128,2048]{3,2,1,0:T(8,128)(2,1)S(1)}, u32[]{:S(2)}, u32[]{:S(2)}) collective-permute-start(bf16[2,1,128,2048]{3,2,1,0:T(8,128)(2,1)} %pad_maximum_fusion.7), channel_id=1, source_target_pairs={{0,1},{1,0},{2,3},{3,2},{4,5},{5,4},{6,7},{7,6},{8,9},{9,8},{10,11... | collective-permute-start | bytes 3145736 | tf_op jit(solution)/shard_map/ppermute | solution.py:99
  379.1 25.2 %copy-start.63 = (bf16[1024,2048]{1,0:T(8,128)(2,1)S(1)}, bf16[1024,2048]{1,0:T(8,128)(2,1)}, u32[]{:S(2)}) copy-start(bf16[1024,2048]{1,0:T(8,128)(2,1)} %get-tuple-element.65) | copy-start | bytes 12582916
  381.7 22.6 %copy-start.25 = (bf16[8,128,2048]{2,1,0:T(8,128)(2,1)S(1)}, bf16[8,128,2048]{2,1,0:T(8,128)(2,1)}, u32[]{:S(2)}) copy-start(bf16[8,128,2048]{2,1,0:T(8,128)(2,1)} %copy-done.24) | copy-start | bytes 12582916
  381.7 71.4 %collective-permute-start.5 = (bf16[1,1,128,2048]{3,2,1,0:T(8,128)(2,1)}, bf16[1,1,128,2048]{3,2,1,0:T(8,128)(2,1)}, u32[]{:S(2)}, u32[]{:S(2)}) collective-permute-start(bf16[1,1,128,2048]{3,2,1,0:T(8,128)(2,1)} %get-tuple-element.82), channel_id=1, source_target_pairs={{0,2},{1,3},{2,0},{3,1},{4,6},{5,7},{6,4},{7,5},{8,10},{9,11},{10,... | collective-permute-start | bytes 1572872 | tf_op jit(solution)/shard_map/ppermute | solution.py:99
  383.8 69.3 %collective-permute-start.6 = (bf16[2,1,128,2048]{3,2,1,0:T(8,128)(2,1)}, bf16[2,1,128,2048]{3,2,1,0:T(8,128)(2,1)}, u32[]{:S(2)}, u32[]{:S(2)}) collective-permute-start(bf16[2,1,128,2048]{3,2,1,0:T(8,128)(2,1)} %pad_maximum_fusion.4), channel_id=1, source_target_pairs={{0,2},{1,3},{2,0},{3,1},{4,6},{5,7},{6,4},{7,5},{8,10},{9,11},{10,... | collective-permute-start | bytes 3145736 | tf_op jit(solution)/shard_map/ppermute | solution.py:99
  398.5 17.4 %copy-start.37 = (bf16[2,1,128,2048]{3,2,1,0:T(8,128)(2,1)}, bf16[2,1,128,2048]{3,2,1,0:T(8,128)(2,1)S(1)}, u32[]{:S(2)}) copy-start(bf16[2,1,128,2048]{3,2,1,0:T(8,128)(2,1)S(1)} %collective-permute-done.12) | copy-start | bytes 3145732
  401.2 29.4 %collective-permute-start.13 = (bf16[1,1,128,2048]{3,2,1,0:T(8,128)(2,1)}, bf16[1,1,128,2048]{3,2,1,0:T(8,128)(2,1)}, u32[]{:S(2)}, u32[]{:S(2)}) collective-permute-start(bf16[1,1,128,2048]{3,2,1,0:T(8,128)(2,1)} %get-tuple-element.73), channel_id=1, source_target_pairs={{0,2},{1,3},{2,0},{3,1},{4,6},{5,7},{6,4},{7,5},{8,10},{9,11},{10,... | collective-permute-start | bytes 1572872 | tf_op jit(solution)/shard_map/ppermute | solution.py:99
  402.9 46.6 %collective-permute-start.14 = (bf16[2,1,128,2048]{3,2,1,0:T(8,128)(2,1)}, bf16[2,1,128,2048]{3,2,1,0:T(8,128)(2,1)}, u32[]{:S(2)}, u32[]{:S(2)}) collective-permute-start(bf16[2,1,128,2048]{3,2,1,0:T(8,128)(2,1)} %pad_maximum_fusion.8), channel_id=1, source_target_pairs={{0,2},{1,3},{2,0},{3,1},{4,6},{5,7},{6,4},{7,5},{8,10},{9,11},{10,... | collective-permute-start | bytes 3145736 | tf_op jit(solution)/shard_map/ppermute | solution.py:99
  451.6 15.0 %collective-permute-start.15 = (bf16[1,1,128,2048]{3,2,1,0:T(8,128)(2,1)S(1)}, bf16[1,1,128,2048]{3,2,1,0:T(8,128)(2,1)}, u32[]{:S(2)}, u32[]{:S(2)}) collective-permute-start(bf16[1,1,128,2048]{3,2,1,0:T(8,128)(2,1)S(1)} %get-tuple-element.72), channel_id=1, source_target_pairs={{0,1},{1,0},{2,3},{3,2},{4,5},{5,4},{6,7},{7,6},{8,9},{9,8},{10,11... | collective-permute-start | bytes 1572872 | tf_op jit(solution)/shard_map/ppermute | solution.py:99
  453.1 16.3 %copy-start.11 = (f32[2,128,2048]{2,1,0:T(8,128)S(1)}, f32[2,128,2048]{2,1,0:T(8,128)}, u32[]{:S(2)}) copy-start(f32[2,128,2048]{2,1,0:T(8,128)} %get-tuple-element.88) | copy-start | bytes 6291460
  456.1 387.3 %collective-permute-start.7 = (bf16[1,1,128,2048]{3,2,1,0:T(8,128)(2,1)}, bf16[1,1,128,2048]{3,2,1,0:T(8,128)(2,1)}, u32[]{:S(2)}, u32[]{:S(2)}) collective-permute-start(bf16[1,1,128,2048]{3,2,1,0:T(8,128)(2,1)} %get-tuple-element.81), channel_id=1, source_target_pairs={{0,1},{1,0},{2,3},{3,2},{4,5},{5,4},{6,7},{7,6},{8,9},{9,8},{10,11... | collective-permute-start | bytes 1572872 | tf_op jit(solution)/shard_map/ppermute | solution.py:99
  470.3 6.6 copy-start.4
  470.4 8.5 copy-start.19
  479.3 4.5 copy-start.17
  479.3 4.9 copy-start.1
  479.3 4.9 copy-start.46
  484.5 4.5 copy-start.5
  484.5 4.5 copy-start.30
  489.0 5.6 copy-start.35
  503.5 7.2 copy-start.10
  510.7 7.0 copy-start.7
  510.7 7.0 copy-start.45
  510.7 7.0 copy-start.57
  510.7 7.0 copy-start.59
  827.0 11.8 %copy-start.34 = (f32[256,2048]{1,0:T(8,128)S(1)}, f32[256,2048]{1,0:T(8,128)}, u32[]{:S(2)}) copy-start(f32[256,2048]{1,0:T(8,128)} %get-tuple-element.148) | copy-start | bytes 6291460
  840.6 4.1 copy-start.61
  (21 other events, 41.3 us)
Sparse Core Ops, SparseCore 0:
  146.7 81.3 all-gather.1

commit v3 on v2

--- a/solution.py
+++ b/solution.py
@@ -1,4 +1,3 @@
-import functools
 from functools import partial
 
 import jax
@@ -17,6 +16,8 @@
 MESH = pl.DeviceIdType.MESH
 LAG_MID = 2
 LAG_OUT = 4
+NORM_STEP = 4
+RING = 6
 
 
 def mm(left, right):
@@ -37,14 +38,6 @@
     spread = jnp.mean(offset * offset, axis=-1, keepdims=True)
     rate = lax.rsqrt(spread + EPS)
     return offset * rate, rate
-
-
-def norm_back(grad, unit, rate, gain):
-    e = grad * gain
-    back = rate * (
-        e - jnp.mean(e, axis=-1, keepdims=True) - unit * jnp.mean(e * unit, axis=-1, keepdims=True)
-    )
-    return back, jnp.sum(grad * unit, axis=0), jnp.sum(grad, axis=0)
 
 
 def row_ends(lengths_row):
@@ -88,20 +81,6 @@
     return held
 
 
-def cube_scatter(blocks, count, axis):
-    orders = cube_orders(count)
-    held = [dict(b) for b in blocks]
-    for step in range(len(orders[0])):
-        for k in range(2):
-            mask = 1 << orders[k][step]
-            away = [q for q in sorted(held[k]) if q & mask]
-            pack = jnp.stack([held[k].pop(q) for q in away])
-            got = lax.ppermute(pack, axis, flips(count, mask))
-            for i, q in enumerate(away):
-                held[k][q ^ mask] = held[k][q ^ mask] + got[i]
-    return held[0][0], held[1][0]
-
-
 def near_first(count):
     return sorted(range(1, count), key=lambda q: (bin(q).count("1"), q))
 
@@ -203,7 +182,7 @@
 
     def first(a, src):
         for way in range(2):
-            pl.when(may_send(way, 1))(functools.partial(along, a, way, 1, src, p))
+            pl.when(may_send(way, 1))(partial(along, a, way, 1, src, p))
         aside(a, src, p, 0)
 
     for a in range(3):
@@ -229,7 +208,7 @@
             return
         for way in range(2):
             z = p - hop if way == 0 else p + hop
-            pl.when(may_take(way, hop))(functools.partial(plane, z))
+            pl.when(may_take(way, hop))(partial(plane, z))
 
     def arrive(a, hop):
         for way in range(2):
@@ -241,7 +220,7 @@
                 wait(ref, zr.at[a, way, hop])
                 if hop + 1 < chips:
                     pl.when(may_send(way, hop + 1))(
-                        functools.partial(along, a, way, hop + 1, ref, z)
+                        partial(along, a, way, hop + 1, ref, z)
                     )
                 if a < 3:
                     across(a, ref, z, 0)
@@ -261,7 +240,7 @@
         for way in range(2):
             for hop in range(1, chips):
                 pl.when(may_send(way, hop))(
-                    functools.partial(wait, spot(a, p, me), zs.at[a, way, hop])
+                    partial(wait, spot(a, p, me), zs.at[a, way, hop])
                 )
     for a in range(3):
         wait(whole[a].at[pl.ds(0, chips * (count - 1) * size)], ps.at[a])
@@ -280,7 +259,7 @@
     dma = pltpu.SemaphoreType.DMA
     tall = lambda x: jax.ShapeDtypeStruct((n * x.shape[0], x.shape[1]), x.dtype)
     return pl.pallas_call(
-        functools.partial(gather_kernel, groups, count),
+        partial(gather_kernel, groups, count),
         out_shape=(
             tall(wq), tall(wo), tall(kvs),
             jax.ShapeDtypeStruct((n * upc.shape[1], upc.shape[2]), upc.dtype),
@@ -297,13 +276,22 @@
     )(wq, wo, kvs, upc)
 
 
-def reduce_kernel(groups, count, subs, plain, *refs):
+def back_kernel(groups, count, subs, plain, sizes, share, *refs):
     n = len(subs)
     take = iter(refs)
-    many = lambda: [next(take) for _ in range(n)]
-    terms, final, land = many(), many(), many()
-    part, held, outer, mid, load = many(), many(), many(), many(), many()
-    sib, ld, sent, came, zs, z_in, z_mid, os, z_fin, xs, xr, loc, ss = take
+    many = lambda k: [next(take) for _ in range(k)]
+    down_term, up_term, slices, wq, wo, middle_far = many(6)
+    grad_out, attended, queries, keyvals, normed, tokens, bias, gains, wkv, early = many(10)
+    final, land = many(n), many(n)
+    input_grad = next(take)
+    own_part = {m: next(take) for m in range(n) if share[m] == m}
+    part = [own_part[share[m]] for m in range(n)]
+    held = many(n)
+    ring_of = sorted(set(sizes))
+    load, outer, mid = many(len(ring_of)), many(len(ring_of)), many(len(ring_of))
+    load = [load[ring_of.index(size)] for size in sizes]
+    arrived, middle, grad_mid, branch, grad_q, tiles, stage, stage_kv, grad_kv, sums = many(10)
+    sib, ld, sent, came, zs, z_in, z_mid, os, z_fin, xs, xr, loc, ss, gs, gr, ws, ms, free_in, free_mid = take
     chips = groups // 2
     g, me = lax.axis_index("grp"), lax.axis_index("shard")
     p, c = lax.div(g, 2), lax.rem(g, 2)
@@ -311,8 +299,9 @@
     inn = jnp.where(low, g + 2, g - 2)
     out = jnp.where(low, g - 2, g + 2)
     end = (p == 0) | (p == chips - 1)
-    middle = (p == chips // 2 - 1) | (p == chips // 2)
+    middle_chip = (p == chips // 2 - 1) | (p == chips // 2)
     other = g + 1 - 2 * c
+    near = near_first(count)
 
     barrier = pltpu.get_barrier_semaphore()
 
@@ -340,9 +329,7 @@
         pltpu.make_async_copy(ref, ref, sem).wait()
 
     def add(dst, *more):
-        rows = dst.shape[0]
-
-        @pl.loop(0, rows // 16)
+        @pl.loop(0, dst.shape[0] // 16)
         def _(i):
             at = pl.ds(pl.multiple_of(i * 16, 16), 16)
             total = dst[at].astype(F32)
@@ -350,35 +337,36 @@
                 total = total + ref[at].astype(F32)
             dst[at] = total.astype(BF)
 
-    size = [terms[m].shape[2] // subs[m] for m in range(n)]
-    cut = lambda m, j: pl.ds(j * size[m], size[m])
-
-    for m in range(n):
-        for q in near_first(count) + [0]:
-            send(
-                terms[m].at[lax.bitwise_xor(me, q), 1 - c], land[m].at[q], ss.at[m], sib.at[m, q],
-                (other, me),
-            )
-
-    pair_tasks = []
-    for m in range(n):
-        pair_tasks.append([(m, j, q) for j in range(subs[m]) for q in near_first(count) + [0]])
+    cut = lambda m, j: pl.ds(j * sizes[m][0], sizes[m][0])
+    away = lambda q: lax.bitwise_xor(me, q)
+
+    given = (down_term, up_term)
+    for m in range(2):
+        for q in near + [0]:
+            send(given[m].at[away(q), 1 - c], land[m].at[q], ss.at[m, q], sib.at[m, q], (other, me))
+    own_slice = pltpu.make_async_copy(slices.at[me], arrived.at[0], gr.at[0])
+    own_slice.start()
+    middle_copy = pltpu.make_async_copy(middle_far, middle, ms)
+    middle_copy.start()
+
+    def send_slices():
+        for q in near:
+            send(slices.at[away(q)], arrived.at[q], gs.at[q], gr.at[q], (g, away(q)))
+
+    pair_tasks = [[(m, j, q) for j in range(subs[m]) for q in near + [0]] for m in range(n)]
     flat = [task for tasks in pair_tasks for task in tasks]
 
-    def place(m, j, q):
-        if q:
-            return part[m].at[q - 1, cut(m, j)]
-        return held[m].at[me, cut(m, j)]
+    def spot(m, q):
+        return part[m].at[q - 1] if q else held[m].at[me]
 
     def loads(k):
         m, j, q = flat[k]
         slot = k % 2
-        return (
-            pltpu.make_async_copy(
-                terms[m].at[lax.bitwise_xor(me, q), c, cut(m, j)], place(m, j, q), ld.at[slot, 0]
-            ),
-            pltpu.make_async_copy(land[m].at[q, cut(m, j)], load[m].at[slot], ld.at[slot, 1]),
-        )
+        copies = [pltpu.make_async_copy(land[m].at[q, cut(m, j)], load[m].at[slot], ld.at[slot, 1])]
+        if m < 2:
+            place = spot(m, q).at[cut(m, j)]
+            copies.append(pltpu.make_async_copy(given[m].at[away(q), c, cut(m, j)], place, ld.at[slot, 0]))
+        return copies
 
     def begin(k):
         m, j, q = flat[k]
@@ -389,29 +377,35 @@
 
     def pair(k):
         m, j, q = flat[k]
-        if k == 0:
-            begin(0)
-        if k + 1 < len(flat):
+        if k == 0 or flat[k - 1][0] != m:
+            begin(k)
+        if k + 1 < len(flat) and flat[k + 1][0] == m:
             begin(k + 1)
         for copy in loads(k):
             copy.wait()
-        ref = place(m, j, q)
+        ref = spot(m, q).at[cut(m, j)]
         add(ref, load[m].at[k % 2])
         if q:
-            send(ref, held[m].at[me, cut(m, j)], sent.at[m], came.at[m, j, q], (g, lax.bitwise_xor(me, q)))
+            send(ref, held[m].at[me, cut(m, j)], sent.at[m], came.at[m, j, q], (g, away(q)))
 
     units = []
     for m in range(n):
         for j in range(subs[m]):
             units += [(m, j, q) for q in range(count)] if plain[m] else [(m, j, 0)]
+    rings = [ring_of.index(sizes[m]) for m, j, q in units]
+    index = [rings[:u].count(rings[u]) for u in range(len(units))]
+    total_in = [rings.count(r) for r in range(len(ring_of))]
+    slot_of = lambda u: index[u] % outer[rings[u]].shape[0]
+    reused = lambda u: index[u] >= outer[rings[u]].shape[0]
+    again = lambda u: index[u] + outer[rings[u]].shape[0] < total_in[rings[u]]
 
     def value(u):
         m, j, q = units[u]
-        return held[m].at[lax.bitwise_xor(me, q), cut(m, j)]
+        return held[m].at[away(q), cut(m, j)]
 
     def result(u, half):
         m, j, q = units[u]
-        return final[m].at[half, lax.bitwise_xor(me, q) if plain[m] else 0, cut(m, j)]
+        return final[m].at[half, away(q) if plain[m] else 0, cut(m, j)]
 
     def inward(u):
         m, j, q = units[u]
@@ -420,33 +414,42 @@
             if q:
                 wait(ref, came.at[m, j, q])
         else:
-            others = [held[m].at[lax.bitwise_xor(me, r), cut(m, j)] for r in near_first(count)]
-            for r, other_ref in zip(near_first(count), others):
+            others = [held[m].at[away(r), cut(m, j)] for r in near]
+            for r, other_ref in zip(near, others):
                 wait(other_ref, came.at[m, j, r])
             add(ref, *others)
+        box, slot = rings[u], slot_of(u)
 
         @pl.when(jnp.logical_not(end))
         def _():
-            wait(outer[m].at[q, cut(m, j)], z_in.at[u])
-            add(ref, outer[m].at[q, cut(m, j)])
-
-        @pl.when(middle)
+            wait(outer[box].at[slot], z_in.at[u])
+            add(ref, outer[box].at[slot])
+            if again(u):
+                pl.semaphore_signal(free_in.at[box, slot], inc=1, device_id=(out, me), device_id_type=MESH)
+
+        @pl.when(middle_chip)
         def _():
-            send(ref, mid[m].at[q, cut(m, j)], zs.at[u], z_mid.at[u], (inn, me))
-
-        @pl.when(jnp.logical_not(middle))
+            if reused(u):
+                pl.semaphore_wait(free_mid.at[box, slot], 1)
+            send(ref, mid[box].at[slot], zs.at[u], z_mid.at[u], (inn, me))
+
+        @pl.when(jnp.logical_not(middle_chip))
         def _():
-            send(ref, outer[m].at[q, cut(m, j)], zs.at[u], z_in.at[u], (inn, me))
+            if reused(u):
+                pl.semaphore_wait(free_in.at[box, slot], 1)
+            send(ref, outer[box].at[slot], zs.at[u], z_in.at[u], (inn, me))
 
     def centre(u):
-        m, j, q = units[u]
-
-        @pl.when(middle)
+        box, slot = rings[u], slot_of(u)
+
+        @pl.when(middle_chip)
         def _():
             ref = value(u)
             wait(ref, zs.at[u])
-            wait(mid[m].at[q, cut(m, j)], z_mid.at[u])
-            add(ref, mid[m].at[q, cut(m, j)])
+            wait(mid[box].at[slot], z_mid.at[u])
+            add(ref, mid[box].at[slot])
+            if again(u):
+                pl.semaphore_signal(free_mid.at[box, slot], inc=1, device_id=(inn, me), device_id_type=MESH)
             pl.when(jnp.logical_not(end))(
                 lambda: send(ref, result(u, c), os.at[u], z_fin.at[u], (out, me))
             )
@@ -454,7 +457,7 @@
             pltpu.make_async_copy(ref, result(u, c), loc.at[u]).start()
 
     def outward(u):
-        @pl.when(jnp.logical_not(middle))
+        @pl.when(jnp.logical_not(middle_chip))
         def _():
             ref = result(u, c)
             wait(ref, z_fin.at[u])
@@ -463,63 +466,288 @@
             )
             send(ref, ref, xs.at[u], xr.at[u], (other, me))
 
-    done = 0
-    for _ in pair_tasks[0]:
-        pair(done)
-        done += 1
-    for step in range(len(units) + LAG_OUT):
-        for _ in range(3):
-            if done < len(flat):
-                pair(done)
-                done += 1
+    rows, width = attended.shape
+    length = bias.shape[1]
+    scale = HD**-0.5
+    band = 32
+    column = lambda at, size: pl.ds(pl.multiple_of(at, 128), size)
+
+    def moments(x):
+        centre_ = jnp.mean(x, axis=1, keepdims=True)
+        offset = x - centre_
+        rate = lax.rsqrt(jnp.mean(offset * offset, axis=1, keepdims=True) + EPS)
+        return offset * rate, rate
+
+    def clear():
+        sums[...] = jnp.zeros_like(sums)
+        grad_kv[...] = jnp.zeros_like(grad_kv)
+
+    def tally(k, x):
+        sums[k : k + 1, :] += jnp.sum(x, axis=0, keepdims=True)
+
+    def second_norm(lo, hi):
+        gain = gains[1:2, :]
+
+        @pl.loop(lo, hi)
+        def _(i):
+            at = pl.ds(pl.multiple_of(i * band, band), band)
+            grad = arrived[0, at, :].astype(F32)
+            for q in range(1, count):
+                grad = grad + arrived[q, at, :].astype(F32)
+            unit, rate = moments(middle[at, :])
+            tally(0, grad * unit)
+            tally(1, grad)
+            e = grad * gain
+            back = rate * (
+                e - jnp.mean(e, axis=1, keepdims=True) - unit * jnp.mean(e * unit, axis=1, keepdims=True)
+            )
+            whole = back + grad_out[at, :].astype(F32)
+            grad_mid[at, :] = whole
+            short = whole.astype(BF)
+            branch[at, :] = short
+            tally(2, short.astype(F32))
+
+    def first_norm(lo, hi):
+        gain = gains[0:1, :]
+
+        @pl.loop(lo, hi)
+        def _(i):
+            at = pl.ds(pl.multiple_of(i * band, band), band)
+            grad = middle[at, :]
+            unit, rate = moments(tokens[at, :].astype(F32))
+            tally(3, grad * unit)
+            tally(4, grad)
+            e = grad * gain
+            back = rate * (
+                e - jnp.mean(e, axis=1, keepdims=True) - unit * jnp.mean(e * unit, axis=1, keepdims=True)
+            )
+            input_grad[at, :] = (back + grad_mid[at, :]).astype(BF)
+            tally(5, grad_q[at, :].astype(F32))
+
+    part_cols = min(512, width)
+
+    def outer_product(dst, left, start, size, right):
+        lhs = left[:, column(start, size)]
+
+        @pl.loop(0, right.shape[1] // min(part_cols, right.shape[1]))
+        def _(k):
+            cols = column(k * min(part_cols, right.shape[1]), min(part_cols, right.shape[1]))
+            dst[:, cols] = lax.dot_general(
+                lhs, right[:, cols], (((0,), (0,)), ((), ())), preferred_element_type=F32
+            ).astype(BF)
+
+    staged = []
+
+    def weight_terms(m, left, right, some):
+        size = width // count // 2
+        for q in some:
+            k = len(staged)
+            if k >= 2:
+                wait(stage.at[k % 2], ss.at[staged[k - 2][0], staged[k - 2][1]])
+            outer_product(stage.at[k % 2], left, (away(q) * 2 + 1 - c) * size, size, right)
+            send(stage.at[k % 2], land[m].at[q], ss.at[m, q], sib.at[m, q], (other, me))
+            staged.append((m, q))
+            outer_product(spot(m, q), left, (away(q) * 2 + c) * size, size, right)
+
+    tile_rows = tiles.shape[1]
+    tile_count = width // tile_rows
+
+    def weight_tile(source, i):
+        at = pl.multiple_of(i * tile_rows, tile_rows)
+        slot = lax.rem(i, 2)
+        return pltpu.make_async_copy(source.at[pl.ds(at, tile_rows)], tiles.at[slot], ws.at[slot])
+
+    def attention_tiles(lo, hi):
+        @pl.loop(lo, hi)
+        def _(i):
+            pl.when(i + 1 < tile_count)(lambda: weight_tile(wo, i + 1).start())
+            weight_tile(wo, i).wait()
+            cols = column(i * tile_rows, tile_rows)
+            grad_att = lax.dot_general(
+                branch[...], tiles[lax.rem(i, 2)], (((1,), (1,)), ((), ())), preferred_element_type=F32
+            ).astype(BF)
+            query = queries[:, cols]
+            heads = tile_rows // HD
+            fold = lambda x: jnp.concatenate([x[:, h * HD : (h + 1) * HD] for h in range(heads)], axis=0)
+            for m in range(rows // length):
+                at = pl.ds(m * length, length)
+                q = fold(query[m * length : (m + 1) * length])
+                ga = fold(grad_att[m * length : (m + 1) * length])
+                k, v = keyvals[at, :HD], keyvals[at, HD:]
+                shut = jnp.concatenate([bias[at, :]] * heads, axis=0)
+                s = lax.dot_general(q, k, (((1,), (1,)), ((), ())), preferred_element_type=F32) * scale + shut
+                e = jnp.exp(s - jnp.max(s, axis=1, keepdims=True))
+                probs = e / jnp.sum(e, axis=1, keepdims=True)
+                gp = lax.dot_general(ga, v, (((1,), (1,)), ((), ())), preferred_element_type=F32)
+                ds = (probs * (gp - jnp.sum(probs * gp, axis=1, keepdims=True))).astype(BF)
+                dq = (jnp.dot(ds, k, preferred_element_type=F32) * scale).astype(BF)
+                for h in range(heads):
+                    grad_q[at, column(i * tile_rows + h * HD, HD)] = dq[h * length : (h + 1) * length]
+                tn = (((0,), (0,)), ((), ()))
+                dk = lax.dot_general(ds, q, tn, preferred_element_type=F32) * scale
+                dv = lax.dot_general(probs.astype(BF), ga, tn, preferred_element_type=F32)
+                grad_kv[at, :HD] += dk
+                grad_kv[at, HD:] += dv
+
+    def query_tiles(lo, hi):
+        low_kv = grad_kv[...].astype(BF)
+
+        @pl.loop(lo, hi)
+        def _(i):
+            pl.when(i + 1 < tile_count)(lambda: weight_tile(wq, i + 1).start())
+            weight_tile(wq, i).wait()
+            cols = column(i * tile_rows, tile_rows)
+            nt = (((1,), (1,)), ((), ()))
+            middle[:, cols] = lax.dot_general(
+                grad_q[...], tiles[lax.rem(i, 2)], nt, preferred_element_type=F32
+            ) + lax.dot_general(
+                low_kv, wkv[pl.ds(pl.multiple_of(i * tile_rows, tile_rows), tile_rows)], nt,
+                preferred_element_type=F32,
+            )
+
+    def keyval_terms():
+        low_kv = grad_kv[...].astype(BF)
+        size = width // count // 2
+        last = n - 1
+        line = jnp.sum(low_kv[:, HD:].astype(F32), axis=0, keepdims=True)
+        for k in range(width // size):
+            sums[6:7, k * size : k * size + HD] = line
+        for q in near + [0]:
+            for ref, which in ((stage_kv.at[q], 1 - c), (spot(last, q), c)):
+                start = (away(q) * 2 + which) * size
+                ref[pl.ds(0, size), :] = lax.dot_general(
+                    normed[:, column(start, size)], low_kv, (((0,), (0,)), ((), ())),
+                    preferred_element_type=F32,
+                ).astype(BF)
+                ref[pl.ds(size, 16), :] = jnp.zeros((16, 2 * HD), BF)
+                ref[pl.ds(size, 16), :size] = sums[:, column(start, size)].astype(BF)
+                ref[pl.ds(size + 16, early.shape[2]), :] = early[away(q), which]
+            send(stage_kv.at[q], land[last].at[q], ss.at[last, q], sib.at[last, q], (other, me))
+
+    def reuse(m):
+        if share[m] != m:
+            wait(part[m], sent.at[share[m]])
+
+    bands = rows // band
+    plan = {}
+
+    def at_step(step, *work):
+        plan.setdefault(step, []).extend(work)
+
+    P_ = partial
+    starts = [sum(len(t) for t in pair_tasks[:m]) for m in range(n)]
+    pairs_ = lambda m, lo, hi: [P_(pair, starts[m] + k) for k in range(lo, min(hi, len(pair_tasks[m])))]
+    per = len(pair_tasks[1])
+    for s in range(4):
+        at_step(s, *pairs_(1, s * per // 4, (s + 1) * per // 4))
+
+    def got_slices():
+        clear()
+        middle_copy.wait()
+        own_slice.wait()
+        for q in near:
+            wait(arrived.at[q], gr.at[q])
+
+    order = near + [0]
+    half = len(order) // 2
+    at_step(NORM_STEP, got_slices, P_(second_norm, 0, bands // 2))
+    at_step(NORM_STEP + 1, P_(second_norm, bands // 2, bands), lambda: weight_tile(wo, 0).start(), P_(reuse, 2))
+    at_step(NORM_STEP + 2, P_(weight_terms, 2, attended, branch, order[:half]))
+    at_step(NORM_STEP + 3, P_(weight_terms, 2, attended, branch, order[half:]))
+    for k in range(4):
+        at_step(NORM_STEP + 4 + k, P_(attention_tiles, k * tile_count // 4, (k + 1) * tile_count // 4))
+    per = len(pair_tasks[2])
+    at_step(NORM_STEP + 5, *pairs_(2, 0, per // 2))
+    at_step(NORM_STEP + 6, *pairs_(2, per // 2, per))
+    at_step(NORM_STEP + 7, lambda: weight_tile(wq, 0).start(), P_(reuse, 3))
+    at_step(NORM_STEP + 8, P_(weight_terms, 3, normed, grad_q, order[:half]))
+    at_step(NORM_STEP + 9, P_(weight_terms, 3, normed, grad_q, order[half:]))
+    at_step(NORM_STEP + 10, P_(query_tiles, 0, tile_count // 2), *pairs_(3, 0, per // 2))
+    at_step(NORM_STEP + 11, P_(query_tiles, tile_count // 2, tile_count), *pairs_(3, per // 2, per))
+    at_step(NORM_STEP + 12, P_(first_norm, 0, bands // 2))
+    at_step(NORM_STEP + 13, P_(first_norm, bands // 2, bands), keyval_terms)
+    at_step(NORM_STEP + 14, *pairs_(4, 0, 99))
+
+    per = len(pair_tasks[0])
+    for work in pairs_(0, 0, per // 2):
+        work()
+    send_slices()
+    for work in pairs_(0, per // 2, per):
+        work()
+    steps = max(len(units) + LAG_OUT, max(plan) + 1)
+    for step in range(steps):
         if step < len(units):
             inward(step)
         if 0 <= step - LAG_MID < len(units):
             centre(step - LAG_MID)
         if 0 <= step - LAG_OUT < len(units):
             outward(step - LAG_OUT)
+        for work in plan.get(step, ()):
+            work()
 
     for m in range(n):
-        wait(land[m], ss.at[m])
-        for q in range(count - 1):
-            wait(part[m].at[q], sent.at[m])
+        if m not in share[m + 1 :]:
+            wait(part[m], sent.at[m])
+        for q in near + [0]:
+            if m < 2 or m == n - 1 or (m, q) in staged[-2:]:
+                wait(land[m].at[q], ss.at[m, q])
+    for q in near:
+        wait(arrived.at[q], gs.at[q])
     for u in range(len(units)):
         wait(result(u, 1 - c), xr.at[u])
         wait(result(u, c), xs.at[u])
-        pl.when(jnp.logical_not(end))(functools.partial(wait, result(u, c), os.at[u]))
-        pl.when(middle)(functools.partial(wait, result(u, c), loc.at[u]))
-        pl.when(jnp.logical_not(middle))(functools.partial(wait, value(u), zs.at[u]))
-
-
-def reduce_all(groups, count, terms, plain, subs):
-    n = len(terms)
-    any_ = pl.BlockSpec(memory_space=pl.ANY)
-    dma = pltpu.SemaphoreType.DMA
-    shape = lambda x, a, b: tuple(d for d in (a, b) if d) + x.shape[2:]
-    out = [jax.ShapeDtypeStruct(shape(x, 2, count if f else 1), BF) for x, f in zip(terms, plain)]
-    land = [jax.ShapeDtypeStruct(shape(x, count, 0), BF) for x in terms]
-    part = [pltpu.VMEM(shape(x, count - 1, 0), BF) for x in terms]
-    held = [pltpu.VMEM(shape(x, count, 0), BF) for x in terms]
-    line = [pltpu.VMEM(shape(x, count if f else 1, 0), BF) for x, f in zip(terms, plain)]
-    load = [pltpu.VMEM((2, x.shape[2] // s, x.shape[3]), BF) for x, s in zip(terms, subs)]
+        pl.when(jnp.logical_not(end))(partial(wait, result(u, c), os.at[u]))
+        pl.when(middle_chip)(partial(wait, result(u, c), loc.at[u]))
+        pl.when(jnp.logical_not(middle_chip))(partial(wait, value(u), zs.at[u]))
+
+
+def back_all(groups, count, given, far, near_by, early):
+    rows, width = near_by[0].shape
+    size = width // count // 2
+    low = (size + 16 + early.shape[2], 2 * HD)
+    shapes = [x.shape[2:] for x in given] + [(size, width), (size, width), low]
+    plain, subs = (True, True, False, False, False), (2, 2, 2, 2, 1)
+    n = len(shapes)
+    sizes = [(s[0] // k, s[1]) for s, k in zip(shapes, subs)]
+    share = list(range(n))
+    for m in (2, 3):
+        if shapes[m] == shapes[m - 2]:
+            share[m] = m - 2
+    rings = sorted(set(sizes))
     units = sum(s * (count if f else 1) for s, f in zip(subs, plain))
+    slots = [min(RING, sum(s * (count if f else 1) for s, f, z in zip(subs, plain, sizes) if z == r)) for r in rings]
+    any_, vmem = pl.BlockSpec(memory_space=pl.ANY), pl.BlockSpec(memory_space=pltpu.VMEM)
+    dma, regular = pltpu.SemaphoreType.DMA, pltpu.SemaphoreType.REGULAR
+    out = [jax.ShapeDtypeStruct((2, count if f else 1) + s, BF) for s, f in zip(shapes, plain)]
+    out += [jax.ShapeDtypeStruct((count,) + s, BF) for s in shapes]
+    tile = 2 * HD
+    scratch = [pltpu.VMEM((count - 1,) + shapes[m], BF) for m in range(n) if share[m] == m]
+    scratch += [pltpu.VMEM((count,) + s, BF) for s in shapes]
+    scratch += [pltpu.VMEM((2,) + r, BF) for r in rings]
+    scratch += [pltpu.VMEM((k,) + r, BF) for k, r in zip(slots, rings)] * 2
+    scratch += [
+        pltpu.VMEM((count, rows, width), BF), pltpu.VMEM((rows, width), F32), pltpu.VMEM((rows, width), F32),
+        pltpu.VMEM((rows, width), BF), pltpu.VMEM((rows, width), BF), pltpu.VMEM((2, tile, width), BF),
+        pltpu.VMEM((2, size, width), BF), pltpu.VMEM((count,) + low, BF), pltpu.VMEM((rows, 2 * HD), F32),
+        pltpu.VMEM((16, width), F32),
+        dma((n, count)), dma((2, 2)), dma((n,)), dma((n, max(subs), count)), dma((units,)), dma((units,)),
+        dma((units,)), dma((units,)), dma((units,)), dma((units,)), dma((units,)), dma((units,)),
+        dma((n, count)), dma((count,)), dma((count,)), dma((2,)), dma,
+        regular((len(rings), max(slots))), regular((len(rings), max(slots))),
+    ]
     got = pl.pallas_call(
-        functools.partial(reduce_kernel, groups, count, subs, plain),
-        out_shape=tuple(out + land),
-        in_specs=[any_] * n,
-        out_specs=(any_,) * (2 * n),
-        scratch_shapes=part + held + line + line + load + [
-            dma((n, count)), dma((2, 2)), dma((n,)), dma((n, max(subs), count)),
-            dma((units,)), dma((units,)), dma((units,)), dma((units,)), dma((units,)),
-            dma((units,)), dma((units,)), dma((units,)), dma((n,)),
-        ],
+        partial(back_kernel, groups, count, subs, plain, sizes, share),
+        out_shape=tuple(out) + (jax.ShapeDtypeStruct((rows, width), BF),),
+        in_specs=[any_] * 6 + [vmem] * 10,
+        out_specs=(any_,) * (2 * n) + (vmem,),
+        scratch_shapes=scratch,
         compiler_params=pltpu.CompilerParams(
             collective_id=2, has_side_effects=True, vmem_limit_bytes=60 * 1024 * 1024
         ),
         cost_estimate=pl.CostEstimate(flops=0, bytes_accessed=200_000_000, transcendentals=0),
-        name="reduce_all",
-    )(*terms)
-    return got[:n]
+        name="back_all",
+    )(*given, *far, *near_by, early)
+    return got[:n], got[-1]
 
 
 def spread_kernel(block, x_ref, o_ref):
@@ -535,7 +763,7 @@
     _, count, rows, hidden = values.shape
     step = rows // 4
     return pl.pallas_call(
-        functools.partial(spread_kernel, block),
+        partial(spread_kernel, block),
         out_shape=jax.ShapeDtypeStruct((2 * rows, count * hidden), F32),
         grid=(2, rows // step),
         in_specs=[pl.BlockSpec((1, count, step, hidden), lambda h, i: (h, 0, i, 0))],
@@ -620,17 +848,6 @@
                     out = lax.dynamic_update_slice(out, held[k][q][i][None], (place_of(row), 0, 0))
         return out.reshape(group_rows * length, width)
 
-    def scatter_rows(values, place_of):
-        blocks = []
-        for k in range(2):
-            terms = {}
-            for q in range(count):
-                terms[q] = jnp.stack(
-                    [pick(values, place_of((me ^ q) * micro + k * half + i)) for i in range(half)]
-                )
-            blocks.append(terms)
-        return jnp.concatenate(cube_scatter(blocks, count, "shard"))
-
     dealt_place = lambda row: pick(inverse, row)
     same_place = lambda row: row
 
@@ -647,7 +864,6 @@
     queries = (mm(normed_one, weight_query) + bias_query).astype(BF)
     value_pad = jnp.concatenate([jnp.zeros((HD,), F32), bias_value])
     keyvals = (mm(normed_one, weight_keyval) + value_pad).astype(BF)
-    kept = []
     attended = []
     for m in range(micro):
         mask = jnp.repeat(allowed_pairs(own_lengths[m], length), HEADS, axis=0)
@@ -661,7 +877,6 @@
         probs = powers / totals
         probs_low = probs.astype(BF)
         attended.append(mm(probs_low, value_rows).reshape(length, width).astype(BF))
-        kept.append((mask, query_rows, key_rows, value_rows, top + jnp.log(totals), probs_low))
     attended = jnp.concatenate(attended)
     middle = inputs + mm(attended, weight_out) + bias_out
     unit_two, rate_two = normalize(middle)
@@ -675,7 +890,7 @@
     grad_down = grad_down.reshape(group_rows * length, width)
     grad_hidden = gelu_pull(mm_nt(grad_down, weight_down))[0].astype(BF)
     grad_two = mm_nt(grad_hidden, weight_up).astype(BF).reshape(group_rows, length, width)
-    grad_normed_two = scatter_rows(grad_two, dealt_place).astype(F32).reshape(rows, width)
+    slices = jnp.stack([pick(grad_two, inverse[r]) for r in range(group_rows)]).reshape(count, rows, width)
     down_grad = mm_tn(activated, grad_down).astype(BF)
     up_grad = mm_tn(normed_two, grad_hidden).astype(BF)
 
@@ -685,79 +900,57 @@
         at = dealt_place(me * micro + m)
         row = (pick(result, at).astype(F32) + middle_rows[m]).astype(BF)
         result = lax.dynamic_update_slice(result, row[None], (at, 0, 0))
-    result = scatter_rows(result, same_place).astype(F32)
+    result = lax.psum_scatter(
+        result.reshape(group_rows * length, width), "shard", scatter_dimension=0, tiled=True
+    )
+    result = result.reshape(micro, length, width).astype(F32)
     block_output = ((result + bias_down) * own_live[:, :, None]).astype(BF)
 
     own_cot = jnp.stack([pick(cot_rows, dealt_place(me * micro + m)) for m in range(micro)])
     given_live = jnp.stack([live(own_lengths[m], length) for m in range(micro)])
-    grad_out = (own_cot.astype(F32) * given_live[:, :, None]).reshape(rows, width)
-    down_bias_grad = jnp.sum(grad_out.astype(BF).astype(F32), axis=0)
-    back_two, gain_two_grad, shift_two_grad = norm_back(grad_normed_two, unit_two, rate_two, gain_two)
-    grad_middle = back_two + grad_out
-    grad_branch = grad_middle.astype(BF)
-    out_bias_grad = jnp.sum(grad_branch.astype(F32), axis=0)
-    out_grad = mm_tn(attended, grad_branch).astype(BF)
-    grad_attended = mm_nt(grad_branch, weight_out).astype(BF)
-    grad_queries = []
-    grad_keyvals = []
-    for m in range(micro):
-        mask, query_rows, key_rows, value_rows, log_total, probs_low = kept[m]
-        grad_rows = grad_attended[m * length : (m + 1) * length].reshape(length * HEADS, HD)
-        again = jnp.where(mask, mm_nt(query_rows, key_rows) * scale, NEGATIVE)
-        probs = jnp.exp(again - log_total)
-        grad_probs = mm_nt(grad_rows, value_rows)
-        centre = jnp.sum(probs * grad_probs, axis=1, keepdims=True)
-        grad_scores = (probs * (grad_probs - centre)).astype(BF)
-        grad_queries.append((mm(grad_scores, key_rows) * scale).reshape(length, width).astype(BF))
-        grad_keys = mm_tn(grad_scores, query_rows) * scale
-        grad_values = mm_tn(probs_low, grad_rows)
-        grad_keyvals.append(jnp.concatenate([grad_keys, grad_values], axis=1).astype(BF))
-    grad_queries = jnp.concatenate(grad_queries)
-    grad_keyvals = jnp.concatenate(grad_keyvals)
-    query_grad = mm_tn(normed_one, grad_queries).astype(BF)
-    keyval_grad = mm_tn(normed_one, grad_keyvals).astype(BF)
-    grad_normed_one = mm_nt(grad_queries, weight_query) + mm_nt(grad_keyvals, weight_keyval)
-    back_one, gain_one_grad, shift_one_grad = norm_back(grad_normed_one, unit_one, rate_one, gain_one)
-    input_grad = (back_one + grad_middle).astype(BF).reshape(micro, length, width)
-
-    up_bias_part = jnp.sum(grad_hidden.astype(F32), axis=0).reshape(groups, 1, block)
-    value_bias_grad = jnp.sum(grad_keyvals[:, HD:].astype(F32), axis=0)
-    query_bias_grad = jnp.sum(grad_queries.astype(F32), axis=0)
-    spot = (jnp.arange(count, dtype=jnp.int32) == me)[None, :, None]
-    up_bias_grad = jnp.where(spot, up_bias_part, 0.0).reshape(-1)
-    vectors = (
-        gain_one_grad, shift_one_grad, query_bias_grad, value_bias_grad, out_bias_grad,
-        gain_two_grad, shift_two_grad, up_bias_grad, down_bias_grad,
+    grad_out = (own_cot.astype(F32) * given_live[:, :, None]).reshape(rows, width).astype(BF)
+    per = groups // count
+    up_bias_part = jnp.sum(grad_hidden.astype(F32), axis=0).reshape(count, per, 1, block)
+    spot = (jnp.arange(count, dtype=jnp.int32) == me)[None, None, :, None]
+    up_bias_part = jnp.where(spot, up_bias_part, 0.0).reshape(count, 2, -1)
+    down_bias_part = jnp.sum(grad_out.astype(F32), axis=0).reshape(count, 2, -1)
+    early = jnp.concatenate([up_bias_part, down_bias_part], axis=2).astype(BF)
+    fill = -early.shape[2] % (16 * 2 * HD)
+    early = jnp.pad(early, ((0, 0), (0, 0), (0, fill))).reshape(count, 2, -1, 2 * HD)
+
+    bias = jnp.concatenate(
+        [jnp.where(allowed_pairs(own_lengths[m], length), 0.0, NEGATIVE) for m in range(micro)]
     )
-    line = jnp.concatenate([item.reshape(count, -1) for item in vectors], axis=1).astype(BF)
-    unit = 2 * 16 * 2 * HD
-    more = -(-line.shape[1] // unit)
-    line = jnp.pad(line, ((0, 0), (0, more * unit - line.shape[1])))
-    line = line.reshape(count, 2, more * 16, 2 * HD)
-
+    gains = jnp.pad(jnp.stack([gain_one, gain_two]), ((0, 6), (0, 0)))
     cut = lambda x: x.reshape(count, 2, x.shape[0] // count // 2, x.shape[1])
-    terms = [cut(x) for x in (down_grad, up_grad, out_grad, query_grad, keyval_grad)]
-    terms[4] = jnp.concatenate([terms[4], line], axis=2)
-    down_full, up_full, out_full, query_full, last = reduce_all(
-        groups, count, terms, (True, True, False, False, False), (2, 2, 2, 2, 1)
+    near_by = (
+        grad_out, attended, queries, keyvals, normed_one, tokens.reshape(rows, width), bias, gains, weight_keyval,
     )
-    down_full = down_full.reshape(-1, width).astype(F32)
-    up_full = spread(up_full, block)
-    out_full = out_full.reshape(-1, width).astype(F32)
-    query_full = query_full.reshape(-1, width).astype(F32)
-    tall = width // count // 2
-    keyval_full = last[:, 0, :tall].reshape(2 * tall, 2 * HD).astype(F32)
-    summed = last[:, 0, tall:].reshape(-1).astype(F32)
-    parts = []
-    at = 0
-    for item in vectors:
-        size = item.shape[0] // count
-        parts.append(summed[at : at + size])
-        at += size
+    full, input_grad = back_all(
+        groups, count, (cut(down_grad), cut(up_grad)),
+        (slices, weight_query, weight_out, middle), near_by, early,
+    )
+    input_grad = input_grad.reshape(micro, length, width)
+
+    down_full = full[0].reshape(-1, width).astype(F32)
+    up_full = spread(full[1], block)
+    out_full = full[2].reshape(-1, width).astype(F32)
+    query_full = full[3].reshape(-1, width).astype(F32)
+    size = width // count // 2
+    last = full[4][:, 0]
+    keyval_full = last[:, :size].reshape(2 * size, 2 * HD).astype(F32)
+    sums = last[:, size : size + 16, :size].swapaxes(0, 1).reshape(16, 2 * size).astype(F32)
+    gain_two_grad, shift_two_grad, out_bias_grad, gain_one_grad, shift_one_grad, query_bias_grad = sums[:6]
+    short = value_bias.shape[0] * groups
+    value_bias_grad = lax.dynamic_slice(sums[6, :HD], (me * short,), (short,))
+    tail = last[:, size + 16 :].reshape(2, -1).astype(F32)
+    up_bias_grad = tail[:, : hidden // 2].reshape(-1)
+    down_bias_grad = tail[:, hidden // 2 : hidden // 2 + size].reshape(-1)
 
     return (
-        block_output, input_grad, parts[0], parts[1], query_full, parts[2], keyval_full, parts[3],
-        out_full, parts[4], parts[5], parts[6], up_full, parts[7], down_full, parts[8],
+        block_output, input_grad, gain_one_grad, shift_one_grad, query_full, query_bias_grad, keyval_full,
+        value_bias_grad, out_full, out_bias_grad, gain_two_grad, shift_two_grad, up_full, up_bias_grad,
+        down_full, down_bias_grad,
     )
 
 

time: 859 us -> 783 us (0.912)
  waiting for transfers between devices: 89.4 us -> 27.9 us
  matrix products: 144 us -> 105 us
  Pallas kernels: 423 us -> 456 us
  other arithmetic: 74.7 us -> 48.5 us
  between operations: 47 us -> 61.6 us
  local copies, waits for them, and re-layouts: 59 us -> 69 us
    ppermute x8 -> x0, waiting for transfers between devices: 57.2 us -> none  [cube_scatter(): got = lax.ppermute(pack, axis, flips(count, mask))]
    pallas_call x3, Pallas kernels: 423 us -> 456 us  [the longest x1 315 us: back_all(): pl.pallas_call(partial(back_kernel, groups, count, subs, plain, sizes, sh...]
    dot_general x9 -> x2, matrix products: 46.6 us -> 27.7 us  [mm_tn(): lax.dot_general(left, right, (((0,), (0,)), ((), ())), preferred_element_...]
    dot_general x9 -> x4, matrix products: 51.6 us -> 33.8 us  [mm_nt(): lax.dot_general(left, right, (((1,), (1,)), ((), ())), preferred_element_...]
    dynamic_update_slice x15, local copies, waits for them, and re-layouts: 10.5 us -> 20.8 us  [gather_rows(): lax.dynamic_update_slice(out, held[k][q][i][None], (place_of(row), 0, 0))]
    another operation x7 -> x2, other arithmetic: 9.8 us -> 0.66 us  [the longest x1 0.64 us: shards(): gains = jnp.pad(jnp.stack([gain_one, gain_two]), ((0, 6), (0, 0)))]
    convert_element_type x10 -> x5, other arithmetic: 22.8 us -> 19.1 us  [the longest x1 11.8 us: shards(): down_full = full[0].reshape(-1, width).astype(F32)]
    dot_general x9 -> x7, matrix products: 45.7 us -> 43.2 us  [mm(): return jnp.dot(left, right, preferred_element_type=F32)]
  transfers between devices with their start and end apart: 17 -> 10, of which waited for: 6 -> 2; matrix products, arithmetic and copies ran while one was open for 28% -> 20% of each run, Pallas kernels for 34% -> 42%
where the time goes in v3:
time: 783 us; the launch traced here: 776 us
  Pallas kernels  456 us (58%)
  matrix products  105 us (13%)
  local copies, waits for them, and re-layouts  69 us (9%)
  between operations  61.6 us (8%)
  other arithmetic  48.5 us (6%)
  waiting for transfers between devices  27.9 us (4%)
  starting transfers between devices  8.45 us (1%)
    pallas_call x1, Pallas kernels, back_all(): pl.pallas_call(partial(back_kernel, groups, count, subs, plain, sizes, sh...  315 us
    pallas_call x1, Pallas kernels, gather_all(): pl.pallas_call(partial(gather_kernel, groups, count), out_shape=(tall(wq)...  129 us
    dot_general x7, matrix products, mm(): return jnp.dot(left, right, preferred_element_type=F32)  43.2 us
    dot_general x4, matrix products, mm_nt(): lax.dot_general(left, right, (((1,), (1,)), ((), ())), preferred_element_...  33.8 us
    ppermute x8, waiting for transfers between devices, cube_gather(): got = lax.ppermute(pack, axis, flips(count, mask))  27.8 us
    dot_general x2, matrix products, mm_tn(): lax.dot_general(left, right, (((0,), (0,)), ((), ())), preferred_element_...  27.7 us
    dynamic_update_slice x15, local copies, waits for them, and re-layouts, gather_rows(): lax.dynamic_update_slice(out, held[k][q][i][None], (place_of(row), 0, 0))  20.8 us
  transfers between devices with their start and end apart: 10, of which 2 were waited for; matrix products, arithmetic and copies ran while one was open for 20% of the time, Pallas kernels for 42%

profile of v3, /device:TPU:0, one launch (start us, length us, event | category | flops | bytes accessed | tf_op | source)
XLA Modules:
  0.0 775.7 jit_solution(13271634386066420295)
XLA Ops:
  7.2 6.1 concatenate.21
  13.3 1.8 reshape.354
  15.3 1.3 reshape.355.upc
  17.3 129.3 %gather_all.1 = (bf16[2048,2048]{1,0:T(8,128)(2,1)}, bf16[2048,2048]{1,0:T(8,128)(2,1)}, bf16[2048,384]{1,0:T(8,128)(2,1)}, bf16[2048,2048]{1,0:T(8,128)(2,1)}) custom-call(bf16[64,2048]{1,0:T(8,128)(2,1)} %wq.1, bf16[64,2048]{1,0:T(8,128)(2,1)} %wo.1, bf16[64,384]{1,0:T(8,128)(2,1)} %pad_maximum_fusion.5.kvs, bf16[4,64,2048]{2,1,0:T(8,128)(2,1)} %reshape.355.upc), custom_call_target="tpu_custom_call" | custom-call | bytes 100000000 | tf_op jit(solution)/shard_map/gather_all/pallas_call | solution.py:261
  146.9 2.5 broadcast.175.clone.1
  150.3 1.2 slice_bitcast_fusion.12
  152.1 1.5 collective-permute-start.4
  165.2 1.1 slice.180
  166.3 1.0 reshape.356
  168.1 1.5 slice_convert_fusion.1
  175.4 0.9 fusion.53
  177.4 1.1 copy.43
  181.8 6.0 fusion.8.refs_8_
  187.9 0.9 copy-done.6
  191.7 6.4 fusion.68
  199.0 1.0 slice_bitcast_fusion.10
  200.4 1.4 collective-permute-start
  202.8 1.3 iota_compare_fusion.12
  204.1 1.3 iota_compare_fusion.14
  205.4 1.2 iota_compare_fusion.16
  206.6 1.3 iota_compare_fusion.10
  208.0 1.3 iota_compare_fusion.8
  214.2 2.9 broadcast.175.clone
  238.4 2.3 slice.185.refs_14_
  250.4 1.3 pad_maximum_fusion.3
  252.5 1.3 pad_maximum_fusion.2
  253.8 1.6 collective-permute-start.6
  255.4 1.3 pad_maximum_fusion.1
  257.2 2.3 pad_maximum_fusion
  259.4 1.4 collective-permute-start.2
  260.8 1.9 bitcast_dynamic-update-slice_fusion.1
  262.7 1.9 bitcast_dynamic-update-slice_fusion.3
  264.5 15.4 %collective-permute-done.6 = bf16[2,1,128,2048]{3,2,1,0:T(8,128)(2,1)S(1)} collective-permute-done((bf16[2,1,128,2048]{3,2,1,0:T(8,128)(2,1)S(1)}, bf16[2,1,128,2048]{3,2,1,0:T(8,128)(2,1)S(1)}, u32[]{:S(2)}, u32[]{:S(2)}) %collective-permute-start.6) | collective-permute-done | bytes 1048608 | tf_op jit(solution)/shard_map/ppermute | solution.py:78
  281.6 1.9 bitcast_dynamic-update-slice_fusion
  285.1 1.3 constant_dynamic-slice_fusion.2
  286.4 1.6 fusion.19
  288.0 12.4 %collective-permute-done.2 = bf16[2,1,128,2048]{3,2,1,0:T(8,128)(2,1)} collective-permute-done((bf16[2,1,128,2048]{3,2,1,0:T(8,128)(2,1)}, bf16[2,1,128,2048]{3,2,1,0:T(8,128)(2,1)}, u32[]{:S(2)}, u32[]{:S(2)}) %collective-permute-start.2) | collective-permute-done | bytes 1048608 | tf_op jit(solution)/shard_map/ppermute | solution.py:78
  300.4 1.9 fusion.35
  302.3 1.9 fusion.34
  304.2 1.9 bitcast_dynamic-update-slice_fusion.2
  306.1 1.9 fusion.33
  308.0 1.9 fusion.32
  309.9 1.1 fusion.13.refs_6_
  311.0 2.9 multiply_convert_fusion
  314.0 14.0 %fusion.69 = f32[1024,2048]{1,0:T(8,128)S(1)} fusion(bf16[1024,2048]{1,0:T(8,128)(2,1)} %bitcast.25, bf16[2048,2048]{1,0:T(8,128)(2,1)} %get-tuple-element.39), kind=kOutput, calls=%fused_computation.206 | convolution fusion | flops 8589934592 | bytes 20971520 | tf_op jit(solution)/shard_map/dot_general | solution.py:24
  328.0 3.4 copy-done.34
  331.3 12.7 %convolution_convert_fusion.1 = bf16[2048,2048]{1,0:T(8,128)(2,1)} fusion(bf16[1024,2048]{1,0:T(8,128)(2,1)S(1)} %bitcast.197, f32[1024,2048]{1,0:T(8,128)S(1)} %fusion.69, f32[2048]{0:T(1024)S(1)} %bitcast.216), kind=kOutput, calls=%fused_computation.14 | convolution fusion | flops 8615100416 | bytes 20979712 | tf_op jit(solution)/shard_map/dot_general | solution.py:28
  344.1 18.8 %convert_reduce_fusion = (bf16[2048]{0:T(1024)(128)(2,1)S(1)}, bf16[1024,2048]{1,0:T(8,128)(2,1)S(1)}) fusion(f32[1024,2048]{1,0:T(8,128)} %copy-done.34, f32[2048]{0:T(1024)S(1)} %bitcast.217, bf16[1024,2048]{1,0:T(8,128)(2,1)} %bitcast.198, bf16[2048,2048]{1,0:T(8,128)(2,1)} %all-gather.2.cloned.1.call-done), kind=kOutput, calls=%fused_computation.10 | convolution fusion | flops 8638167040 | bytes 25178112 | tf_op jit(solution)/shard_map/dot_general | solution.py:32
  362.9 14.4 %convolution_convert_fusion.2 = bf16[1024,2048]{1,0:T(8,128)(2,1)} fusion(bf16[1024,2048]{1,0:T(8,128)(2,1)S(1)} %get-tuple-element.61, bf16[2048,2048]{1,0:T(8,128)(2,1)} %get-tuple-element.39), kind=kOutput, calls=%fused_computation.15 | convolution fusion | flops 8592031744 | bytes 16777216 | tf_op jit(solution)/shard_map/dot_general | solution.py:32
  377.3 15.7 %convolution_convert_fusion.3 = bf16[1024,2048]{1,0:T(8,128)(2,1)S(1)} fusion(bf16[2048,2048]{1,0:T(8,128)(2,1)} %all-gather.2.cloned.1.call-done, f32[1024,2048]{1,0:T(8,128)} %copy-done.34, f32[2048]{0:T(1024)S(1)} %bitcast.218), kind=kOutput, calls=%fused_computation.16 | convolution fusion | flops 8613003264 | bytes 20979712 | tf_op jit(solution)/shard_map/dot_general | solution.py:24
  393.3 2.0 copy-done.3
  396.2 1.2 dynamic-slice_dynamic-update-slice_fusion.7
  397.4 1.7 dynamic-slice_dynamic-update-slice_fusion.6
  399.1 1.1 dynamic-slice_dynamic-update-slice_fusion.5
  400.2 1.1 dynamic-slice_dynamic-update-slice_fusion.4
  401.6 14.9 %convolution_convert_fusion = bf16[2048,2048]{1,0:T(8,128)(2,1)} fusion(bf16[1024,2048]{1,0:T(8,128)(2,1)} %bitcast.25, bf16[1024,2048]{1,0:T(8,128)(2,1)S(1)} %copy-done.36), kind=kOutput, calls=%fused_computation.13 | convolution fusion | flops 8594128896 | bytes 16777216 | tf_op jit(solution)/shard_map/dot_general | solution.py:28
  416.5 315.4 %back_all.1 = (bf16[2,4,256,2048]{3,2,1,0:T(8,128)(2,1)}, bf16[2,4,256,2048]{3,2,1,0:T(8,128)(2,1)}, bf16[2,1,256,2048]{3,2,1,0:T(8,128)(2,1)}, bf16[2,1,256,204...) custom-call(bf16[4,2,256,2048]{3,2,1,0:T(8,128)(2,1)} %bitcast.191, ...), custom_call_target="tpu_custom_call" | custom-call | bytes 200000000 | tf_op jit(solution)/shard_map/back_all/pallas_call | solution.py:738
  732.0 1.0 slice.263
  734.9 10.9 %spread.1 = f32[512,8192]{1,0:T(8,128)} custom-call(bf16[2,4,256,2048]{3,2,1,0:T(8,128)(2,1)} %get-tuple-element.46.x_ref), custom_call_target="tpu_custom_call" | custom-call | tf_op jit(solution)/shard_map/spread/pallas_call | solution.py:765
  747.8 2.7 bitcast_convert_fusion.2
  750.5 2.7 bitcast_convert_fusion.1
  753.2 11.8 %bitcast_convert_fusion = f32[2048,2048]{1,0:T(8,128)} fusion(bf16[2,4,256,2048]{3,2,1,0:T(8,128)(2,1)} %get-tuple-element.47), kind=kLoop, calls=%fused_computation.9 | loop fusion | flops 4194304 | bytes 25165824 | tf_op jit(solution)/shard_map/convert_element_type | solution.py:935
  764.9 2.5 fusion.12
  767.4 1.0 copy.82
  (183 shorter events, 29.7 us)
Async XLA Ops:
  7.2 9.5 %copy-start.24 = (bf16[64,256]{1,0:T(8,128)(2,1)S(1)}, bf16[64,256]{1,0:T(8,128)(2,1)}, u32[]{:S(2)}) copy-start(bf16[64,256]{1,0:T(8,128)(2,1)} %param.26) | copy-start | bytes 98308
  7.2 336.9 %all-gather.2.cloned.1.call-start = ((), (), s32[]{:S(2)}) async-start(), calls=%async_computation.1 | async-start | bytes 9437184 | tf_op jit(solution)/shard_map/all_gather | solution.py:828
  15.3 134.1 %copy-start.10 = (bf16[2,128,2048]{2,1,0:T(8,128)(2,1)S(1)}, bf16[2,128,2048]{2,1,0:T(8,128)(2,1)}, u32[]{:S(2)}) copy-start(bf16[2,128,2048]{2,1,0:T(8,128)(2,1)} %param.19) | copy-start | bytes 3145732
  146.6 7.0 copy-start.33
  146.6 618.3 %reduce-scatter.2.cloned.1.call-start = ((), (), s32[]{:S(2)}) async-start(), calls=%async_computation.2 | async-start | bytes 5242880 | tf_op jit(solution)/shard_map/reduce_scatter | solution.py:903
  146.9 22.7 %copy-start.1 = (bf16[2,128,2048]{2,1,0:T(8,128)(2,1)S(1)}, bf16[2,128,2048]{2,1,0:T(8,128)(2,1)}, u32[]{:S(2)}) copy-start(bf16[2,128,2048]{2,1,0:T(8,128)(2,1)} %param.18) | copy-start | bytes 3145732
  149.4 26.0 %copy-start.17 = (s32[8,4]{0,1:T(4,128)S(1)}, s32[8,4]{0,1:T(4,128)}, u32[]{:S(2)}) copy-start(s32[8,4]{0,1:T(4,128)} %param.20) | copy-start | bytes 388
  151.4 101.0 %collective-permute-start.5 = (bf16[1,1,128,2048]{3,2,1,0:T(8,128)(2,1)}, bf16[1,1,128,2048]{3,2,1,0:T(8,128)(2,1)}, u32[]{:S(2)}, u32[]{:S(2)}) collective-permute-start(bf16[1,1,128,2048]{3,2,1,0:T(8,128)(2,1)} %get-tuple-element.66), channel_id=1, source_target_pairs={{0,2},{1,3},{2,0},{3,1},{4,6},{5,7},{6,4},{7,5},{8,10},{9,11},{10,... | collective-permute-start | bytes 1572872 | tf_op jit(solution)/shard_map/ppermute | solution.py:78
  152.1 98.2 %collective-permute-start.4 = (bf16[1,1,128,2048]{3,2,1,0:T(8,128)(2,1)}, bf16[1,1,128,2048]{3,2,1,0:T(8,128)(2,1)}, u32[]{:S(2)}, u32[]{:S(2)}) collective-permute-start(bf16[1,1,128,2048]{3,2,1,0:T(8,128)(2,1)} %get-tuple-element.67), channel_id=1, source_target_pairs={{0,1},{1,0},{2,3},{3,2},{4,5},{5,4},{6,7},{7,6},{8,9},{9,8},{10,11... | collective-permute-start | bytes 1572872 | tf_op jit(solution)/shard_map/ppermute | solution.py:78
  153.6 0.5 copy-start.25
  164.4 16.9 %copy-start.13 = (bf16[2048,384]{1,0:T(8,128)(2,1)S(1)}, bf16[2048,384]{1,0:T(8,128)(2,1)}, u32[]{:S(2)}) copy-start(bf16[2048,384]{1,0:T(8,128)(2,1)} %get-tuple-element.36) | copy-start | bytes 4718596
  169.6 11.2 %copy-start.18 = (f32[32,64]{1,0:T(8,128)}, f32[32,64]{1,0:T(8,128)S(1)}, u32[]{:S(2)}) copy-start(f32[32,64]{1,0:T(8,128)S(1)} %get-tuple-element.75) | copy-start | bytes 24580
  176.7 4.1 copy-start.27
  176.7 4.1 copy-start.29
  181.3 6.5 copy-start.5
  181.8 9.2 %copy-start.16 = (bf16[256,256]{1,0:T(8,128)(2,1)}, bf16[256,256]{1,0:T(8,128)(2,1)S(1)}, u32[]{:S(2)}) copy-start(bf16[256,256]{1,0:T(8,128)(2,1)S(1)} %fusion.18.refs_9_) | copy-start | bytes 393220
  181.8 7.2 copy-start.14
  187.8 1.0 copy-start.6
  190.8 0.9 copy-start.31
  191.6 6.4 copy-start.9
  191.7 6.8 copy-start.22
  191.7 6.8 copy-start.23
  198.1 195.1 %copy-start = (f32[256,2048]{1,0:T(8,128)}, f32[256,2048]{1,0:T(8,128)S(1)}, u32[]{:S(2)}) copy-start(f32[256,2048]{1,0:T(8,128)S(1)} %get-tuple-element.124.refs_5_) | copy-start | bytes 6291460
  198.1 3.7 copy-start.26
  198.1 3.8 copy-start.30
  198.1 14.5 %copy-start.19 = (f32[32,64]{1,0:T(8,128)S(1)}, f32[32,64]{1,0:T(8,128)}, u32[]{:S(2)}) copy-start(f32[32,64]{1,0:T(8,128)} %copy-done.18) | copy-start | bytes 24580
  198.1 16.0 %copy-start.28 = (s32[128]{0:T(128)S(1)}, s32[128]{0:T(128)}, u32[]{:S(2)}) copy-start(s32[128]{0:T(128)} %copy-done.27) | copy-start | bytes 1540
  200.0 57.1 %collective-permute-start.1 = (bf16[1,1,128,2048]{3,2,1,0:T(8,128)(2,1)}, bf16[1,1,128,2048]{3,2,1,0:T(8,128)(2,1)}, u32[]{:S(2)}, u32[]{:S(2)}) collective-permute-start(bf16[1,1,128,2048]{3,2,1,0:T(8,128)(2,1)} %get-tuple-element.69), channel_id=1, source_target_pairs={{0,2},{1,3},{2,0},{3,1},{4,6},{5,7},{6,4},{7,5},{8,10},{9,11},{10,... | collective-permute-start | bytes 1572872 | tf_op jit(solution)/shard_map/ppermute | solution.py:78
  200.4 55.0 %collective-permute-start = (bf16[1,1,128,2048]{3,2,1,0:T(8,128)(2,1)}, bf16[1,1,128,2048]{3,2,1,0:T(8,128)(2,1)}, u32[]{:S(2)}, u32[]{:S(2)}) collective-permute-start(bf16[1,1,128,2048]{3,2,1,0:T(8,128)(2,1)} %get-tuple-element.70), channel_id=1, source_target_pairs={{0,1},{1,0},{2,3},{3,2},{4,5},{5,4},{6,7},{7,6},{8,9},{9,8},{10,11... | collective-permute-start | bytes 1572872 | tf_op jit(solution)/shard_map/ppermute | solution.py:78
  214.2 26.6 %copy-start.20 = (f32[32,64]{1,0:T(8,128)S(1)}, f32[32,64]{1,0:T(8,128)}, u32[]{:S(2)}) copy-start(f32[32,64]{1,0:T(8,128)} %get-tuple-element.73) | copy-start | bytes 24580
  251.7 29.1 %collective-permute-start.7 = (bf16[2,1,128,2048]{3,2,1,0:T(8,128)(2,1)S(1)}, bf16[2,1,128,2048]{3,2,1,0:T(8,128)(2,1)S(1)}, u32[]{:S(2)}, u32[]{:S(2)}) collective-permute-start(bf16[2,1,128,2048]{3,2,1,0:T(8,128)(2,1)S(1)} %pad_maximum_fusion.3), channel_id=1, source_target_pairs={{0,2},{1,3},{2,0},{3,1},{4,6},{5,7},{6,4},{7,5},{8,10},{9,11},{10,... | collective-permute-start | bytes 3145736 | tf_op jit(solution)/shard_map/ppermute | solution.py:78
  253.8 26.2 %collective-permute-start.6 = (bf16[2,1,128,2048]{3,2,1,0:T(8,128)(2,1)S(1)}, bf16[2,1,128,2048]{3,2,1,0:T(8,128)(2,1)S(1)}, u32[]{:S(2)}, u32[]{:S(2)}) collective-permute-start(bf16[2,1,128,2048]{3,2,1,0:T(8,128)(2,1)S(1)} %pad_maximum_fusion.2), channel_id=1, source_target_pairs={{0,1},{1,0},{2,3},{3,2},{4,5},{5,4},{6,7},{7,6},{8,9},{9,8},{10,11... | collective-permute-start | bytes 3145736 | tf_op jit(solution)/shard_map/ppermute | solution.py:78
  256.7 45.6 %collective-permute-start.3 = (bf16[2,1,128,2048]{3,2,1,0:T(8,128)(2,1)S(1)}, bf16[2,1,128,2048]{3,2,1,0:T(8,128)(2,1)}, u32[]{:S(2)}, u32[]{:S(2)}) collective-permute-start(bf16[2,1,128,2048]{3,2,1,0:T(8,128)(2,1)S(1)} %pad_maximum_fusion.1), channel_id=1, source_target_pairs={{0,2},{1,3},{2,0},{3,1},{4,6},{5,7},{6,4},{7,5},{8,10},{9,11},{10,... | collective-permute-start | bytes 3145736 | tf_op jit(solution)/shard_map/ppermute | solution.py:78
  259.4 41.0 %collective-permute-start.2 = (bf16[2,1,128,2048]{3,2,1,0:T(8,128)(2,1)}, bf16[2,1,128,2048]{3,2,1,0:T(8,128)(2,1)}, u32[]{:S(2)}, u32[]{:S(2)}) collective-permute-start(bf16[2,1,128,2048]{3,2,1,0:T(8,128)(2,1)} %pad_maximum_fusion), channel_id=1, source_target_pairs={{0,1},{1,0},{2,3},{3,2},{4,5},{5,4},{6,7},{7,6},{8,9},{9,8},{10,11... | collective-permute-start | bytes 3145736 | tf_op jit(solution)/shard_map/ppermute | solution.py:78
  288.0 21.9 %copy-start.2 = (f32[2,128,2048]{2,1,0:T(8,128)S(1)}, f32[2,128,2048]{2,1,0:T(8,128)}, u32[]{:S(2)}) copy-start(f32[2,128,2048]{2,1,0:T(8,128)} %get-tuple-element.65) | copy-start | bytes 6291460
  313.9 14.0 %copy-start.7 = (bf16[8,128,2048]{2,1,0:T(8,128)(2,1)}, bf16[8,128,2048]{2,1,0:T(8,128)(2,1)S(1)}, u32[]{:S(2)}) copy-start(bf16[8,128,2048]{2,1,0:T(8,128)(2,1)S(1)} %multiply_convert_fusion) | copy-start | bytes 12582916
  327.9 3.4 copy-start.34
  362.9 14.4 %copy-start.35 = (bf16[1024,2048]{1,0:T(8,128)(2,1)}, bf16[1024,2048]{1,0:T(8,128)(2,1)S(1)}, u32[]{:S(2)}) copy-start(bf16[1024,2048]{1,0:T(8,128)(2,1)S(1)} %get-tuple-element.61) | copy-start | bytes 12582916
  393.3 2.0 copy-start.3
  396.2 5.2 copy-start.8
  396.2 5.4 copy-start.36
  401.6 14.9 %copy-start.4 = (bf16[8,128,2048]{2,1,0:T(8,128)(2,1)}, bf16[8,128,2048]{2,1,0:T(8,128)(2,1)S(1)}, u32[]{:S(2)}) copy-start(bf16[8,128,2048]{2,1,0:T(8,128)(2,1)S(1)} %dynamic-slice_dynamic-update-slice_fusion) | copy-start | bytes 12582916
  734.9 12.9 %copy-start.12 = (bf16[2,1,256,2048]{3,2,1,0:T(8,128)(2,1)S(1)}, bf16[2,1,256,2048]{3,2,1,0:T(8,128)(2,1)}, u32[]{:S(2)}) copy-start(bf16[2,1,256,2048]{3,2,1,0:T(8,128)(2,1)} %get-tuple-element.44) | copy-start | bytes 6291460
  745.8 4.7 copy-start.11
  753.2 11.8 %copy-start.21 = (f32[2048]{0:T(1024)S(1)}, f32[2048]{0:T(1024)}, u32[]{:S(2)}) copy-start(f32[2048]{0:T(1024)} %reshape.384) | copy-start | bytes 24580
  753.2 11.8 %copy-start.32 = (f32[2,128]{1,0:T(2,128)S(1)}, f32[2,128]{1,0:T(2,128)}, u32[]{:S(2)}) copy-start(f32[2,128]{1,0:T(2,128)} %pad_maximum_fusion.6) | copy-start | bytes 3076
  753.2 14.2 %copy-start.15 = (bf16[256,2048]{1,0:T(8,128)(2,1)S(1)}, bf16[256,2048]{1,0:T(8,128)(2,1)}, u32[]{:S(2)}) copy-start(bf16[256,2048]{1,0:T(8,128)(2,1)} %get-tuple-element.42) | copy-start | bytes 3145732
Sparse Core Ops, SparseCore 0:
  146.7 81.3 all-gather.1
  395.5 74.4 reduce-scatter.1

commit v4 on v3

--- a/solution.py
+++ b/solution.py
@@ -16,7 +16,9 @@
 MESH = pl.DeviceIdType.MESH
 LAG_MID = 2
 LAG_OUT = 4
-NORM_STEP = 4
+NORM_STEP = 5
+AHEAD = 4
+SLICE_STEP = 1
 RING = 6
 
 
@@ -30,55 +32,6 @@
 
 def mm_nt(left, right):
     return lax.dot_general(left, right, (((1,), (1,)), ((), ())), preferred_element_type=F32)
-
-
-def normalize(values):
-    centre = jnp.mean(values, axis=-1, keepdims=True)
-    offset = values - centre
-    spread = jnp.mean(offset * offset, axis=-1, keepdims=True)
-    rate = lax.rsqrt(spread + EPS)
-    return offset * rate, rate
-
-
-def row_ends(lengths_row):
-    docs = lengths_row.shape[0]
-    at = jnp.arange(docs, dtype=jnp.int32)
-    return jnp.sum(jnp.where(at[None, :] <= at[:, None], lengths_row[None, :], 0), axis=1)
-
-
-def live(lengths_row, length):
-    places = jnp.arange(length, dtype=jnp.int32)
-    return (places < jnp.sum(lengths_row)).astype(F32)
-
-
-def allowed_pairs(lengths_row, length):
-    ends = row_ends(lengths_row)
-    places = jnp.arange(length, dtype=jnp.int32)
-    segment = jnp.sum((places[:, None] >= ends[None, :]).astype(jnp.int32), axis=1)
-    return (segment[:, None] == segment[None, :]) & (places[None, :] <= places[:, None])
-
-
-def flips(count, mask):
-    return [(i, i ^ mask) for i in range(count)]
-
-
-def cube_orders(count):
-    order = list(range(count.bit_length() - 1))
-    return order, order[::-1]
-
-
-def cube_gather(halves, count, axis):
-    orders = cube_orders(count)
-    held = [{0: half} for half in halves]
-    for step in range(len(orders[0])):
-        for k in range(2):
-            mask = 1 << orders[k][step]
-            keys = sorted(held[k])
-            pack = jnp.stack([held[k][q] for q in keys])
-            got = lax.ppermute(pack, axis, flips(count, mask))
-            for i, q in enumerate(keys):
-                held[k][q ^ mask] = got[i]
-    return held
 
 
 def near_first(count):
@@ -98,7 +51,7 @@
 
 
 def gather_kernel(
-    groups, count, wq, wo, kvs, upc, q_all, o_all, kvs_all, up_all,
+    groups, count, wq, wo, wkv, small, upc, q_all, o_all, kv_all, small_all, up_all,
     zs, zr, ps, pr, bs, br, us, ur, loc,
 ):
     chips = groups // 2
@@ -134,18 +87,20 @@
     def wait(ref, sem):
         pltpu.make_async_copy(ref, ref, sem).wait()
 
-    own = (wq, wo, kvs)
-    whole = (q_all, o_all, kvs_all)
-    parity = (0, 1, 0)
-    size = wq.shape[0]
+    own = (wq, wo, wkv, small)
+    whole = (q_all, o_all, kv_all, small_all)
+    parity = (0, 1, 0, 1)
+    size = [x.shape[0] for x in own]
+    full = len(own)
+    cuts = (full, full + 1)
     up_size = upc.shape[1]
     up_half = up_size * count // 2
 
     def spot(a, z, col):
-        if a < 3:
-            at = ((z * 2 + c) * count + col) * size
-            return whole[a].at[pl.ds(pl.multiple_of(at, 16), size)]
-        at = (z * 2 + c) * up_half * 2 + (a - 3) * up_half
+        if a < full:
+            at = ((z * 2 + c) * count + col) * size[a]
+            return whole[a].at[pl.ds(pl.multiple_of(at, 16), size[a])]
+        at = (z * 2 + c) * up_half * 2 + (a - full) * up_half
         return up_all.at[pl.ds(pl.multiple_of(at, 16), up_half)]
 
     def along(a, way, hop, src, z):
@@ -174,8 +129,8 @@
     for q in near_first(count):
         to = lax.bitwise_xor(me, q)
         send(upc.at[to], up_rows(me), us, ur.at[q], (g, to))
-    mine = [pltpu.make_async_copy(upc.at[me], up_rows(me), loc.at[3])]
-    for a in range(3):
+    mine = [pltpu.make_async_copy(upc.at[me], up_rows(me), loc.at[full])]
+    for a in range(full):
         mine.append(pltpu.make_async_copy(own[a], spot(a, p, me), loc.at[a]))
     for copy in mine:
         copy.start()
@@ -185,18 +140,18 @@
             pl.when(may_send(way, 1))(partial(along, a, way, 1, src, p))
         aside(a, src, p, 0)
 
-    for a in range(3):
+    for a in range(full):
         first(a, own[a])
         across(a, own[a], p, 0)
     mine[0].wait()
     for q in near_first(count):
         wait(up_rows(me), ur.at[q])
-    for a in (3, 4):
+    for a in cuts:
         first(a, spot(a, p, me))
 
     def plane(z):
         for q in near_first(count):
-            for a in range(3):
+            for a in range(full):
                 ref = spot(a, z, lax.bitwise_xor(me, q))
                 wait(ref, pr.at[a, z, q])
                 across(a, ref, z, q)
@@ -222,37 +177,37 @@
                     pl.when(may_send(way, hop + 1))(
                         partial(along, a, way, hop + 1, ref, z)
                     )
-                if a < 3:
+                if a < full:
                     across(a, ref, z, 0)
                 aside(a, ref, z, 0)
 
     for hop in range(1, chips):
-        for a in range(3):
+        for a in range(full):
             arrive(a, hop)
         planes(hop - 1)
-        for a in (3, 4):
+        for a in cuts:
             arrive(a, hop)
     planes(chips - 1)
 
     for copy in mine[1:]:
         copy.wait()
-    for a in range(5):
+    for a in range(full + 2):
         for way in range(2):
             for hop in range(1, chips):
                 pl.when(may_send(way, hop))(
                     partial(wait, spot(a, p, me), zs.at[a, way, hop])
                 )
-    for a in range(3):
-        wait(whole[a].at[pl.ds(0, chips * (count - 1) * size)], ps.at[a])
-        wait(whole[a].at[pl.ds(0, chips * count * size)], bs.at[a])
-        wait(whole[a].at[pl.ds(0, chips * count * size)], br.at[a])
-    for a in (3, 4):
+    for a in range(full):
+        wait(whole[a].at[pl.ds(0, chips * (count - 1) * size[a])], ps.at[a])
+        wait(whole[a].at[pl.ds(0, chips * count * size[a])], bs.at[a])
+        wait(whole[a].at[pl.ds(0, chips * count * size[a])], br.at[a])
+    for a in cuts:
         wait(up_all.at[pl.ds(0, chips * up_half)], bs.at[a])
         wait(up_all.at[pl.ds(0, chips * up_half)], br.at[a])
     wait(up_all.at[pl.ds(0, (count - 1) * up_size)], us)
 
 
-def gather_all(groups, count, wq, wo, kvs, upc):
+def gather_all(groups, count, wq, wo, wkv, small, upc):
     chips = groups // 2
     n = groups * count
     any_ = pl.BlockSpec(memory_space=pl.ANY)
@@ -261,27 +216,205 @@
     return pl.pallas_call(
         partial(gather_kernel, groups, count),
         out_shape=(
-            tall(wq), tall(wo), tall(kvs),
+            tall(wq), tall(wo), tall(wkv), tall(small),
             jax.ShapeDtypeStruct((n * upc.shape[1], upc.shape[2]), upc.dtype),
         ),
-        in_specs=[any_] * 4,
-        out_specs=(any_,) * 4,
+        in_specs=[any_] * 5,
+        out_specs=(any_,) * 5,
         scratch_shapes=[
-            dma((5, 2, chips)), dma((5, 2, chips)), dma((3,)), dma((3, chips, count)),
-            dma((5,)), dma((5,)), dma, dma((count,)), dma((4,)),
+            dma((6, 2, chips)), dma((6, 2, chips)), dma((4,)), dma((4, chips, count)),
+            dma((6,)), dma((6,)), dma, dma((count,)), dma((5,)),
         ],
         compiler_params=pltpu.CompilerParams(collective_id=1, has_side_effects=True),
         cost_estimate=pl.CostEstimate(flops=0, bytes_accessed=100_000_000, transcendentals=0),
         name="gather_all",
-    )(wq, wo, kvs, upc)
+    )(wq, wo, wkv, small, upc)
+
+
+def attend_kernel(
+    groups, count, tokens, small_all, lengths, cot, wq, wo, wkv,
+    near_all, cot_all, normed, queries, keyvals, attended, middle, vectors, up_part, bias,
+    wq_v, wo_v, wkv_v, second, ws, ns, nr, cs, cr, loc,
+):
+    g, me = lax.axis_index("grp"), lax.axis_index("shard")
+    barrier = pltpu.get_barrier_semaphore()
+    nearest = [1 << d for d in range(count.bit_length() - 1)]
+    for m in nearest:
+        pl.semaphore_signal(
+            barrier, inc=1, device_id=(g, lax.bitwise_xor(me, m)), device_id_type=MESH
+        )
+    pl.semaphore_wait(barrier, len(nearest))
+
+    loads = [
+        pltpu.make_async_copy(a, b, ws.at[i])
+        for i, (a, b) in enumerate(((wkv, wkv_v), (wq, wq_v), (wo, wo_v)))
+    ]
+    for load in loads:
+        load.start()
+
+    rows, width = tokens.shape
+    length = bias.shape[1]
+    half = rows // 2
+    near = near_first(count)
+    place = lambda ref, k, col: ref.at[pl.ds(pl.multiple_of(col * rows + k * half, 16), half)]
+
+    def send(src, dst, send_sem, recv_sem, m):
+        pltpu.make_async_remote_copy(
+            src_ref=src, dst_ref=dst, send_sem=send_sem, recv_sem=recv_sem,
+            device_id=(g, lax.bitwise_xor(me, m)), device_id_type=MESH,
+        ).start()
+
+    def wait(ref, sem):
+        pltpu.make_async_copy(ref, ref, sem).wait()
+
+    def pass_on(ref, src, k, q, sends, gets):
+        for m in cube_tree(count, k, q):
+            send(src, place(ref, k, lax.bitwise_xor(me, q)), sends.at[k], gets.at[k, q ^ m], m)
+
+    def take_all(ref, sends, gets):
+        for q in near:
+            for k in range(2):
+                got = place(ref, k, lax.bitwise_xor(me, q))
+                wait(got, gets.at[k, q])
+                pass_on(ref, got, k, q, sends, gets)
+
+    for k in range(2):
+        pass_on(cot_all, cot.at[pl.ds(k * half, half)], k, 0, cs, cr)
+    own_cot = pltpu.make_async_copy(cot, cot_all.at[pl.ds(pl.multiple_of(me * rows, 16), rows)], loc.at[0])
+    own_cot.start()
+
+    lot = small_all.shape[0] // (groups * count)
+    piece = width // (groups * count)
+    join = 128 // piece
+    for k in range(width // 128):
+        parts = [
+            small_all[(k * join + i) * lot : (k * join + i) * lot + 16, :piece].astype(F32) for i in range(join)
+        ]
+        vectors[:, k * 128 : (k + 1) * 128] = jnp.concatenate(parts, axis=1)
+    total = small_all[0:16, :].astype(F32)
+    for d in range(1, groups * count):
+        total = total + small_all[d * lot : d * lot + 16, :].astype(F32)
+    vectors[7:8, :128] = total[7:8, :]
+    pieces = []
+    for k in range(groups):
+        at = pl.multiple_of((k * count + me) * lot, 16)
+        mine = small_all[pl.ds(at, 16), :].astype(F32)
+        pieces += [mine[8 + r : 9 + r, :piece] for r in range(up_part.shape[1] // groups // piece)]
+    for k in range(up_part.shape[1] // 128):
+        up_part[:, k * 128 : (k + 1) * 128] = jnp.concatenate(pieces[k * join : (k + 1) * join], axis=1)
+
+    band = 32
+    spots = [lax.broadcasted_iota(jnp.int32, (length, length), d) for d in range(2)]
+    for m in range(rows // length):
+        segments = [jnp.zeros((length, length), jnp.int32)] * 2
+        stop = 0
+        for k in range(lengths.shape[1]):
+            stop = stop + lengths[me * (rows // length) + m, k]
+            segments = [a + (spot >= stop).astype(jnp.int32) for a, spot in zip(segments, spots)]
+        allowed = (segments[0] == segments[1]) & (spots[1] <= spots[0])
+        bias[m * length : (m + 1) * length, :] = jnp.where(allowed, 0.0, NEGATIVE)
+
+    def norm(x, gain, shift):
+        offset = x - jnp.mean(x, axis=1, keepdims=True)
+        rate = lax.rsqrt(jnp.mean(offset * offset, axis=1, keepdims=True) + EPS)
+        return (offset * rate * gain + shift).astype(BF)
+
+    @pl.loop(0, rows // band)
+    def _(i):
+        at = pl.ds(pl.multiple_of(i * band, band), band)
+        normed[at, :] = norm(tokens[at, :].astype(F32), vectors[0:1, :], vectors[1:2, :])
+
+    loads[0].wait()
+    kv = jnp.dot(normed[...], wkv_v[...], preferred_element_type=F32)
+    keyvals[:, :HD] = kv[:, :HD].astype(BF)
+    keyvals[:, HD:] = (kv[:, HD:] + vectors[7:8, :HD]).astype(BF)
+    loads[1].wait()
+    tile = 2 * HD
+    scale = HD**-0.5
+    fold = lambda x: jnp.concatenate([x[:, h * HD : (h + 1) * HD] for h in range(tile // HD)], axis=0)
+
+    @pl.loop(0, width // tile)
+    def _(i):
+        cols = pl.ds(pl.multiple_of(i * tile, tile), tile)
+        query = jnp.dot(normed[...], wq_v[:, cols], preferred_element_type=F32)
+        query = (query + vectors[2:3, cols]).astype(BF)
+        queries[:, cols] = query
+        for m in range(rows // length):
+            at = pl.ds(m * length, length)
+            q = fold(query[m * length : (m + 1) * length])
+            k, v = keyvals[at, :HD], keyvals[at, HD:]
+            shut = jnp.concatenate([bias[at, :]] * (tile // HD), axis=0)
+            s = lax.dot_general(q, k, (((1,), (1,)), ((), ())), preferred_element_type=F32) * scale + shut
+            e = jnp.exp(s - jnp.max(s, axis=1, keepdims=True))
+            probs = (e / jnp.sum(e, axis=1, keepdims=True)).astype(BF)
+            got = jnp.dot(probs, v, preferred_element_type=F32).astype(BF)
+            for h in range(tile // HD):
+                attended[at, pl.ds(pl.multiple_of(i * tile + h * HD, HD), HD)] = got[
+                    h * length : (h + 1) * length
+                ]
+
+    loads[2].wait()
+    wide = min(512, width)
+
+    @pl.loop(0, width // wide)
+    def _(i):
+        cols = pl.ds(pl.multiple_of(i * wide, wide), wide)
+        branch = jnp.dot(attended[...], wo_v[:, cols], preferred_element_type=F32)
+        middle[:, cols] = tokens[:, cols].astype(F32) + branch + vectors[3:4, cols]
+
+    take_all(cot_all, cs, cr)
+    for k in range(2):
+
+        @pl.loop(k * half // band, (k + 1) * half // band)
+        def _(i):
+            at = pl.ds(pl.multiple_of(i * band, band), band)
+            second[at, :] = norm(middle[at, :], vectors[4:5, :], vectors[5:6, :])
+
+        pass_on(near_all, second.at[pl.ds(k * half, half)], k, 0, ns, nr)
+    own = pltpu.make_async_copy(second, near_all.at[pl.ds(pl.multiple_of(me * rows, 16), rows)], loc.at[1])
+    own.start()
+    take_all(near_all, ns, nr)
+    own_cot.wait()
+    own.wait()
+    for k in range(2):
+        wait(cot_all.at[pl.ds(0, (count - 1) * half)], cs.at[k])
+        wait(near_all.at[pl.ds(0, (count - 1) * half)], ns.at[k])
+
+
+def attend(groups, count, tokens, small_all, lengths, cot, wq, wo, wkv, hidden, length):
+    rows, width = tokens.shape
+    any_, vmem = pl.BlockSpec(memory_space=pl.ANY), pl.BlockSpec(memory_space=pltpu.VMEM)
+    dma = pltpu.SemaphoreType.DMA
+    shape = jax.ShapeDtypeStruct
+    return pl.pallas_call(
+        partial(attend_kernel, groups, count),
+        out_shape=(
+            shape((count * rows, width), BF), shape((count * rows, width), BF), shape((rows, width), BF),
+            shape((rows, width), BF), shape((rows, 2 * HD), BF), shape((rows, width), BF),
+            shape((rows, width), F32), shape((16, width), F32), shape((1, hidden), F32),
+            shape((rows, length), F32),
+        ),
+        in_specs=[vmem, vmem, pl.BlockSpec(memory_space=pltpu.SMEM), any_, any_, any_, any_],
+        out_specs=(any_, any_) + (vmem,) * 8,
+        scratch_shapes=[
+            pltpu.VMEM(wq.shape, BF), pltpu.VMEM(wo.shape, BF), pltpu.VMEM(wkv.shape, BF),
+            pltpu.VMEM((rows, width), BF), dma((3,)), dma((2,)), dma((2, count)), dma((2,)),
+            dma((2, count)), dma((2,)),
+        ],
+        compiler_params=pltpu.CompilerParams(
+            collective_id=3, has_side_effects=True, vmem_limit_bytes=48 * 1024 * 1024
+        ),
+        cost_estimate=pl.CostEstimate(flops=5_000_000_000, bytes_accessed=100_000_000, transcendentals=0),
+        name="attend",
+    )(tokens, small_all, lengths, cot, wq, wo, wkv)
 
 
 def back_kernel(groups, count, subs, plain, sizes, share, *refs):
     n = len(subs)
     take = iter(refs)
     many = lambda k: [next(take) for _ in range(k)]
-    down_term, up_term, slices, wq, wo, middle_far = many(6)
-    grad_out, attended, queries, keyvals, normed, tokens, bias, gains, wkv, early = many(10)
+    down_term, up_term, slices, wq, wo, middle_far, down_rows = many(7)
+    attended, queries, keyvals, normed, tokens, bias, gains, wkv, early = many(9)
     final, land = many(n), many(n)
     input_grad = next(take)
     own_part = {m: next(take) for m in range(n) if share[m] == m}
@@ -290,7 +423,7 @@
     ring_of = sorted(set(sizes))
     load, outer, mid = many(len(ring_of)), many(len(ring_of)), many(len(ring_of))
     load = [load[ring_of.index(size)] for size in sizes]
-    arrived, middle, grad_mid, branch, grad_q, tiles, stage, stage_kv, grad_kv, sums = many(10)
+    arrived, middle, grad_out, grad_mid, branch, grad_q, tiles, stage, stage_kv, grad_kv, sums = many(11)
     sib, ld, sent, came, zs, z_in, z_mid, os, z_fin, xs, xr, loc, ss, gs, gr, ws, ms, free_in, free_mid = take
     chips = groups // 2
     g, me = lax.axis_index("grp"), lax.axis_index("shard")
@@ -342,18 +475,26 @@
 
     given = (down_term, up_term)
     for m in range(2):
-        for q in near + [0]:
+        for q in [0] + near:
             send(given[m].at[away(q), 1 - c], land[m].at[q], ss.at[m, q], sib.at[m, q], (other, me))
     own_slice = pltpu.make_async_copy(slices.at[me], arrived.at[0], gr.at[0])
     own_slice.start()
-    middle_copy = pltpu.make_async_copy(middle_far, middle, ms)
-    middle_copy.start()
+    span = pl.ds(pl.multiple_of(me * attended.shape[0], 16), attended.shape[0])
+    own_copies = [
+        pltpu.make_async_copy(middle_far, middle, ms.at[0]),
+        pltpu.make_async_copy(down_rows.at[span], grad_out, ms.at[1]),
+    ]
+    for copy in own_copies:
+        copy.start()
 
     def send_slices():
         for q in near:
             send(slices.at[away(q)], arrived.at[q], gs.at[q], gr.at[q], (g, away(q)))
 
-    pair_tasks = [[(m, j, q) for j in range(subs[m]) for q in near + [0]] for m in range(n)]
+    pair_tasks = [
+        [(m, j, q) for j in range(subs[m]) for q in ([0] + near if plain[m] else near + [0])]
+        for m in range(n)
+    ]
     flat = [task for tasks in pair_tasks for task in tasks]
 
     def spot(m, q):
@@ -391,7 +532,7 @@
     units = []
     for m in range(n):
         for j in range(subs[m]):
-            units += [(m, j, q) for q in range(count)] if plain[m] else [(m, j, 0)]
+            units += [(m, j, q) for q in [0] + near] if plain[m] else [(m, j, 0)]
     rings = [ring_of.index(sizes[m]) for m, j, q in units]
     index = [rings[:u].count(rings[u]) for u in range(len(units))]
     total_in = [rings.count(r) for r in range(len(ring_of))]
@@ -486,7 +627,7 @@
         sums[k : k + 1, :] += jnp.sum(x, axis=0, keepdims=True)
 
     def second_norm(lo, hi):
-        gain = gains[1:2, :]
+        gain = gains[4:5, :]
 
         @pl.loop(lo, hi)
         def _(i):
@@ -501,7 +642,9 @@
             back = rate * (
                 e - jnp.mean(e, axis=1, keepdims=True) - unit * jnp.mean(e * unit, axis=1, keepdims=True)
             )
-            whole = back + grad_out[at, :].astype(F32)
+            away_grad = grad_out[at, :].astype(F32)
+            tally(7, away_grad)
+            whole = back + away_grad
             grad_mid[at, :] = whole
             short = whole.astype(BF)
             branch[at, :] = short
@@ -637,13 +780,15 @@
     P_ = partial
     starts = [sum(len(t) for t in pair_tasks[:m]) for m in range(n)]
     pairs_ = lambda m, lo, hi: [P_(pair, starts[m] + k) for k in range(lo, min(hi, len(pair_tasks[m])))]
-    per = len(pair_tasks[1])
-    for s in range(4):
-        at_step(s, *pairs_(1, s * per // 4, (s + 1) * per // 4))
+    first = [*pairs_(0, 0, 99), *pairs_(1, 0, 99)]
+    for s, work in enumerate(first[AHEAD:]):
+        at_step(s // 2, work)
+    at_step(SLICE_STEP, send_slices)
 
     def got_slices():
         clear()
-        middle_copy.wait()
+        for copy in own_copies:
+            copy.wait()
         own_slice.wait()
         for q in near:
             wait(arrived.at[q], gr.at[q])
@@ -668,11 +813,7 @@
     at_step(NORM_STEP + 13, P_(first_norm, bands // 2, bands), keyval_terms)
     at_step(NORM_STEP + 14, *pairs_(4, 0, 99))
 
-    per = len(pair_tasks[0])
-    for work in pairs_(0, 0, per // 2):
-        work()
-    send_slices()
-    for work in pairs_(0, per // 2, per):
+    for work in first[:AHEAD]:
         work()
     steps = max(len(units) + LAG_OUT, max(plan) + 1)
     for step in range(steps):
@@ -726,19 +867,20 @@
     scratch += [pltpu.VMEM((2,) + r, BF) for r in rings]
     scratch += [pltpu.VMEM((k,) + r, BF) for k, r in zip(slots, rings)] * 2
     scratch += [
-        pltpu.VMEM((count, rows, width), BF), pltpu.VMEM((rows, width), F32), pltpu.VMEM((rows, width), F32),
+        pltpu.VMEM((count, rows, width), BF), pltpu.VMEM((rows, width), F32), pltpu.VMEM((rows, width), BF),
+        pltpu.VMEM((rows, width), F32),
         pltpu.VMEM((rows, width), BF), pltpu.VMEM((rows, width), BF), pltpu.VMEM((2, tile, width), BF),
         pltpu.VMEM((2, size, width), BF), pltpu.VMEM((count,) + low, BF), pltpu.VMEM((rows, 2 * HD), F32),
         pltpu.VMEM((16, width), F32),
         dma((n, count)), dma((2, 2)), dma((n,)), dma((n, max(subs), count)), dma((units,)), dma((units,)),
         dma((units,)), dma((units,)), dma((units,)), dma((units,)), dma((units,)), dma((units,)),
-        dma((n, count)), dma((count,)), dma((count,)), dma((2,)), dma,
+        dma((n, count)), dma((count,)), dma((count,)), dma((2,)), dma((2,)),
         regular((len(rings), max(slots))), regular((len(rings), max(slots))),
     ]
     got = pl.pallas_call(
         partial(back_kernel, groups, count, subs, plain, sizes, share),
         out_shape=tuple(out) + (jax.ShapeDtypeStruct((rows, width), BF),),
-        in_specs=[any_] * 6 + [vmem] * 10,
+        in_specs=[any_] * 7 + [vmem] * 9,
         out_specs=(any_,) * (2 * n) + (vmem,),
         scratch_shapes=scratch,
         compiler_params=pltpu.CompilerParams(
@@ -750,26 +892,132 @@
     return got[:n], got[-1]
 
 
-def spread_kernel(block, x_ref, o_ref):
-    _, count, rows, hidden = x_ref.shape
+def widen_kernel(block, size, down, up, out, query, low, o_down, o_up, o_out, o_query, o_low, *lines):
+    o_down[...] = down[...].astype(F32)
+    o_out[...] = out[...].astype(F32)
+    o_query[...] = query[...].astype(F32)
+    _, count, rows, hidden = up.shape
     for source in range(count):
         for k in range(hidden // block):
-            o_ref[:, pl.ds((k * count + source) * block, block)] = x_ref[
-                0, source, :, pl.ds(k * block, block)
-            ].astype(F32)
-
-
-def spread(values, block):
-    _, count, rows, hidden = values.shape
-    step = rows // 4
+            o_up[:, pl.ds((k * count + source) * block, block)] = up[0, source, :, pl.ds(k * block, block)].astype(F32)
+
+    @pl.when(pl.program_id(0) == 0)
+    def _():
+        for half in range(2):
+            o_low[half * size : (half + 1) * size, :] = low[half, :size, :].astype(F32)
+            sums = low[half, size : size + 16, :size].astype(F32)
+            for v in range(8):
+                lines[v][:, half * size : (half + 1) * size] = sums[v : v + 1, :]
+            tail = low[half, size + 16 :, :].astype(F32)
+            wide = tail.shape[1]
+            for r in range(hidden // 2 // wide):
+                start = half * hidden // 2 + r * wide
+                lines[8][:, start : start + wide] = tail[r : r + 1, :]
+
+
+def widen(full, block):
+    down, up, out, query, low = full
+    flat = lambda x: x.reshape(-1, x.shape[-1])
+    down, out, query, low = flat(down), flat(out), flat(query), low[:, 0]
+    _, count, rows, hidden = up.shape
+    steps = 16
+    step = 2 * rows // steps
+    size = out.shape[0] // 2
+    row = lambda x: pl.BlockSpec((x.shape[0] // steps, x.shape[1]), lambda i: (i, 0))
+    still = lambda *shape: pl.BlockSpec(shape, lambda i: (0,) * len(shape))
+    shape = lambda *dims: jax.ShapeDtypeStruct(dims, F32)
+    vectors = [(1, 2 * size)] * 8 + [(1, hidden)]
     return pl.pallas_call(
-        partial(spread_kernel, block),
-        out_shape=jax.ShapeDtypeStruct((2 * rows, count * hidden), F32),
-        grid=(2, rows // step),
-        in_specs=[pl.BlockSpec((1, count, step, hidden), lambda h, i: (h, 0, i, 0))],
-        out_specs=pl.BlockSpec((step, count * hidden), lambda h, i: (h * (rows // step) + i, 0)),
-        name="spread",
-    )(values)
+        partial(widen_kernel, block, size),
+        out_shape=(
+            shape(*down.shape), shape(2 * rows, count * hidden), shape(*out.shape), shape(*query.shape),
+            shape(2 * size, low.shape[2]),
+        ) + tuple(shape(*v) for v in vectors),
+        grid=(steps,),
+        in_specs=[
+            row(down), pl.BlockSpec((1, count, step, hidden), lambda i: (i // (steps // 2), 0, i % (steps // 2), 0)),
+            row(out), row(query), still(*low.shape),
+        ],
+        out_specs=(
+            row(down), pl.BlockSpec((step, count * hidden), lambda i: (i, 0)), row(out), row(query),
+            still(2 * size, low.shape[2]),
+        ) + tuple(still(*v) for v in vectors),
+        name="widen",
+    )(down, up, out, query, low)
+
+
+def used(lengths, row):
+    total = lengths[row, 0]
+    for k in range(1, lengths.shape[1]):
+        total = total + lengths[row, k]
+    return total
+
+
+def masked(x, lengths, row):
+    places = lax.broadcasted_iota(jnp.int32, x.shape, 0)
+    return jnp.where(places < used(lengths, row), x, 0.0)
+
+
+def take_kernel(order, lengths, x, out):
+    out[0] = masked(x[0].astype(F32), lengths, pl.program_id(0)).astype(BF)
+
+
+def take_rows(values, order, lengths):
+    _, length, width = values.shape
+    spec = lambda f: pl.BlockSpec((1, length, width), f)
+    return pl.pallas_call(
+        take_kernel,
+        out_shape=jax.ShapeDtypeStruct(values.shape, BF),
+        grid_spec=pltpu.PrefetchScalarGridSpec(
+            num_scalar_prefetch=2,
+            grid=(values.shape[0],),
+            in_specs=[spec(lambda r, order, lengths: (order[r], 0, 0))],
+            out_specs=spec(lambda r, order, lengths: (r, 0, 0)),
+        ),
+        name="take_rows",
+    )(order, lengths, values)
+
+
+def finish_kernel(deal, lengths, place, x, middle, table, out):
+    row = deal[pl.program_id(0)]
+    micro = middle.shape[0]
+    term = x[0].astype(F32)
+    own = lax.div(row, micro) == place[0]
+
+    @pl.when(own)
+    def _():
+        whole = term + middle[lax.rem(row, micro)] + table[6:7, :]
+        out[0] = masked(whole, lengths, row).astype(BF)
+
+    @pl.when(jnp.logical_not(own))
+    def _():
+        out[0] = masked(term, lengths, row).astype(BF)
+
+
+def finish_rows(values, deal, lengths, me, middle, table):
+    _, length, width = values.shape
+    spec = lambda f: pl.BlockSpec((1, length, width), f)
+    return pl.pallas_call(
+        finish_kernel,
+        out_shape=jax.ShapeDtypeStruct(values.shape, BF),
+        grid_spec=pltpu.PrefetchScalarGridSpec(
+            num_scalar_prefetch=3,
+            grid=(values.shape[0],),
+            in_specs=[
+                spec(lambda j, deal, lengths, me: (deal[j], 0, 0)),
+                pl.BlockSpec(middle.shape, lambda j, deal, lengths, me: (0, 0, 0)),
+                pl.BlockSpec(table.shape, lambda j, deal, lengths, me: (0, 0)),
+            ],
+            out_specs=spec(lambda j, deal, lengths, me: (j, 0, 0)),
+        ),
+        name="finish_rows",
+    )(deal, lengths, me.reshape(1), values, middle, table)
+
+
+def cut_kernel(groups, count, block, x, out):
+    for to in range(count):
+        for k in range(groups):
+            out[to, :, k * block : (k + 1) * block] = x[:, (k * count + to) * block : (k * count + to + 1) * block]
 
 
 def shards(
@@ -804,148 +1052,83 @@
     hidden = block * groups
     rows = micro * length
 
-    local_deal = dealing - group * group_rows
+    deal = dealing - group * group_rows
     steps = jnp.arange(group_rows, dtype=jnp.int32)
-    inverse = jnp.sum(jnp.where(local_deal[:, None] == steps[None, :], steps[:, None], 0), axis=0)
-    pick = lambda table, at: lax.dynamic_index_in_dim(table, at, 0, keepdims=False)
-
-    small = (
-        first_gain, first_shift, query_bias, value_bias, out_bias,
-        second_gain, second_shift, up_bias, down_bias,
+    inverse = jnp.sum(jnp.where(deal[:, None] == steps[None, :], steps[:, None], 0), axis=0)
+
+    line = lambda x: jnp.pad(x, (0, 128 - x.shape[0]))
+    piece = first_gain.shape[0]
+    device = group * count + me
+    value_line = lax.dynamic_update_slice(
+        jnp.zeros((128,), BF), value_bias, (device * value_bias.shape[0],)
     )
+    small = [first_gain, first_shift, query_bias, out_bias, second_gain, second_shift, down_bias]
+    small = [line(x) for x in small] + [value_line]
+    small += [line(up_bias[k * piece : (k + 1) * piece]) for k in range(block // piece)]
+    small = jnp.stack(small + [jnp.zeros((128,), BF)] * (16 - len(small)))
     up_rows = up_weight.shape[0]
-    beside = jnp.concatenate(small)
-    beside = jnp.pad(beside, (0, up_rows * 128 - beside.shape[0])).reshape(up_rows, 128)
-    keyval_wide = jnp.concatenate([keyval_weight, beside], axis=1)
-    up_cut = up_weight.reshape(up_rows, groups, count, block).transpose(2, 0, 1, 3)
-    up_cut = up_cut.reshape(count, up_rows, hidden)
-    weight_query, weight_out, keyval_all, weight_up = gather_all(
-        groups, count, query_weight, out_weight, keyval_wide, up_cut
+    up_cut = pl.pallas_call(
+        partial(cut_kernel, groups, count, block),
+        out_shape=jax.ShapeDtypeStruct((count, up_rows, hidden), BF),
+        name="cut",
+    )(up_weight)
+    weight_query, weight_out, weight_keyval, small_all, weight_up = gather_all(
+        groups, count, query_weight, out_weight, keyval_weight, small, up_cut
     )
-    weight_query, weight_out, keyval_all, weight_up, down_weight, cotangent = lax.optimization_barrier(
-        (weight_query, weight_out, keyval_all, weight_up, down_weight, cotangent)
+    weight_query, weight_out, weight_up, down_weight = lax.optimization_barrier(
+        (weight_query, weight_out, weight_up, down_weight)
     )
     weight_down = lax.all_gather(down_weight, "grp", axis=0, tiled=True)
-    weight_keyval = keyval_all[:, : 2 * HD]
-    packed = keyval_all[:, 2 * HD :].reshape(groups * count, up_rows * 128)
-    wide = []
-    at = 0
-    for item in small:
-        wide.append(packed[:, at : at + item.shape[0]].astype(F32))
-        at += item.shape[0]
-    up_part = pick(wide[7].reshape(groups, count, block).swapaxes(0, 1), me).reshape(hidden)
-    gain_one, shift_one, bias_query, bias_value, bias_out, gain_two, shift_two, _, bias_down = [
-        item.reshape(-1) for item in wide
-    ]
-
-    def gather_rows(values, place_of):
-        held = cube_gather((values[:half], values[half:]), count, "shard")
-        out = jnp.zeros((group_rows, length, width), values.dtype)
-        for q in range(count):
-            for k in range(2):
-                for i in range(half):
-                    row = (me ^ q) * micro + k * half + i
-                    out = lax.dynamic_update_slice(out, held[k][q][i][None], (place_of(row), 0, 0))
-        return out.reshape(group_rows * length, width)
-
-    dealt_place = lambda row: pick(inverse, row)
-    same_place = lambda row: row
-
-    cot_rows = gather_rows(cotangent, same_place).reshape(group_rows, length, width)
-    dealt_live = jnp.stack([live(pick(lengths, local_deal[j]), length) for j in range(group_rows)])
-    grad_down = (cot_rows.astype(F32) * dealt_live[:, :, None]).astype(BF)
-    own_live = jnp.stack([pick(dealt_live, me * micro + m) for m in range(micro)])
-
-    scale = HD**-0.5
-    own_lengths = [pick(lengths, me * micro + m) for m in range(micro)]
-    inputs = tokens.astype(F32).reshape(rows, width)
-    unit_one, rate_one = normalize(inputs)
-    normed_one = (unit_one * gain_one + shift_one).astype(BF)
-    queries = (mm(normed_one, weight_query) + bias_query).astype(BF)
-    value_pad = jnp.concatenate([jnp.zeros((HD,), F32), bias_value])
-    keyvals = (mm(normed_one, weight_keyval) + value_pad).astype(BF)
-    attended = []
-    for m in range(micro):
-        mask = jnp.repeat(allowed_pairs(own_lengths[m], length), HEADS, axis=0)
-        query_rows = queries[m * length : (m + 1) * length].reshape(length * HEADS, HD)
-        key_rows = keyvals[m * length : (m + 1) * length, :HD]
-        value_rows = keyvals[m * length : (m + 1) * length, HD:]
-        scores = jnp.where(mask, mm_nt(query_rows, key_rows) * scale, NEGATIVE)
-        top = jnp.max(scores, axis=1, keepdims=True)
-        powers = jnp.exp(scores - top)
-        totals = jnp.sum(powers, axis=1, keepdims=True)
-        probs = powers / totals
-        probs_low = probs.astype(BF)
-        attended.append(mm(probs_low, value_rows).reshape(length, width).astype(BF))
-    attended = jnp.concatenate(attended)
-    middle = inputs + mm(attended, weight_out) + bias_out
-    unit_two, rate_two = normalize(middle)
-    normed_two_own = (unit_two * gain_two + shift_two).astype(BF)
-
-    normed_two = gather_rows(normed_two_own.reshape(micro, length, width), dealt_place)
+
+    flat_tokens = tokens.reshape(rows, width)
+    (
+        normed_two, cot_rows, normed_one, queries, keyvals, attended, middle, table, up_part, bias,
+    ) = attend(
+        groups, count, flat_tokens, small_all, lengths, cotangent.reshape(rows, width),
+        weight_query, weight_out, weight_keyval, hidden, length,
+    )
+    grad_down = take_rows(cot_rows.reshape(group_rows, length, width), inverse, lengths)
+    grad_down = grad_down.reshape(group_rows * length, width)
+
     hidden_pre = mm(normed_two, weight_up) + up_part
     gelu_tanh = partial(jax.nn.gelu, approximate=True)
     activated_wide, gelu_pull = jax.vjp(gelu_tanh, hidden_pre)
     activated = activated_wide.astype(BF)
-    grad_down = grad_down.reshape(group_rows * length, width)
     grad_hidden = gelu_pull(mm_nt(grad_down, weight_down))[0].astype(BF)
-    grad_two = mm_nt(grad_hidden, weight_up).astype(BF).reshape(group_rows, length, width)
-    slices = jnp.stack([pick(grad_two, inverse[r]) for r in range(group_rows)]).reshape(count, rows, width)
+    slices = mm_nt(grad_hidden, weight_up).astype(BF).reshape(count, rows, width)
     down_grad = mm_tn(activated, grad_down).astype(BF)
     up_grad = mm_tn(normed_two, grad_hidden).astype(BF)
 
     result = mm(activated, weight_down).astype(BF).reshape(group_rows, length, width)
-    middle_rows = middle.reshape(micro, length, width)
-    for m in range(micro):
-        at = dealt_place(me * micro + m)
-        row = (pick(result, at).astype(F32) + middle_rows[m]).astype(BF)
-        result = lax.dynamic_update_slice(result, row[None], (at, 0, 0))
-    result = lax.psum_scatter(
+    result = finish_rows(result, deal, lengths, me, middle.reshape(micro, length, width), table)
+    block_output = lax.psum_scatter(
         result.reshape(group_rows * length, width), "shard", scatter_dimension=0, tiled=True
-    )
-    result = result.reshape(micro, length, width).astype(F32)
-    block_output = ((result + bias_down) * own_live[:, :, None]).astype(BF)
-
-    own_cot = jnp.stack([pick(cot_rows, dealt_place(me * micro + m)) for m in range(micro)])
-    given_live = jnp.stack([live(own_lengths[m], length) for m in range(micro)])
-    grad_out = (own_cot.astype(F32) * given_live[:, :, None]).reshape(rows, width).astype(BF)
+    ).reshape(micro, length, width)
+
     per = groups // count
     up_bias_part = jnp.sum(grad_hidden.astype(F32), axis=0).reshape(count, per, 1, block)
     spot = (jnp.arange(count, dtype=jnp.int32) == me)[None, None, :, None]
     up_bias_part = jnp.where(spot, up_bias_part, 0.0).reshape(count, 2, -1)
-    down_bias_part = jnp.sum(grad_out.astype(F32), axis=0).reshape(count, 2, -1)
-    early = jnp.concatenate([up_bias_part, down_bias_part], axis=2).astype(BF)
+    early = up_bias_part.astype(BF)
     fill = -early.shape[2] % (16 * 2 * HD)
     early = jnp.pad(early, ((0, 0), (0, 0), (0, fill))).reshape(count, 2, -1, 2 * HD)
 
-    bias = jnp.concatenate(
-        [jnp.where(allowed_pairs(own_lengths[m], length), 0.0, NEGATIVE) for m in range(micro)]
-    )
-    gains = jnp.pad(jnp.stack([gain_one, gain_two]), ((0, 6), (0, 0)))
     cut = lambda x: x.reshape(count, 2, x.shape[0] // count // 2, x.shape[1])
     near_by = (
-        grad_out, attended, queries, keyvals, normed_one, tokens.reshape(rows, width), bias, gains, weight_keyval,
+        attended, queries, keyvals, normed_one, flat_tokens, bias, table, weight_keyval,
     )
     full, input_grad = back_all(
         groups, count, (cut(down_grad), cut(up_grad)),
-        (slices, weight_query, weight_out, middle), near_by, early,
+        (slices, weight_query, weight_out, middle, grad_down), near_by, early,
     )
     input_grad = input_grad.reshape(micro, length, width)
 
-    down_full = full[0].reshape(-1, width).astype(F32)
-    up_full = spread(full[1], block)
-    out_full = full[2].reshape(-1, width).astype(F32)
-    query_full = full[3].reshape(-1, width).astype(F32)
-    size = width // count // 2
-    last = full[4][:, 0]
-    keyval_full = last[:, :size].reshape(2 * size, 2 * HD).astype(F32)
-    sums = last[:, size : size + 16, :size].swapaxes(0, 1).reshape(16, 2 * size).astype(F32)
-    gain_two_grad, shift_two_grad, out_bias_grad, gain_one_grad, shift_one_grad, query_bias_grad = sums[:6]
+    down_full, up_full, out_full, query_full, keyval_full, *lines = widen(full, block)
+    lines = [line.reshape(-1) for line in lines]
+    gain_two_grad, shift_two_grad, out_bias_grad, gain_one_grad, shift_one_grad, query_bias_grad = lines[:6]
     short = value_bias.shape[0] * groups
-    value_bias_grad = lax.dynamic_slice(sums[6, :HD], (me * short,), (short,))
-    tail = last[:, size + 16 :].reshape(2, -1).astype(F32)
-    up_bias_grad = tail[:, : hidden // 2].reshape(-1)
-    down_bias_grad = tail[:, hidden // 2 : hidden // 2 + size].reshape(-1)
+    value_bias_grad = lax.dynamic_slice(lines[6], (me * short,), (short,))
+    down_bias_grad, up_bias_grad = lines[7:]
 
     return (
         block_output, input_grad, gain_one_grad, shift_one_grad, query_full, query_bias_grad, keyval_full,

time: 783 us -> 694 us (0.89)
  Pallas kernels: 456 us -> 558 us
  local copies, waits for them, and re-layouts: 69 us -> 17.6 us
  between operations: 61.6 us -> 14.6 us
  other arithmetic: 48.5 us -> 1.96 us
  waiting for transfers between devices: 27.9 us -> 0.04 us
  matrix products: 105 us -> 93.3 us
  starting transfers between devices: 8.45 us -> 0.6 us
    pallas_call x1 -> x5, Pallas kernels: 10.9 us -> 117 us  [the longest x1 75.8 us: attend(): pl.pallas_call(partial(attend_kernel, groups, count), out_shape=(shape((c...]
    ppermute x8 -> x0, waiting for transfers between devices: 27.8 us -> none  [cube_gather(): got = lax.ppermute(pack, axis, flips(count, mask))]
    convert_element_type x9 -> x1, other arithmetic: 25.4 us -> 0.02 us  [shards(): early = up_bias_part.astype(BF)]
    dynamic_update_slice x15 -> x1, local copies, waits for them, and re-layouts: 20.8 us -> 0.77 us  [shards(): lax.dynamic_update_slice(jnp.zeros((128,), BF), value_bias, (device * val...]
    dot_general x7 -> x2, matrix products: 43.2 us -> 30.5 us  [mm(): return jnp.dot(left, right, preferred_element_type=F32)]
    ppermute x8 -> x0, starting transfers between devices: 8.16 us -> none  [cube_gather(): got = lax.ppermute(pack, axis, flips(count, mask))]
    dot_general x4 -> x2, matrix products: 33.8 us -> 34.7 us  [mm_nt(): lax.dot_general(left, right, (((1,), (1,)), ((), ())), preferred_element_...]
  transfers between devices with their start and end apart: 10 -> 2, of which waited for: 2 -> 0; matrix products, arithmetic and copies ran while one was open for 20% -> 12% of each run, Pallas kernels for 42% -> 61%
where the time goes in v4:
time: 694 us; the launch traced here: 686 us
  Pallas kernels  558 us (80%)
  matrix products  93.3 us (13%)
  local copies, waits for them, and re-layouts  17.6 us (3%)
  between operations  14.6 us (2%)
    pallas_call x1, Pallas kernels, back_all(): pl.pallas_call(partial(back_kernel, groups, count, subs, plain, sizes, sh...  313 us
    pallas_call x1, Pallas kernels, gather_all(): pl.pallas_call(partial(gather_kernel, groups, count), out_shape=(tall(wq)...  128 us
    pallas_call x1, Pallas kernels, attend(): pl.pallas_call(partial(attend_kernel, groups, count), out_shape=(shape((c...  75.8 us
    dot_general x2, matrix products, mm_nt(): lax.dot_general(left, right, (((1,), (1,)), ((), ())), preferred_element_...  34.7 us
    dot_general x2, matrix products, mm(): return jnp.dot(left, right, preferred_element_type=F32)  30.5 us
    dot_general x2, matrix products, mm_tn(): lax.dot_general(left, right, (((0,), (0,)), ((), ())), preferred_element_...  28.1 us
    pallas_call x1, Pallas kernels, widen(): pl.pallas_call(partial(widen_kernel, block, size), out_shape=(shape(*down...  22.9 us
  transfers between devices with their start and end apart: 2, of which 0 were waited for; matrix products, arithmetic and copies ran while one was open for 12% of the time, Pallas kernels for 61%

profile of v4, /device:TPU:0, one launch (start us, length us, event | category | flops | bytes accessed | tf_op | source)
XLA Modules:
  0.0 686.5 jit_solution(16927851379574169092)
XLA Ops:
  7.2 0.0 all-gather.2.cloned.1.call-start
  7.2 0.7 pad_bitcast_fusion.9
  7.9 0.8 fusion.8
  8.7 2.3 cut.1.upc
  11.0 0.7 pad_bitcast_fusion.7
  11.7 0.7 pad_bitcast_fusion.5
  12.4 0.7 pad_bitcast_fusion.3
  13.1 0.7 pad_bitcast_fusion.2
  13.8 0.8 dynamic_update_slice.4
  14.5 1.2 stack.55.small
  15.7 128.1 %gather_all.1 = (bf16[2048,2048]{1,0:T(8,128)(2,1)}, bf16[2048,2048]{1,0:T(8,128)(2,1)}, bf16[2048,256]{1,0:T(8,128)(2,1)}, bf16[512,128]{1,0:T(8,128)(2,1)}, bf16[2048,2048]{1,0:T(8,128)(2,1)}) custom-call(bf16[64,2048]{1,0:T(8,128)(2,1)} %wq.1, bf16[64,2048]{1,0:T(8,128)(2,1)} %wo.1, bf16[64,256]{1,0:T(8,128)(2,1)} %wkv.1, bf16[16,128]{1,0:T(8,128)(2,1)} %stack.55.small, ...), custom_call_target="tpu_custom_call" | custom-call | bytes 100000000 | tf_op jit(solution)/shard_map/gather_all/pallas_call | solution.py:216
  143.9 0.0 all-gather.2.cloned.1.call-update
  143.9 0.6 reduce-scatter.2.cloned.1.call-start
  144.5 0.1 broadcast_in_dim.50
  144.6 0.8 copy.38.lengths
  145.3 0.0 copy-start.9
  145.3 0.7 broadcast_subtract_fusion.deal
  146.0 0.0 copy-start.12
  146.0 0.6 select_reduce_fusion.order
  146.6 0.0 copy-start
  146.6 1.2 copy-done
  147.8 0.0 copy-start.1
  147.8 1.2 copy-done.1
  149.0 0.0 copy-start.8
  149.0 0.9 copy-done.8
  150.0 75.8 %attend.1 = (bf16[1024,2048]{1,0:T(8,128)(2,1)}, bf16[1024,2048]{1,0:T(8,128)(2,1)}, bf16[256,2048]{1,0:T(8,128)(2,1)S(1)}, bf16[256,2048]{1,0:T(8,128)(2,1)S(1)...) custom-call(bf16[256,2048]{1,0:T(8,128)(2,1)S(1)} %bitcast.62, ...), custom_call_target="tpu_custom_call" | custom-call | flops 5000000000 | bytes 100000000 | tf_op jit(solution)/shard_map/attend/pallas_call | solution.py:389
  225.8 0.0 copy-done.9
  225.8 0.0 copy-done.12
  225.8 0.0 copy-start.2
  225.8 1.0 copy-done.2
  226.8 0.0 copy-start.3
  226.8 1.0 copy-done.3
  227.7 0.0 copy-start.4
  227.7 1.0 copy-done.4
  228.7 0.0 copy-start.5
  228.7 0.7 copy-done.5
  229.4 0.0 copy-start.6
  229.4 0.6 copy-done.6
  230.0 0.0 copy-start.7
  230.0 0.6 copy-done.7
  230.7 7.5 %take_rows.1 = bf16[8,128,2048]{2,1,0:T(8,128)(2,1)} custom-call(s32[8]{0:T(128)} %select_reduce_fusion.order, s32[8,4]{1,0:T(8,128)} %copy-done.9, bf16[8,128,2048]{2,1,0:T(8,128)(2,1)} %bitcast.77), custom_call_target="tpu_custom_call" | custom-call | tf_op jit(solution)/shard_map/take_rows/pallas_call | solution.py:968
  238.2 14.5 %fusion.9 = f32[1024,2048]{1,0:T(8,128)} fusion(bf16[1024,2048]{1,0:T(8,128)(2,1)} %get-tuple-element.62, bf16[2048,2048]{1,0:T(8,128)(2,1)} %get-tuple-element.63), kind=kOutput, calls=%fused_computation.33 | convolution fusion | flops 8589934592 | bytes 20971520 | tf_op jit(solution)/shard_map/dot_general | solution.py:26
  252.7 0.0 all-gather.2.cloned.1.call-done
  252.7 16.0 %convolution_convert_fusion.3 = bf16[1024,2048]{1,0:T(8,128)(2,1)} fusion(bf16[2048,2048]{1,0:T(8,128)(2,1)} %all-gather.2.cloned.1.call-done, f32[1024,2048]{1,0:T(8,128)} %fusion.9, f32[2048]{0:T(1024)S(1)} %bitcast.64), kind=kOutput, calls=%fused_computation.14 | convolution fusion | flops 8613003264 | bytes 20979712 | tf_op jit(solution)/shard_map/dot_general | solution.py:26
  268.7 8.5 %finish_rows.1 = bf16[8,128,2048]{2,1,0:T(8,128)(2,1)} custom-call(s32[8]{0:T(128)} %copy-done.12, s32[8,4]{1,0:T(8,128)} %copy-done.9, s32[1]{0:T(128)} %bitcast.place, bf16[8,128,2048]{2,1,0:T(8,128)(2,1)} %bitcast.76, f32[2,128,2048]{2,1,0:T(8,128)} %bitcast.71, f32[16,2048]{1,0:T(8,128)} %copy-done.5), custom_call_target="tpu_custom_call" | custom-call | tf_op jit(solution)/shard_map/finish_rows/pallas_call | solution.py:1000
  277.2 0.0 reduce-scatter.2.cloned.1.call-update
  277.2 0.0 copy-start.10
  277.2 17.0 %convolution_convert_fusion.1 = bf16[2048,2048]{1,0:T(8,128)(2,1)} fusion(bf16[1024,2048]{1,0:T(8,128)(2,1)} %bitcast.68, f32[1024,2048]{1,0:T(8,128)} %fusion.9, f32[2048]{0:T(1024)S(1)} %bitcast.65), kind=kOutput, calls=%fused_computation.12 | convolution fusion | flops 8615100416 | bytes 20979712 | tf_op jit(solution)/shard_map/dot_general | solution.py:30
  294.2 0.0 copy-done.10
  294.2 20.4 %convert_reduce_fusion = (bf16[2048]{0:T(1024)(128)(2,1)S(1)}, bf16[1024,2048]{1,0:T(8,128)(2,1)}) fusion(f32[1024,2048]{1,0:T(8,128)} %fusion.9, f32[2048]{0:T(1024)S(1)} %bitcast.66, bf16[1024,2048]{1,0:T(8,128)(2,1)S(1)} %bitcast.70, bf16[2048,2048]{1,0:T(8,128)(2,1)} %all-gather.2.cloned.1.call-done), kind=kOutput, calls=%fused_computation.9 | convolution fusion | flops 8638167040 | bytes 25178112 | tf_op jit(solution)/shard_map/dot_general | solution.py:34
  314.7 0.7 reshape.133.refs_15_
  315.4 0.0 copy-start.13
  315.4 0.0 copy-start.14
  315.4 14.3 %convolution_convert_fusion.2 = bf16[1024,2048]{1,0:T(8,128)(2,1)} fusion(bf16[1024,2048]{1,0:T(8,128)(2,1)} %get-tuple-element.95, bf16[2048,2048]{1,0:T(8,128)(2,1)} %get-tuple-element.63), kind=kOutput, calls=%fused_computation.13 | convolution fusion | flops 8592031744 | bytes 16777216 | tf_op jit(solution)/shard_map/dot_general | solution.py:34
  329.6 0.0 copy-done.13
  329.6 0.0 copy-done.14
  329.6 11.2 %convolution_convert_fusion = bf16[2048,2048]{1,0:T(8,128)(2,1)} fusion(bf16[1024,2048]{1,0:T(8,128)(2,1)S(1)} %copy-done.13, bf16[1024,2048]{1,0:T(8,128)(2,1)S(1)} %copy-done.14), kind=kOutput, calls=%fused_computation.11 | convolution fusion | flops 8594128896 | bytes 16777216 | tf_op jit(solution)/shard_map/dot_general | solution.py:30
  340.8 313.2 %back_all.1 = (bf16[2,4,256,2048]{3,2,1,0:T(8,128)(2,1)}, bf16[2,4,256,2048]{3,2,1,0:T(8,128)(2,1)}, bf16[2,1,256,2048]{3,2,1,0:T(8,128)(2,1)}, bf16[2,1,256,204...) custom-call(bf16[4,2,256,2048]{3,2,1,0:T(8,128)(2,1)} %bitcast.73, ...), custom_call_target="tpu_custom_call" | custom-call | bytes 200000000 | tf_op jit(solution)/shard_map/back_all/pallas_call | solution.py:880
  654.0 0.0 copy-start.11
  654.0 22.9 %widen.1 = (f32[2048,2048]{1,0:T(8,128)}, f32[512,8192]{1,0:T(8,128)}, f32[512,2048]{1,0:T(8,128)}, f32[512,2048]{1,0:T(8,128)}, f32[512,256]{1,0:T(8,128)}, /*i...) custom-call(bf16[2048,2048]{1,0:T(8,128)(2,1)} %bitcast.72, ...), custom_call_target="tpu_custom_call" | custom-call | tf_op jit(solution)/shard_map/widen/pallas_call | solution.py:930
  677.0 1.2 dynamic-slice_bitcast_fusion
  678.2 0.0 reduce-scatter.2.cloned.1.call-done
  678.2 0.0 copy-done.11
  678.2 1.0 copy.42
  (10 shorter events, 0.1 us)
Async XLA Ops:
  7.2 245.5 %all-gather.2.cloned.1.call-start = ((), (), s32[]{:S(2)}) async-start(), calls=%async_computation.1 | async-start | bytes 9437184 | tf_op jit(solution)/shard_map/all_gather | solution.py:1081
  143.9 534.3 %reduce-scatter.2.cloned.1.call-start = ((), (), s32[]{:S(2)}) async-start(), calls=%async_computation.2 | async-start | bytes 5242880 | tf_op jit(solution)/shard_map/reduce_scatter | solution.py:1104
  145.3 80.4 %copy-start.9 = (s32[8,4]{1,0:T(8,128)}, s32[8,4]{1,0:T(8,128)S(1)}, u32[]{:S(2)}) copy-start(s32[8,4]{1,0:T(8,128)S(1)} %copy.38.lengths) | copy-start | bytes 388
  146.0 79.8 %copy-start.12 = (s32[8]{0:T(128)}, s32[8]{0:T(128)S(1)}, u32[]{:S(2)}) copy-start(s32[8]{0:T(128)S(1)} %broadcast_subtract_fusion.deal) | copy-start | bytes 100
  146.6 1.2 copy-start
  147.8 1.2 copy-start.1
  149.0 0.9 copy-start.8
  225.8 1.0 copy-start.2
  226.8 1.0 copy-start.3
  227.7 1.0 copy-start.4
  228.7 0.7 copy-start.5
  229.4 0.7 copy-start.6
  230.0 0.6 copy-start.7
  277.2 17.0 %copy-start.10 = (bf16[8,128,2048]{2,1,0:T(8,128)(2,1)S(1)}, bf16[8,128,2048]{2,1,0:T(8,128)(2,1)}, u32[]{:S(2)}) copy-start(bf16[8,128,2048]{2,1,0:T(8,128)(2,1)} %take_rows.1) | copy-start | bytes 12582916
  315.4 14.3 %copy-start.13 = (bf16[1024,2048]{1,0:T(8,128)(2,1)S(1)}, bf16[1024,2048]{1,0:T(8,128)(2,1)}, u32[]{:S(2)}) copy-start(bf16[1024,2048]{1,0:T(8,128)(2,1)} %get-tuple-element.62) | copy-start | bytes 12582916
  315.4 14.3 %copy-start.14 = (bf16[1024,2048]{1,0:T(8,128)(2,1)S(1)}, bf16[1024,2048]{1,0:T(8,128)(2,1)}, u32[]{:S(2)}) copy-start(bf16[1024,2048]{1,0:T(8,128)(2,1)} %get-tuple-element.95) | copy-start | bytes 12582916
  654.0 24.2 %copy-start.11 = (bf16[256,2048]{1,0:T(8,128)(2,1)S(1)}, bf16[256,2048]{1,0:T(8,128)(2,1)}, u32[]{:S(2)}) copy-start(bf16[256,2048]{1,0:T(8,128)(2,1)} %get-tuple-element.74) | copy-start | bytes 3145732
Sparse Core Ops, SparseCore 0:
  144.0 81.3 all-gather.1
  277.3 51.9 reduce-scatter.1

commit v5 on v4

--- a/solution.py
+++ b/solution.py
@@ -15,27 +15,15 @@
 F32 = jnp.float32
 MESH = pl.DeviceIdType.MESH
 LAG_MID = 2
-LAG_OUT = 4
-NORM_STEP = 5
-AHEAD = 4
-SLICE_STEP = 1
+LAG_OUT = 6
+BUDGET = 8.0
+TILE_COST = 4.0
+NORM_STEP = 15
 RING = 6
 
 
 def mm(left, right):
     return jnp.dot(left, right, preferred_element_type=F32)
-
-
-def mm_tn(left, right):
-    return lax.dot_general(left, right, (((0,), (0,)), ((), ())), preferred_element_type=F32)
-
-
-def mm_nt(left, right):
-    return lax.dot_general(left, right, (((1,), (1,)), ((), ())), preferred_element_type=F32)
-
-
-def near_first(count):
-    return sorted(range(1, count), key=lambda q: (bin(q).count("1"), q))
 
 
 def cube_tree(count, parity, q):
@@ -413,9 +401,11 @@
     n = len(subs)
     take = iter(refs)
     many = lambda k: [next(take) for _ in range(k)]
-    down_term, up_term, slices, wq, wo, middle_far, down_rows = many(7)
-    attended, queries, keyvals, normed, tokens, bias, gains, wkv, early = many(9)
+    act, slope, down_rows, wdn, normed_two, wup, wq, wo, middle_far = many(9)
+    far_rows = many(4)
+    keyvals, bias, gains, wkv = many(4)
     final, land = many(n), many(n)
+    slices = next(take)
     input_grad = next(take)
     own_part = {m: next(take) for m in range(n) if share[m] == m}
     part = [own_part[share[m]] for m in range(n)]
@@ -423,8 +413,9 @@
     ring_of = sorted(set(sizes))
     load, outer, mid = many(len(ring_of)), many(len(ring_of)), many(len(ring_of))
     load = [load[ring_of.index(size)] for size in sizes]
-    arrived, middle, grad_out, grad_mid, branch, grad_q, tiles, stage, stage_kv, grad_kv, sums = many(11)
-    sib, ld, sent, came, zs, z_in, z_mid, os, z_fin, xs, xr, loc, ss, gs, gr, ws, ms, free_in, free_mid = take
+    down_all, grad_hidden, strips, slices_stage, middle, grad_out, grad_mid, branch, grad_q, tiles, stage, stage_kv, grad_kv, sums, up_sums = many(15)
+    attended, queries, normed, tokens = many(4)
+    sib, ld, sent, came, zs, z_in, z_mid, os, z_fin, xs, xr, loc, ss, gs, gr, ws, ms, ts, ps, free_in, free_mid, ready = take
     chips = groups // 2
     g, me = lax.axis_index("grp"), lax.axis_index("shard")
     p, c = lax.div(g, 2), lax.rem(g, 2)
@@ -473,54 +464,62 @@
     cut = lambda m, j: pl.ds(j * sizes[m][0], sizes[m][0])
     away = lambda q: lax.bitwise_xor(me, q)
 
-    given = (down_term, up_term)
-    for m in range(2):
-        for q in [0] + near:
-            send(given[m].at[away(q), 1 - c], land[m].at[q], ss.at[m, q], sib.at[m, q], (other, me))
-    own_slice = pltpu.make_async_copy(slices.at[me], arrived.at[0], gr.at[0])
-    own_slice.start()
+    rows, width = attended.shape
+    hidden = grad_hidden.shape[1]
+    everyone = down_all.shape[0]
+    arrived = lambda q: down_all.at[pl.ds(q * rows, rows)]
+    whole_down = pltpu.make_async_copy(down_rows, down_all, ms.at[6])
+    whole_down.start()
     span = pl.ds(pl.multiple_of(me * attended.shape[0], 16), attended.shape[0])
     own_copies = [
         pltpu.make_async_copy(middle_far, middle, ms.at[0]),
         pltpu.make_async_copy(down_rows.at[span], grad_out, ms.at[1]),
     ]
+    for i, (a, b) in enumerate(zip(far_rows, (attended, queries, normed, tokens))):
+        own_copies.append(pltpu.make_async_copy(a, b, ms.at[2 + i]))
     for copy in own_copies:
         copy.start()
 
     def send_slices():
+        pl.semaphore_wait(ready, count - 1)
+        part_of = lambda col: slices.at[pl.ds(pl.multiple_of(col * rows, 16), rows)]
         for q in near:
-            send(slices.at[away(q)], arrived.at[q], gs.at[q], gr.at[q], (g, away(q)))
+            send(part_of(away(q)), arrived(q), gs.at[q], gr.at[q], (g, away(q)))
+        pltpu.make_async_copy(part_of(me), arrived(0), gr.at[0]).start()
+
 
     pair_tasks = [
-        [(m, j, q) for j in range(subs[m]) for q in ([0] + near if plain[m] else near + [0])]
+        [(m, j, q) for q in [0] + near for j in range(subs[m])]
+        if plain[m]
+        else [(m, j, q) for j in range(subs[m]) for q in near + [0]]
         for m in range(n)
     ]
     flat = [task for tasks in pair_tasks for task in tasks]
 
+    begun, paired_set = set(), set()
+
     def spot(m, q):
         return part[m].at[q - 1] if q else held[m].at[me]
 
     def loads(k):
         m, j, q = flat[k]
         slot = k % 2
-        copies = [pltpu.make_async_copy(land[m].at[q, cut(m, j)], load[m].at[slot], ld.at[slot, 1])]
-        if m < 2:
-            place = spot(m, q).at[cut(m, j)]
-            copies.append(pltpu.make_async_copy(given[m].at[away(q), c, cut(m, j)], place, ld.at[slot, 0]))
-        return copies
+        return [pltpu.make_async_copy(land[m].at[q, cut(m, j)], load[m].at[slot], ld.at[slot])]
 
     def begin(k):
         m, j, q = flat[k]
         if j == 0:
             wait(land[m].at[q], sib.at[m, q])
+        begun.add(k)
         for copy in loads(k):
             copy.start()
 
     def pair(k):
         m, j, q = flat[k]
-        if k == 0 or flat[k - 1][0] != m:
+        paired_set.add(k)
+        if k not in begun:
             begin(k)
-        if k + 1 < len(flat) and flat[k + 1][0] == m:
+        if k + 1 < len(flat) and flat[k + 1][0] == m and (flat[k + 1][1] > j or not plain[m]):
             begin(k + 1)
         for copy in loads(k):
             copy.wait()
@@ -531,8 +530,7 @@
 
     units = []
     for m in range(n):
-        for j in range(subs[m]):
-            units += [(m, j, q) for q in [0] + near] if plain[m] else [(m, j, 0)]
+        units += [(m, j, q) for q in ([0] + near if plain[m] else [0]) for j in range(subs[m])]
     rings = [ring_of.index(sizes[m]) for m, j, q in units]
     index = [rings[:u].count(rings[u]) for u in range(len(units))]
     total_in = [rings.count(r) for r in range(len(ring_of))]
@@ -607,7 +605,6 @@
             )
             send(ref, ref, xs.at[u], xr.at[u], (other, me))
 
-    rows, width = attended.shape
     length = bias.shape[1]
     scale = HD**-0.5
     band = 32
@@ -632,9 +629,9 @@
         @pl.loop(lo, hi)
         def _(i):
             at = pl.ds(pl.multiple_of(i * band, band), band)
-            grad = arrived[0, at, :].astype(F32)
-            for q in range(1, count):
-                grad = grad + arrived[q, at, :].astype(F32)
+            grad = jnp.zeros((band, width), F32)
+            for q in range(count):
+                grad = grad + down_all[pl.ds(pl.multiple_of(q * rows + i * band, band), band), :].astype(F32)
             unit, rate = moments(middle[at, :])
             tally(0, grad * unit)
             tally(1, grad)
@@ -670,7 +667,7 @@
     part_cols = min(512, width)
 
     def outer_product(dst, left, start, size, right):
-        lhs = left[:, column(start, size)]
+        lhs = left[:, start : start + size] if isinstance(start, int) else left[:, column(start, size)]
 
         @pl.loop(0, right.shape[1] // min(part_cols, right.shape[1]))
         def _(k):
@@ -681,16 +678,140 @@
 
     staged = []
 
+    def stage_slot(m, q, size):
+        k = len(staged)
+        if k >= 2:
+            before = staged[k - 2]
+            wait(stage.at[k % 2, pl.ds(0, sizes[before[0]][0] * subs[before[0]]), : sizes[before[0]][1]], ss.at[before[0], before[1]])
+        staged.append((m, q))
+        return stage.at[k % 2, pl.ds(0, size), : sizes[m][1]]
+
     def weight_terms(m, left, right, some):
         size = width // count // 2
         for q in some:
-            k = len(staged)
-            if k >= 2:
-                wait(stage.at[k % 2], ss.at[staged[k - 2][0], staged[k - 2][1]])
-            outer_product(stage.at[k % 2], left, (away(q) * 2 + 1 - c) * size, size, right)
-            send(stage.at[k % 2], land[m].at[q], ss.at[m, q], sib.at[m, q], (other, me))
-            staged.append((m, q))
+            slot = stage_slot(m, q, size)
+            outer_product(slot, left, (away(q) * 2 + 1 - c) * size, size, right)
+            send(slot, land[m].at[q], ss.at[m, q], sib.at[m, q], (other, me))
             outer_product(spot(m, q), left, (away(q) * 2 + c) * size, size, right)
+
+    strip_jobs = []
+
+    def strip(source, start, size):
+        strip_jobs.append((source, start, size))
+
+    def strip_copy(k):
+        source, start, size = strip_jobs[k]
+        return pltpu.make_async_copy(
+            source.at[:, column(start, size)], strips.at[k % 2, :, pl.ds(0, size)], ts.at[k % 2]
+        )
+
+    def use_strip(k):
+        strip_copy(k).wait()
+        return strips.at[k % 2]
+
+    def next_strip(k):
+        if k < len(strip_jobs):
+            strip_copy(k).start()
+
+    down_size = hidden // count // 2
+    up_size = width // count // 2
+    tile = tiles.shape[1]
+    for q in [0] + near:
+        strip(act, away(q) * 2 * down_size, 2 * down_size)
+    for f in range(hidden // tile):
+        strip(slope, f * tile, tile)
+    for q in [0] + near:
+        strip(normed_two, (away(q) * 2 + 1 - c) * up_size, up_size)
+        strip(normed_two, (away(q) * 2 + c) * up_size, up_size)
+
+    def down_terms(i):
+        q = ([0] + near)[i]
+        if i == 0:
+            whole_down.wait()
+        left = use_strip(i)
+        slot = stage_slot(0, q, down_size)
+        for k in range(2):
+
+            @pl.when(c == k)
+            def _():
+                outer_product(slot, left, (1 - k) * down_size, down_size, down_all)
+
+        send(slot, land[0].at[q], ss.at[0, q], sib.at[0, q], (other, me))
+        for k in range(2):
+
+            @pl.when(c == k)
+            def _():
+                outer_product(spot(0, q), left, k * down_size, down_size, down_all)
+
+        next_strip(i + 2)
+
+    block = hidden // (groups)
+
+    def hidden_tile(f):
+        k = count + f
+        gate = use_strip(k)
+        if f + 1 < hidden // tile:
+            weight_rows(wdn, f + 1, width).start()
+        weight_rows(wdn, f, width).wait()
+        up_sums[pl.ds(f * (tile // block), tile // block), :] = jnp.zeros((tile // block, block), F32)
+
+        @pl.loop(0, everyone // rows)
+        def _(i):
+            at = pl.ds(pl.multiple_of(i * rows, rows), rows)
+            got = lax.dot_general(
+                down_all[at, :], tiles[f % 2], (((1,), (1,)), ((), ())), preferred_element_type=F32
+            )
+            low_grad = (got * gate[at, :tile].astype(F32)).astype(BF)
+            grad_hidden[at, f * tile : (f + 1) * tile] = low_grad
+            total = jnp.sum(low_grad.astype(F32), axis=0, keepdims=True)
+            for b in range(tile // block):
+                k_ = f * (tile // block) + b
+                up_sums[k_ : k_ + 1, :] += total[:, b * block : (b + 1) * block]
+
+        next_strip(k + 2)
+        if f + 1 == hidden // tile:
+            for q in near:
+                pl.semaphore_signal(ready, inc=1, device_id=(g, away(q)), device_id_type=MESH)
+
+    def up_terms(i):
+        q = ([0] + near)[i]
+        k = count + hidden // tile + 2 * i
+        slot = stage_slot(1, q, up_size)
+        outer_product(slot, use_strip(k), 0, up_size, grad_hidden)
+        next_strip(k + 2)
+        send(slot, land[1].at[q], ss.at[1, q], sib.at[1, q], (other, me))
+        outer_product(spot(1, q), use_strip(k + 1), 0, up_size, grad_hidden)
+        next_strip(k + 3)
+
+    def weight_rows(source, i, size):
+        return pltpu.make_async_copy(
+            source.at[pl.ds(i * tile, tile)], tiles.at[i % 2, :, pl.ds(0, size)], ws.at[i % 2]
+        )
+
+    def slice_out(d):
+        return pltpu.make_async_copy(
+            slices_stage.at[d % 2], slices.at[:, pl.ds(d * tile, tile)], ps.at[d % 2]
+        )
+
+    def slice_tile(d):
+        if d + 1 < width // tile:
+            weight_rows(wup, d + 1, hidden).start()
+        weight_rows(wup, d, hidden).wait()
+        if d >= 2:
+            slice_out(d - 2).wait()
+
+        @pl.loop(0, everyone // rows)
+        def _(i):
+            at = pl.ds(pl.multiple_of(i * rows, rows), rows)
+            slices_stage[d % 2, at, :] = lax.dot_general(
+                grad_hidden[at, :], tiles[d % 2, :, :hidden], (((1,), (1,)), ((), ())),
+                preferred_element_type=F32,
+            ).astype(BF)
+
+        slice_out(d).start()
+        if d + 1 == width // tile:
+            slice_out(d - 1).wait()
+            slice_out(d).wait()
 
     tile_rows = tiles.shape[1]
     tile_count = width // tile_rows
@@ -764,7 +885,12 @@
                 ).astype(BF)
                 ref[pl.ds(size, 16), :] = jnp.zeros((16, 2 * HD), BF)
                 ref[pl.ds(size, 16), :size] = sums[:, column(start, size)].astype(BF)
-                ref[pl.ds(size + 16, early.shape[2]), :] = early[away(q), which]
+                mine = up_sums[pl.ds(away(q) * 2 + which, 1), :]
+                mine = jnp.concatenate([mine] * (2 * HD // block), axis=1)
+                flat_at = lax.broadcasted_iota(jnp.int32, (16, 2 * HD), 0) * (2 * HD)
+                flat_at = flat_at + lax.broadcasted_iota(jnp.int32, (16, 2 * HD), 1)
+                own_place = lax.div(flat_at, block) == me
+                ref[pl.ds(size + 16, 16), :] = jnp.where(own_place, mine, 0.0).astype(BF)
             send(stage_kv.at[q], land[last].at[q], ss.at[last, q], sib.at[last, q], (other, me))
 
     def reuse(m):
@@ -780,60 +906,93 @@
     P_ = partial
     starts = [sum(len(t) for t in pair_tasks[:m]) for m in range(n)]
     pairs_ = lambda m, lo, hi: [P_(pair, starts[m] + k) for k in range(lo, min(hi, len(pair_tasks[m])))]
-    first = [*pairs_(0, 0, 99), *pairs_(1, 0, 99)]
-    for s, work in enumerate(first[AHEAD:]):
-        at_step(s // 2, work)
-    at_step(SLICE_STEP, send_slices)
-
     def got_slices():
         clear()
         for copy in own_copies:
             copy.wait()
-        own_slice.wait()
-        for q in near:
-            wait(arrived.at[q], gr.at[q])
+        for q in [0] + near:
+            wait(arrived(q), gr.at[q])
 
     order = near + [0]
-    half = len(order) // 2
-    at_step(NORM_STEP, got_slices, P_(second_norm, 0, bands // 2))
-    at_step(NORM_STEP + 1, P_(second_norm, bands // 2, bands), lambda: weight_tile(wo, 0).start(), P_(reuse, 2))
-    at_step(NORM_STEP + 2, P_(weight_terms, 2, attended, branch, order[:half]))
-    at_step(NORM_STEP + 3, P_(weight_terms, 2, attended, branch, order[half:]))
-    for k in range(4):
-        at_step(NORM_STEP + 4 + k, P_(attention_tiles, k * tile_count // 4, (k + 1) * tile_count // 4))
-    per = len(pair_tasks[2])
-    at_step(NORM_STEP + 5, *pairs_(2, 0, per // 2))
-    at_step(NORM_STEP + 6, *pairs_(2, per // 2, per))
-    at_step(NORM_STEP + 7, lambda: weight_tile(wq, 0).start(), P_(reuse, 3))
-    at_step(NORM_STEP + 8, P_(weight_terms, 3, normed, grad_q, order[:half]))
-    at_step(NORM_STEP + 9, P_(weight_terms, 3, normed, grad_q, order[half:]))
-    at_step(NORM_STEP + 10, P_(query_tiles, 0, tile_count // 2), *pairs_(3, 0, per // 2))
-    at_step(NORM_STEP + 11, P_(query_tiles, tile_count // 2, tile_count), *pairs_(3, per // 2, per))
-    at_step(NORM_STEP + 12, P_(first_norm, 0, bands // 2))
-    at_step(NORM_STEP + 13, P_(first_norm, bands // 2, bands), keyval_terms)
-    at_step(NORM_STEP + 14, *pairs_(4, 0, 99))
-
-    for work in first[:AHEAD]:
-        work()
+    quarter = lambda k: (k * bands // 4, (k + 1) * bands // 4)
+    tile_of = lambda k: (k * tile_count // 8, (k + 1) * tile_count // 8)
+    subs_0, subs_1 = subs[0], subs[1]
+
+    def begin_all():
+        next_strip(0)
+        next_strip(1)
+        down_terms(0)
+        for work in pairs_(0, 0, subs_0):
+            work()
+
+    queue = []
+    for i in range(1, count):
+        queue += [(3.5, P_(down_terms, i))] + [(0.3, x) for x in pairs_(0, i * subs_0, (i + 1) * subs_0)]
+    queue += [(0.0, lambda: weight_rows(wdn, 0, width).start())]
+    queue += [(12.0 / (hidden // tile), P_(hidden_tile, f)) for f in range(hidden // tile)]
+    queue += [(0.0, lambda: weight_rows(wup, 0, hidden).start())]
+    queue += [(1.5, P_(slice_tile, d)) for d in range(width // tile)]
+    queue += [(0.0, send_slices)]
+    for i in range(count):
+        queue += [(3.5, P_(up_terms, i))] + [(0.3, x) for x in pairs_(1, i * subs_1, (i + 1) * subs_1)]
+    later = [(0.0, got_slices)]
+    later += [(2.5, P_(second_norm, *quarter(k))) for k in range(4)]
+    later += [(0.0, lambda: weight_tile(wo, 0).start()), (0.0, P_(reuse, 2))]
+    later += [(16.0 / count, P_(weight_terms, 2, attended, branch, [q])) for q in order]
+    pairs_2, pairs_3 = pairs_(2, 0, 99), pairs_(3, 0, 99)
+    share_of = lambda work, k: [(0.4, x) for x in work[k * len(work) // 4 : (k + 1) * len(work) // 4]]
+    for k in range(8):
+        later += [(TILE_COST, P_(attention_tiles, *tile_of(k)))]
+        later += share_of(pairs_2, k) if k < 4 else []
+    later += [(0.0, lambda: weight_tile(wq, 0).start()), (0.0, P_(reuse, 3))]
+    later += [(16.0 / count, P_(weight_terms, 3, normed, grad_q, [q])) for q in order]
+    for k in range(8):
+        later += [(0.8, P_(query_tiles, *tile_of(k)))]
+        later += share_of(pairs_3, k) if k < 4 else []
+    later += [(2.5, P_(first_norm, *quarter(k))) for k in range(4)]
+    later += [(4.0, keyval_terms)]
+    later += [(1.0, work) for work in pairs_(4, 0, 99)]
+    step, spent = 0, 0.0
+    for some, start in ((queue, 0), (later, NORM_STEP)):
+        if start > step:
+            step, spent = start, 0.0
+        for cost, work in some:
+            if spent + cost > BUDGET and spent:
+                spent, step = 0.0, step + 1
+            spent += cost
+            at_step(step, work)
+    needs = {}
+    for m, per_unit in ((0, 1), (1, 1), (2, count), (3, count), (4, count)):
+        base_unit = [u for u in range(len(units)) if units[u][0] == m][0]
+        for k, work in enumerate(pair_tasks[m]):
+            needs.setdefault(base_unit + k // per_unit, []).append((m, k))
+    begin_all()
+    cursor = [0]
     steps = max(len(units) + LAG_OUT, max(plan) + 1)
     for step in range(steps):
         if step < len(units):
+            while any(starts[m] + k not in paired_set for m, k in needs[step]):
+                while not plan.get(cursor[0]):
+                    cursor[0] += 1
+                plan[cursor[0]].pop(0)()
             inward(step)
         if 0 <= step - LAG_MID < len(units):
             centre(step - LAG_MID)
         if 0 <= step - LAG_OUT < len(units):
             outward(step - LAG_OUT)
-        for work in plan.get(step, ()):
-            work()
+        for at in range(cursor[0], step + 1):
+            for work in plan.pop(at, ()):
+                work()
+        cursor[0] = max(cursor[0], step + 1)
 
     for m in range(n):
         if m not in share[m + 1 :]:
             wait(part[m], sent.at[m])
         for q in near + [0]:
-            if m < 2 or m == n - 1 or (m, q) in staged[-2:]:
+            if m == n - 1 or (m, q) in staged[-2:]:
                 wait(land[m].at[q], ss.at[m, q])
     for q in near:
-        wait(arrived.at[q], gs.at[q])
+        wait(arrived(q), gs.at[q])
     for u in range(len(units)):
         wait(result(u, 1 - c), xr.at[u])
         wait(result(u, c), xs.at[u])
@@ -842,18 +1001,19 @@
         pl.when(jnp.logical_not(middle_chip))(partial(wait, value(u), zs.at[u]))
 
 
-def back_all(groups, count, given, far, near_by, early):
-    rows, width = near_by[0].shape
+def back_all(groups, count, far, own, near_by):
+    rows, width = own[0].shape
+    everyone, hidden = far[0].shape
     size = width // count // 2
-    low = (size + 16 + early.shape[2], 2 * HD)
-    shapes = [x.shape[2:] for x in given] + [(size, width), (size, width), low]
-    plain, subs = (True, True, False, False, False), (2, 2, 2, 2, 1)
+    tile = 2 * HD
+    low = (size + 32, 2 * HD)
+    shapes = [(hidden // count // 2, width), (size, hidden), (size, width), (size, width), low]
+    plain, subs = (True, True, False, False, False), (4, 4, 4, 4, 1)
     n = len(shapes)
     sizes = [(s[0] // k, s[1]) for s, k in zip(shapes, subs)]
     share = list(range(n))
     for m in (2, 3):
-        if shapes[m] == shapes[m - 2]:
-            share[m] = m - 2
+        share[m] = m - 2 if shapes[m] == shapes[m - 2] else 2
     rings = sorted(set(sizes))
     units = sum(s * (count if f else 1) for s, f in zip(subs, plain))
     slots = [min(RING, sum(s * (count if f else 1) for s, f, z in zip(subs, plain, sizes) if z == r)) for r in rings]
@@ -861,35 +1021,63 @@
     dma, regular = pltpu.SemaphoreType.DMA, pltpu.SemaphoreType.REGULAR
     out = [jax.ShapeDtypeStruct((2, count if f else 1) + s, BF) for s, f in zip(shapes, plain)]
     out += [jax.ShapeDtypeStruct((count,) + s, BF) for s in shapes]
-    tile = 2 * HD
     scratch = [pltpu.VMEM((count - 1,) + shapes[m], BF) for m in range(n) if share[m] == m]
     scratch += [pltpu.VMEM((count,) + s, BF) for s in shapes]
     scratch += [pltpu.VMEM((2,) + r, BF) for r in rings]
     scratch += [pltpu.VMEM((k,) + r, BF) for k, r in zip(slots, rings)] * 2
     scratch += [
-        pltpu.VMEM((count, rows, width), BF), pltpu.VMEM((rows, width), F32), pltpu.VMEM((rows, width), BF),
-        pltpu.VMEM((rows, width), F32),
+        pltpu.VMEM((everyone, width), BF), pltpu.VMEM((everyone, hidden), BF),
+        pltpu.VMEM((2, everyone, max(2 * hidden // count // 2, tile)), BF), pltpu.VMEM((2, everyone, tile), BF),
+        pltpu.VMEM((rows, width), F32), pltpu.VMEM((rows, width), BF), pltpu.VMEM((rows, width), F32),
         pltpu.VMEM((rows, width), BF), pltpu.VMEM((rows, width), BF), pltpu.VMEM((2, tile, width), BF),
-        pltpu.VMEM((2, size, width), BF), pltpu.VMEM((count,) + low, BF), pltpu.VMEM((rows, 2 * HD), F32),
-        pltpu.VMEM((16, width), F32),
-        dma((n, count)), dma((2, 2)), dma((n,)), dma((n, max(subs), count)), dma((units,)), dma((units,)),
+        pltpu.VMEM((2, max(s[0] for s in shapes[:4]), width), BF), pltpu.VMEM((count,) + low, BF),
+        pltpu.VMEM((rows, 2 * HD), F32),
+        pltpu.VMEM((16, width), F32), pltpu.VMEM((max(16, groups), hidden // groups), F32),
+        pltpu.VMEM((rows, width), BF), pltpu.VMEM((rows, width), BF), pltpu.VMEM((rows, width), BF),
+        pltpu.VMEM((rows, width), BF),
+        dma((n, count)), dma((2,)), dma((n,)), dma((n, max(subs), count)), dma((units,)), dma((units,)),
         dma((units,)), dma((units,)), dma((units,)), dma((units,)), dma((units,)), dma((units,)),
-        dma((n, count)), dma((count,)), dma((count,)), dma((2,)), dma((2,)),
-        regular((len(rings), max(slots))), regular((len(rings), max(slots))),
+        dma((n, count)), dma((count,)), dma((count,)), dma((2,)), dma((7,)), dma((2,)), dma((2,)),
+        regular((len(rings), max(slots))), regular((len(rings), max(slots))), regular,
     ]
     got = pl.pallas_call(
         partial(back_kernel, groups, count, subs, plain, sizes, share),
-        out_shape=tuple(out) + (jax.ShapeDtypeStruct((rows, width), BF),),
-        in_specs=[any_] * 7 + [vmem] * 9,
-        out_specs=(any_,) * (2 * n) + (vmem,),
+        out_shape=tuple(out) + (jax.ShapeDtypeStruct((everyone, width), BF), jax.ShapeDtypeStruct((rows, width), BF)),
+        in_specs=[any_] * 13 + [vmem] * 4,
+        out_specs=(any_,) * (2 * n + 1) + (vmem,),
         scratch_shapes=scratch,
         compiler_params=pltpu.CompilerParams(
             collective_id=2, has_side_effects=True, vmem_limit_bytes=60 * 1024 * 1024
         ),
         cost_estimate=pl.CostEstimate(flops=0, bytes_accessed=200_000_000, transcendentals=0),
         name="back_all",
-    )(*given, *far, *near_by, early)
+    )(*far, *own, *near_by)
     return got[:n], got[-1]
+
+
+def lift_kernel(rows, weight, bias, act, slope):
+    u = jnp.dot(rows[...], weight[...], preferred_element_type=F32) + bias[...]
+    root = 0.7978845608028654
+    t = jnp.tanh(root * (u + 0.044715 * (u * u * u)))
+    half = 0.5 * (1.0 + t)
+    act[...] = (u * half).astype(BF)
+    slope[...] = (half + 0.5 * u * (1.0 - t * t) * (root * (1.0 + 3 * 0.044715 * (u * u)))).astype(BF)
+
+
+def lift(rows, weight, bias):
+    n, hidden = rows.shape[0], weight.shape[1]
+    tile = 2 * HD
+    out = jax.ShapeDtypeStruct((n, hidden), BF)
+    column = lambda k: pl.BlockSpec((k, tile), lambda i: (0, i))
+    return pl.pallas_call(
+        lift_kernel,
+        out_shape=(out, out),
+        grid=(hidden // tile,),
+        in_specs=[pl.BlockSpec(rows.shape, lambda i: (0, 0)), column(weight.shape[0]), column(1)],
+        out_specs=(column(n), column(n)),
+        compiler_params=pltpu.CompilerParams(vmem_limit_bytes=48 * 1024 * 1024),
+        name="lift",
+    )(rows, weight, bias)
 
 
 def widen_kernel(block, size, down, up, out, query, low, o_down, o_up, o_out, o_query, o_low, *lines):
@@ -1090,36 +1278,17 @@
     grad_down = take_rows(cot_rows.reshape(group_rows, length, width), inverse, lengths)
     grad_down = grad_down.reshape(group_rows * length, width)
 
-    hidden_pre = mm(normed_two, weight_up) + up_part
-    gelu_tanh = partial(jax.nn.gelu, approximate=True)
-    activated_wide, gelu_pull = jax.vjp(gelu_tanh, hidden_pre)
-    activated = activated_wide.astype(BF)
-    grad_hidden = gelu_pull(mm_nt(grad_down, weight_down))[0].astype(BF)
-    slices = mm_nt(grad_hidden, weight_up).astype(BF).reshape(count, rows, width)
-    down_grad = mm_tn(activated, grad_down).astype(BF)
-    up_grad = mm_tn(normed_two, grad_hidden).astype(BF)
-
+    activated, slope = lift(normed_two, weight_up, up_part)
     result = mm(activated, weight_down).astype(BF).reshape(group_rows, length, width)
     result = finish_rows(result, deal, lengths, me, middle.reshape(micro, length, width), table)
     block_output = lax.psum_scatter(
         result.reshape(group_rows * length, width), "shard", scatter_dimension=0, tiled=True
     ).reshape(micro, length, width)
 
-    per = groups // count
-    up_bias_part = jnp.sum(grad_hidden.astype(F32), axis=0).reshape(count, per, 1, block)
-    spot = (jnp.arange(count, dtype=jnp.int32) == me)[None, None, :, None]
-    up_bias_part = jnp.where(spot, up_bias_part, 0.0).reshape(count, 2, -1)
-    early = up_bias_part.astype(BF)
-    fill = -early.shape[2] % (16 * 2 * HD)
-    early = jnp.pad(early, ((0, 0), (0, 0), (0, fill))).reshape(count, 2, -1, 2 * HD)
-
-    cut = lambda x: x.reshape(count, 2, x.shape[0] // count // 2, x.shape[1])
-    near_by = (
-        attended, queries, keyvals, normed_one, flat_tokens, bias, table, weight_keyval,
-    )
     full, input_grad = back_all(
-        groups, count, (cut(down_grad), cut(up_grad)),
-        (slices, weight_query, weight_out, middle, grad_down), near_by, early,
+        groups, count,
+        (activated, slope, grad_down, weight_down, normed_two, weight_up, weight_query, weight_out, middle),
+        (attended, queries, normed_one, flat_tokens), (keyvals, bias, table, weight_keyval),
     )
     input_grad = input_grad.reshape(micro, length, width)
 

time: 694 us -> 621 us (0.89)
  matrix products: 93.3 us -> 13.8 us
  Pallas kernels: 558 us -> 566 us
    dot_general x4 -> x0, matrix products: 62.8 us -> none  [the longest x2 34.7 us: mm_nt(): lax.dot_general(left, right, (((1,), (1,)), ((), ())), preferred_element_...]
    pallas_call x0 -> x1, Pallas kernels: none -> 17.9 us  [lift(): pl.pallas_call(lift_kernel, out_shape=(out, out), grid=(hidden // tile,),...]
    dot_general x2 -> x1, matrix products: 30.5 us -> 13.8 us  [mm(): return jnp.dot(left, right, preferred_element_type=F32)]
    pallas_call x1, Pallas kernels: 313 us -> 303 us  [back_all(): pl.pallas_call(partial(back_kernel, groups, count, subs, plain, sizes, sh...]
  transfers between devices with their start and end apart: 2 -> 2, of which waited for: 0 -> 0; matrix products, arithmetic and copies ran while one was open for 12% -> 0% of each run, Pallas kernels for 61% -> 70%
where the time goes in v5:
time: 621 us; the launch traced here: 611 us
  Pallas kernels  566 us (91%)
  local copies, waits for them, and re-layouts  14.4 us (2%)
  between operations  14.4 us (2%)
  matrix products  13.8 us (2%)
    pallas_call x1, Pallas kernels, back_all(): pl.pallas_call(partial(back_kernel, groups, count, subs, plain, sizes, sh...  303 us
    pallas_call x1, Pallas kernels, gather_all(): pl.pallas_call(partial(gather_kernel, groups, count), out_shape=(tall(wq)...  128 us
    pallas_call x1, Pallas kernels, attend(): pl.pallas_call(partial(attend_kernel, groups, count), out_shape=(shape((c...  75.9 us
    pallas_call x1, Pallas kernels, widen(): pl.pallas_call(partial(widen_kernel, block, size), out_shape=(shape(*down...  22.9 us
    pallas_call x1, Pallas kernels, lift(): pl.pallas_call(lift_kernel, out_shape=(out, out), grid=(hidden // tile,),...  17.9 us
    dot_general x1, matrix products, mm(): return jnp.dot(left, right, preferred_element_type=F32)  13.8 us
  transfers between devices with their start and end apart: 2, of which 0 were waited for; matrix products, arithmetic and copies ran while one was open for 0% of the time, Pallas kernels for 70%

profile of v5, /device:TPU:0, one launch (start us, length us, event | category | flops | bytes accessed | tf_op | source)
XLA Modules:
  0.0 610.7 jit_solution(8211934117086767311)
XLA Ops:
  7.2 0.0 copy-start.12
  7.2 0.0 copy-start
  7.2 0.0 copy-start.5
  7.2 0.0 all-gather.2.cloned.1.call-start
  7.3 0.9 fusion
  8.2 0.7 pad_bitcast_fusion.9
  8.8 2.3 cut.1.upc
  11.1 0.7 pad_bitcast_fusion.2
  11.8 0.7 pad_bitcast_fusion.3
  12.5 0.7 pad_bitcast_fusion.5
  13.2 0.7 pad_bitcast_fusion.7
  13.9 0.8 dynamic_update_slice.4
  14.6 1.2 stack.55.small
  15.8 128.1 %gather_all.1 = (bf16[2048,2048]{1,0:T(8,128)(2,1)}, bf16[2048,2048]{1,0:T(8,128)(2,1)}, bf16[2048,256]{1,0:T(8,128)(2,1)}, bf16[512,128]{1,0:T(8,128)(2,1)}, bf16[2048,2048]{1,0:T(8,128)(2,1)}) custom-call(bf16[64,2048]{1,0:T(8,128)(2,1)} %wq.1, bf16[64,2048]{1,0:T(8,128)(2,1)} %wo.1, bf16[64,256]{1,0:T(8,128)(2,1)} %wkv.1, bf16[16,128]{1,0:T(8,128)(2,1)} %stack.55.small, ...), custom_call_target="tpu_custom_call" | custom-call | bytes 100000000 | tf_op jit(solution)/shard_map/gather_all/pallas_call | solution.py:204
  143.9 0.0 all-gather.2.cloned.1.call-update
  144.0 0.0 reduce-scatter.2.cloned.1.call-start
  144.0 0.0 copy-done.12
  144.0 0.1 copy.38.lengths
  144.1 0.0 copy-start.10
  144.1 0.0 copy-done
  144.1 0.0 copy-done.5
  144.1 0.0 copy-start.9
  144.1 0.9 copy-done.9
  145.0 75.9 %attend.1 = (bf16[1024,2048]{1,0:T(8,128)(2,1)}, bf16[1024,2048]{1,0:T(8,128)(2,1)}, bf16[256,2048]{1,0:T(8,128)(2,1)S(1)}, bf16[256,2048]{1,0:T(8,128)(2,1)S(1)...) custom-call(bf16[256,2048]{1,0:T(8,128)(2,1)S(1)} %bitcast.50, ...), custom_call_target="tpu_custom_call" | custom-call | flops 5000000000 | bytes 100000000 | tf_op jit(solution)/shard_map/attend/pallas_call | solution.py:377
  220.9 0.0 copy-done.10
  220.9 0.0 copy-start.2
  220.9 1.0 copy-done.2
  221.9 0.0 copy-start.3
  221.9 1.0 copy-done.3
  222.9 0.0 copy-start.4
  222.9 1.0 copy-done.4
  223.8 0.0 copy-start.6
  223.8 0.0 copy-start.7
  223.8 0.0 copy-start.8
  223.8 0.0 copy-start.14
  223.8 17.9 %lift.1 = (bf16[1024,2048]{1,0:T(8,128)(2,1)S(1)}, bf16[1024,2048]{1,0:T(8,128)(2,1)}) custom-call(bf16[1024,2048]{1,0:T(8,128)(2,1)} %get-tuple-element.64.rows.refs_4_, bf16[2048,2048]{1,0:T(8,128)(2,1)} %get-tuple-element.65.weight.refs_5_, f32[1,2048]{1,0:T(1,128)S(1)} %get-tuple-element.66.bias), custom_call_target="tpu_custom_call" | custom-call | tf_op jit(solution)/shard_map/lift/pallas_call | solution.py:1072
  241.7 0.0 copy-done.6
  241.7 0.0 copy-done.7
  241.7 0.0 copy-done.8
  241.7 0.0 copy-start.1
  241.7 2.0 copy-done.1
  243.7 0.0 copy-done.14
  243.7 0.5 broadcast_subtract_fusion.deal
  244.2 0.0 all-gather.2.cloned.1.call-done.refs_3_
  244.2 13.8 %convolution_convert_fusion = bf16[1024,2048]{1,0:T(8,128)(2,1)} fusion(bf16[1024,2048]{1,0:T(8,128)(2,1)} %copy-done.1, bf16[2048,2048]{1,0:T(8,128)(2,1)} %all-gather.2.cloned.1.call-done.refs_3_), kind=kOutput, calls=%fused_computation | convolution fusion | flops 8592031744 | bytes 16777216 | tf_op jit(solution)/shard_map/dot_general | solution.py:26
  258.0 8.5 %finish_rows.1 = bf16[8,128,2048]{2,1,0:T(8,128)(2,1)} custom-call(s32[8]{0:T(128)} %broadcast_subtract_fusion.deal, s32[8,4]{1,0:T(8,128)} %copy-done.10, s32[1]{0:T(128)} %bitcast.place, bf16[8,128,2048]{2,1,0:T(8,128)(2,1)} %bitcast.56, f32[2,128,2048]{2,1,0:T(8,128)} %bitcast.54, f32[16,2048]{1,0:T(8,128)} %copy-done.6), custom_call_target="tpu_custom_call" | custom-call | tf_op jit(solution)/shard_map/finish_rows/pallas_call | solution.py:1188
  266.5 0.0 copy-start.13
  266.5 0.0 reduce-scatter.2.cloned.1.call-update
  266.6 0.6 copy-done.13
  267.2 0.6 select_reduce_fusion.order
  267.8 7.7 %take_rows.1 = bf16[8,128,2048]{2,1,0:T(8,128)(2,1)} custom-call(s32[8]{0:T(128)} %select_reduce_fusion.order, s32[8,4]{1,0:T(8,128)} %copy-done.10, bf16[8,128,2048]{2,1,0:T(8,128)(2,1)} %bitcast.57), custom_call_target="tpu_custom_call" | custom-call | tf_op jit(solution)/shard_map/take_rows/pallas_call | solution.py:1156
  275.5 303.1 %back_all.1 = (bf16[2,4,256,2048]{3,2,1,0:T(8,128)(2,1)}, bf16[2,4,256,2048]{3,2,1,0:T(8,128)(2,1)}, bf16[2,1,256,2048]{3,2,1,0:T(8,128)(2,1)}, bf16[2,1,256,204...) custom-call(bf16[1024,2048]{1,0:T(8,128)(2,1)} %copy-done.1, ...), custom_call_target="tpu_custom_call" | custom-call | bytes 200000000 | tf_op jit(solution)/shard_map/back_all/pallas_call | solution.py:1043
  578.5 0.0 copy-start.11
  578.6 22.9 %widen.1 = (f32[2048,2048]{1,0:T(8,128)}, f32[512,8192]{1,0:T(8,128)}, f32[512,2048]{1,0:T(8,128)}, f32[512,2048]{1,0:T(8,128)}, f32[512,256]{1,0:T(8,128)}, /*i...) custom-call(bf16[2048,2048]{1,0:T(8,128)(2,1)} %bitcast.55, ...), custom_call_target="tpu_custom_call" | custom-call | tf_op jit(solution)/shard_map/widen/pallas_call | solution.py:1118
  601.5 1.2 dynamic-slice_bitcast_fusion
  602.7 0.0 reduce-scatter.2.cloned.1.call-done
  602.7 0.0 copy-done.11
  602.7 1.0 copy.42
  (3 shorter events, 0.0 us)
Async XLA Ops:
  7.2 136.8 %copy-start.12 = (s32[8,4]{0,1:T(4,128)S(1)}, s32[8,4]{0,1:T(4,128)}, u32[]{:S(2)}) copy-start(s32[8,4]{0,1:T(4,128)} %param.20) | copy-start | bytes 388
  7.2 136.9 %copy-start = (bf16[2,128,2048]{2,1,0:T(8,128)(2,1)S(1)}, bf16[2,128,2048]{2,1,0:T(8,128)(2,1)}, u32[]{:S(2)}) copy-start(bf16[2,128,2048]{2,1,0:T(8,128)(2,1)} %param.18) | copy-start | bytes 3145732
  7.2 136.9 %copy-start.5 = (bf16[2,128,2048]{2,1,0:T(8,128)(2,1)S(1)}, bf16[2,128,2048]{2,1,0:T(8,128)(2,1)}, u32[]{:S(2)}) copy-start(bf16[2,128,2048]{2,1,0:T(8,128)(2,1)} %param.19) | copy-start | bytes 3145732
  7.2 237.0 %all-gather.2.cloned.1.call-start = ((), (), s32[]{:S(2)}) async-start(), calls=%async_computation.1 | async-start | bytes 9437184 | tf_op jit(solution)/shard_map/all_gather | solution.py:1269
  144.0 458.8 %reduce-scatter.2.cloned.1.call-start = ((), (), s32[]{:S(2)}) async-start(), calls=%async_computation.2 | async-start | bytes 5242880 | tf_op jit(solution)/shard_map/reduce_scatter | solution.py:1284
  144.1 76.8 %copy-start.10 = (s32[8,4]{1,0:T(8,128)}, s32[8,4]{1,0:T(8,128)S(1)}, u32[]{:S(2)}) copy-start(s32[8,4]{1,0:T(8,128)S(1)} %copy.38.lengths) | copy-start | bytes 388
  144.1 0.9 copy-start.9
  220.9 1.0 copy-start.2
  221.9 1.0 copy-start.3
  222.9 1.0 copy-start.4
  223.8 17.9 %copy-start.6 = (f32[16,2048]{1,0:T(8,128)}, f32[16,2048]{1,0:T(8,128)S(1)}, u32[]{:S(2)}) copy-start(f32[16,2048]{1,0:T(8,128)S(1)} %get-tuple-element.70.table.refs_15_) | copy-start | bytes 393220
  223.8 17.9 %copy-start.7 = (bf16[256,256]{1,0:T(8,128)(2,1)}, bf16[256,256]{1,0:T(8,128)(2,1)S(1)}, u32[]{:S(2)}) copy-start(bf16[256,256]{1,0:T(8,128)(2,1)S(1)} %get-tuple-element.76.refs_13_) | copy-start | bytes 393220
  223.8 17.9 %copy-start.8 = (f32[256,128]{1,0:T(8,128)}, f32[256,128]{1,0:T(8,128)S(1)}, u32[]{:S(2)}) copy-start(f32[256,128]{1,0:T(8,128)S(1)} %get-tuple-element.77.refs_14_) | copy-start | bytes 393220
  223.8 19.9 %copy-start.14 = (s32[8]{0:T(128)S(1)}, s32[8]{0:T(128)}, u32[]{:S(2)}) copy-start(s32[8]{0:T(128)} %param.21) | copy-start | bytes 100
  241.7 2.0 copy-start.1
  266.5 0.7 copy-start.13
  578.5 24.2 %copy-start.11 = (bf16[256,2048]{1,0:T(8,128)(2,1)S(1)}, bf16[256,2048]{1,0:T(8,128)(2,1)}, u32[]{:S(2)}) copy-start(bf16[256,2048]{1,0:T(8,128)(2,1)} %get-tuple-element.78) | copy-start | bytes 3145732
Sparse Core Ops, SparseCore 0:
  144.1 81.3 all-gather.1
  266.7 63.7 reduce-scatter.1

commit v6 on v5

--- a/solution.py
+++ b/solution.py
@@ -22,10 +22,6 @@
 RING = 6
 
 
-def mm(left, right):
-    return jnp.dot(left, right, preferred_element_type=F32)
-
-
 def cube_tree(count, parity, q):
     order = list(range(count.bit_length() - 1))
     if parity:
@@ -137,21 +133,23 @@
     for a in cuts:
         first(a, spot(a, p, me))
 
-    def plane(z):
+    def plane(z, far):
         for q in near_first(count):
+            if far != (q & (q - 1) != 0):
+                continue
             for a in range(full):
                 ref = spot(a, z, lax.bitwise_xor(me, q))
                 wait(ref, pr.at[a, z, q])
                 across(a, ref, z, q)
                 aside(a, ref, z, q)
 
-    def planes(hop):
+    def planes(hop, far):
         if hop == 0:
-            plane(p)
+            plane(p, far)
             return
         for way in range(2):
             z = p - hop if way == 0 else p + hop
-            pl.when(may_take(way, hop))(partial(plane, z))
+            pl.when(may_take(way, hop))(partial(plane, z, far))
 
     def arrive(a, hop):
         for way in range(2):
@@ -172,10 +170,14 @@
     for hop in range(1, chips):
         for a in range(full):
             arrive(a, hop)
-        planes(hop - 1)
+        planes(hop - 1, False)
+        if hop > 1:
+            planes(hop - 2, True)
         for a in cuts:
             arrive(a, hop)
-    planes(chips - 1)
+    planes(chips - 1, False)
+    for hop in (chips - 2, chips - 1):
+        planes(hop, True)
 
     for copy in mine[1:]:
         copy.wait()
@@ -259,8 +261,10 @@
         for m in cube_tree(count, k, q):
             send(src, place(ref, k, lax.bitwise_xor(me, q)), sends.at[k], gets.at[k, q ^ m], m)
 
-    def take_all(ref, sends, gets):
+    def take(ref, sends, gets, far):
         for q in near:
+            if far != (q & (q - 1) != 0):
+                continue
             for k in range(2):
                 got = place(ref, k, lax.bitwise_xor(me, q))
                 wait(got, gets.at[k, q])
@@ -341,6 +345,7 @@
                     h * length : (h + 1) * length
                 ]
 
+    take(cot_all, cs, cr, False)
     loads[2].wait()
     wide = min(512, width)
 
@@ -350,7 +355,6 @@
         branch = jnp.dot(attended[...], wo_v[:, cols], preferred_element_type=F32)
         middle[:, cols] = tokens[:, cols].astype(F32) + branch + vectors[3:4, cols]
 
-    take_all(cot_all, cs, cr)
     for k in range(2):
 
         @pl.loop(k * half // band, (k + 1) * half // band)
@@ -361,7 +365,9 @@
         pass_on(near_all, second.at[pl.ds(k * half, half)], k, 0, ns, nr)
     own = pltpu.make_async_copy(second, near_all.at[pl.ds(pl.multiple_of(me * rows, 16), rows)], loc.at[1])
     own.start()
-    take_all(near_all, ns, nr)
+    take(cot_all, cs, cr, True)
+    take(near_all, ns, nr, False)
+    take(near_all, ns, nr, True)
     own_cot.wait()
     own.wait()
     for k in range(2):
@@ -1146,60 +1152,69 @@
     return jnp.where(places < used(lengths, row), x, 0.0)
 
 
-def take_kernel(order, lengths, x, out):
-    out[0] = masked(x[0].astype(F32), lengths, pl.program_id(0)).astype(BF)
+def take_kernel(order, lengths, values, out, held, got, put):
+    count = held.shape[0]
+    takes = [pltpu.make_async_copy(values.at[order[r]], held.at[r], got.at[r]) for r in range(count)]
+    puts = [pltpu.make_async_copy(held.at[r], out.at[r], put.at[r]) for r in range(count)]
+    for take in takes:
+        take.start()
+    for r in range(count):
+        takes[r].wait()
+        held[r] = masked(held[r].astype(F32), lengths, r).astype(BF)
+        puts[r].start()
+    for copy in puts:
+        copy.wait()
 
 
 def take_rows(values, order, lengths):
-    _, length, width = values.shape
-    spec = lambda f: pl.BlockSpec((1, length, width), f)
+    count = values.shape[0]
+    smem, any_ = pl.BlockSpec(memory_space=pltpu.SMEM), pl.BlockSpec(memory_space=pl.ANY)
     return pl.pallas_call(
         take_kernel,
         out_shape=jax.ShapeDtypeStruct(values.shape, BF),
-        grid_spec=pltpu.PrefetchScalarGridSpec(
-            num_scalar_prefetch=2,
-            grid=(values.shape[0],),
-            in_specs=[spec(lambda r, order, lengths: (order[r], 0, 0))],
-            out_specs=spec(lambda r, order, lengths: (r, 0, 0)),
-        ),
+        in_specs=[smem, smem, any_],
+        out_specs=any_,
+        scratch_shapes=[
+            pltpu.VMEM(values.shape, BF), pltpu.SemaphoreType.DMA((count,)), pltpu.SemaphoreType.DMA((count,)),
+        ],
+        compiler_params=pltpu.CompilerParams(vmem_limit_bytes=32 * 1024 * 1024),
         name="take_rows",
     )(order, lengths, values)
 
 
-def finish_kernel(deal, lengths, place, x, middle, table, out):
-    row = deal[pl.program_id(0)]
-    micro = middle.shape[0]
-    term = x[0].astype(F32)
-    own = lax.div(row, micro) == place[0]
-
-    @pl.when(own)
-    def _():
-        whole = term + middle[lax.rem(row, micro)] + table[6:7, :]
-        out[0] = masked(whole, lengths, row).astype(BF)
-
-    @pl.when(jnp.logical_not(own))
-    def _():
-        out[0] = masked(term, lengths, row).astype(BF)
-
-
-def finish_rows(values, deal, lengths, me, middle, table):
-    _, length, width = values.shape
-    spec = lambda f: pl.BlockSpec((1, length, width), f)
+def finish_kernel(deal, lengths, place, first, second, weight, middle, table, out):
+    step = pl.program_id(0)
+    micro, length, width = middle.shape
+    wide = min(512, width)
+    left = jnp.concatenate([first[0], second[0]], axis=0)
+    for k in range(width // wide):
+        cols = pl.ds(k * wide, wide)
+        got = jnp.dot(left, weight[:, cols], preferred_element_type=F32)
+        for i in range(2):
+            row = deal[2 * step + i]
+            term = got[i * length : (i + 1) * length]
+            own = lax.div(row, micro) == place[0]
+            extra = middle[lax.rem(row, micro), :, cols] + table[6:7, cols]
+            out[i, :, cols] = masked(term + jnp.where(own, extra, 0.0), lengths, row).astype(BF)
+
+
+def finish_rows(values, weight, deal, lengths, me, middle, table):
+    count, length, depth = values.shape
+    width = weight.shape[1]
+    row = lambda i: pl.BlockSpec((1, length, depth), lambda j, deal, lengths, me: (deal[2 * j + i], 0, 0))
+    still = lambda x: pl.BlockSpec(x.shape, lambda j, deal, lengths, me: (0,) * x.ndim)
     return pl.pallas_call(
         finish_kernel,
-        out_shape=jax.ShapeDtypeStruct(values.shape, BF),
+        out_shape=jax.ShapeDtypeStruct((count, length, width), BF),
         grid_spec=pltpu.PrefetchScalarGridSpec(
             num_scalar_prefetch=3,
-            grid=(values.shape[0],),
-            in_specs=[
-                spec(lambda j, deal, lengths, me: (deal[j], 0, 0)),
-                pl.BlockSpec(middle.shape, lambda j, deal, lengths, me: (0, 0, 0)),
-                pl.BlockSpec(table.shape, lambda j, deal, lengths, me: (0, 0)),
-            ],
-            out_specs=spec(lambda j, deal, lengths, me: (j, 0, 0)),
+            grid=(count // 2,),
+            in_specs=[row(0), row(1), still(weight), still(middle), still(table)],
+            out_specs=pl.BlockSpec((2, length, width), lambda j, deal, lengths, me: (j, 0, 0)),
         ),
+        compiler_params=pltpu.CompilerParams(vmem_limit_bytes=48 * 1024 * 1024),
         name="finish_rows",
-    )(deal, lengths, me.reshape(1), values, middle, table)
+    )(deal, lengths, me.reshape(1), values, values, weight, middle, table)
 
 
 def cut_kernel(groups, count, block, x, out):
@@ -1279,8 +1294,10 @@
     grad_down = grad_down.reshape(group_rows * length, width)
 
     activated, slope = lift(normed_two, weight_up, up_part)
-    result = mm(activated, weight_down).astype(BF).reshape(group_rows, length, width)
-    result = finish_rows(result, deal, lengths, me, middle.reshape(micro, length, width), table)
+    result = finish_rows(
+        activated.reshape(group_rows, length, hidden), weight_down, deal, lengths, me,
+        middle.reshape(micro, length, width), table,
+    )
     block_output = lax.psum_scatter(
         result.reshape(group_rows * length, width), "shard", scatter_dimension=0, tiled=True
     ).reshape(micro, length, width)

time: 621 us -> 604 us (0.973)
  matrix products: 13.8 us -> 0 us
  Pallas kernels: 566 us -> 559 us
    dot_general x1 -> x0, matrix products: 13.8 us -> none  [mm(): return jnp.dot(left, right, preferred_element_type=F32)]
    pallas_call x1, Pallas kernels: 128 us -> 120 us  [gather_all(): pl.pallas_call(partial(gather_kernel, groups, count), out_shape=(tall(wq)...]
    pallas_call x1, Pallas kernels: 8.52 us -> 15 us  [finish_rows(): pl.pallas_call(finish_kernel, out_shape=jax.ShapeDtypeStruct((count, leng...]
    unnamed x32 -> x34, local copies, waits for them, and re-layouts: 7.56 us -> 12.5 us
  transfers between devices with their start and end apart: 2 -> 2, of which waited for: 0 -> 0; matrix products, arithmetic and copies ran while one was open for 0% -> 0% of each run, Pallas kernels for 70% -> 71%
where the time goes in v6:
time: 604 us; the launch traced here: 594 us
  Pallas kernels  559 us (93%)
  local copies, waits for them, and re-layouts  19.3 us (3%)
  between operations  14.6 us (2%)
    pallas_call x1, Pallas kernels, back_all(): pl.pallas_call(partial(back_kernel, groups, count, subs, plain, sizes, sh...  304 us
    pallas_call x1, Pallas kernels, gather_all(): pl.pallas_call(partial(gather_kernel, groups, count), out_shape=(tall(wq)...  120 us
    pallas_call x1, Pallas kernels, attend(): pl.pallas_call(partial(attend_kernel, groups, count), out_shape=(shape((c...  75 us
    pallas_call x1, Pallas kernels, widen(): pl.pallas_call(partial(widen_kernel, block, size), out_shape=(shape(*down...  22.9 us
    pallas_call x1, Pallas kernels, lift(): pl.pallas_call(lift_kernel, out_shape=(out, out), grid=(hidden // tile,),...  17.8 us
    pallas_call x1, Pallas kernels, finish_rows(): pl.pallas_call(finish_kernel, out_shape=jax.ShapeDtypeStruct((count, leng...  15 us
    unnamed x34, local copies, waits for them, and re-layouts  12.5 us
  transfers between devices with their start and end apart: 2, of which 0 were waited for; matrix products, arithmetic and copies ran while one was open for 0% of the time, Pallas kernels for 71%

profile of v6, /device:TPU:0, one launch (start us, length us, event | category | flops | bytes accessed | tf_op | source)
XLA Modules:
  0.0 593.8 jit_solution(8764908599356035868)
XLA Ops:
  7.2 0.0 copy-start.14
  7.2 0.0 copy-start.3
  7.2 0.0 copy-start.8
  7.2 0.0 all-gather.2.cloned.1.call-start
  7.3 0.9 fusion
  8.2 0.7 pad_bitcast_fusion.9
  8.8 2.3 cut.1.upc
  11.1 0.7 pad_bitcast_fusion.2
  11.8 0.7 pad_bitcast_fusion.3
  12.5 0.7 pad_bitcast_fusion.5
  13.2 0.7 pad_bitcast_fusion.7
  13.9 0.8 dynamic_update_slice.4
  14.6 1.2 stack.55.small
  15.8 119.5 %gather_all.1 = (bf16[2048,2048]{1,0:T(8,128)(2,1)}, bf16[2048,2048]{1,0:T(8,128)(2,1)}, bf16[2048,256]{1,0:T(8,128)(2,1)}, bf16[512,128]{1,0:T(8,128)(2,1)}, bf16[2048,2048]{1,0:T(8,128)(2,1)}) custom-call(bf16[64,2048]{1,0:T(8,128)(2,1)} %wq.1, bf16[64,2048]{1,0:T(8,128)(2,1)} %wo.1, bf16[64,256]{1,0:T(8,128)(2,1)} %wkv.1, bf16[16,128]{1,0:T(8,128)(2,1)} %stack.55.small, ...), custom_call_target="tpu_custom_call" | custom-call | bytes 100000000 | tf_op jit(solution)/shard_map/gather_all/pallas_call | solution.py:206
  135.4 0.0 all-gather.2.cloned.1.call-update
  135.4 0.0 reduce-scatter.2.cloned.1.call-start
  135.5 0.0 copy-done.14
  135.5 0.1 copy.38.lengths
  135.6 0.0 copy-done.3
  135.6 0.0 copy-done.8
  135.6 0.0 copy-start.12
  135.6 0.9 copy-done.12
  136.5 75.0 %attend.1 = (bf16[1024,2048]{1,0:T(8,128)(2,1)}, bf16[1024,2048]{1,0:T(8,128)(2,1)}, bf16[256,2048]{1,0:T(8,128)(2,1)S(1)}, bf16[256,2048]{1,0:T(8,128)(2,1)S(1)...) custom-call(bf16[256,2048]{1,0:T(8,128)(2,1)S(1)} %bitcast.52, ...), custom_call_target="tpu_custom_call" | custom-call | flops 5000000000 | bytes 100000000 | tf_op jit(solution)/shard_map/attend/pallas_call | solution.py:383
  211.5 0.0 copy-start.5
  211.5 1.0 copy-done.5
  212.5 0.0 copy-start.6
  212.5 1.0 copy-done.6
  213.5 0.0 copy-start.7
  213.5 1.0 copy-done.7
  214.4 0.0 copy-start.10
  214.4 0.7 copy-done.10
  215.1 0.0 copy-start.11
  215.1 0.7 copy-done.11
  215.7 0.0 copy-start.9
  215.7 0.0 copy-start.15
  215.7 0.0 copy-start.2
  215.8 17.8 %lift.1 = (bf16[1024,2048]{1,0:T(8,128)(2,1)S(1)}, bf16[1024,2048]{1,0:T(8,128)(2,1)}) custom-call(bf16[1024,2048]{1,0:T(8,128)(2,1)} %get-tuple-element.64.rows.refs_4_, bf16[2048,2048]{1,0:T(8,128)(2,1)} %get-tuple-element.65.weight.refs_5_, f32[1,2048]{1,0:T(1,128)S(1)} %get-tuple-element.66.bias), custom_call_target="tpu_custom_call" | custom-call | tf_op jit(solution)/shard_map/lift/pallas_call | solution.py:1078
  233.6 0.0 copy-start
  233.6 2.0 copy-done
  235.6 0.0 copy-done.15
  235.6 0.0 all-gather.2.cloned.1.call-done.weight.refs_3_
  235.6 0.0 copy-done.9
  235.6 0.0 copy-done.2
  235.6 15.0 %finish_rows.1 = bf16[8,128,2048]{2,1,0:T(8,128)(2,1)} custom-call(s32[8]{0:T(128)S(1)} %broadcast_subtract_fusion.deal, s32[8,4]{1,0:T(8,128)S(1)} %copy.38.lengths, s32[1]{0:T(128)} %bitcast.place, bf16[8,128,2048]{2,1,0:T(8,128)(2,1)} %bitcast.47, bf16[8,128,2048]{2,1,0:T(8,128)(2,1)} %bitcast.48, ...), custom_call_target="tpu_custom_call" | custom-call | tf_op jit(solution)/shard_map/finish_rows/pallas_call | solution.py:1206
  250.6 0.0 reduce-scatter.2.cloned.1.call-update
  250.6 0.1 select_reduce_fusion.order
  250.7 0.0 copy-start.4
  250.7 2.2 copy-done.4
  252.9 2.1 take_rows.1
  255.0 0.0 copy-start.1
  255.0 2.1 copy-done.1
  257.1 304.2 %back_all.1 = (bf16[2,4,256,2048]{3,2,1,0:T(8,128)(2,1)}, bf16[2,4,256,2048]{3,2,1,0:T(8,128)(2,1)}, bf16[2,1,256,2048]{3,2,1,0:T(8,128)(2,1)}, bf16[2,1,256,204...) custom-call(bf16[1024,2048]{1,0:T(8,128)(2,1)} %copy-done, ...), custom_call_target="tpu_custom_call" | custom-call | bytes 200000000 | tf_op jit(solution)/shard_map/back_all/pallas_call | solution.py:1049
  561.3 0.0 copy-start.13
  561.3 22.9 %widen.1 = (f32[2048,2048]{1,0:T(8,128)}, f32[512,8192]{1,0:T(8,128)}, f32[512,2048]{1,0:T(8,128)}, f32[512,2048]{1,0:T(8,128)}, f32[512,256]{1,0:T(8,128)}, /*i...) custom-call(bf16[2048,2048]{1,0:T(8,128)(2,1)} %bitcast.56, ...), custom_call_target="tpu_custom_call" | custom-call | tf_op jit(solution)/shard_map/widen/pallas_call | solution.py:1124
  584.3 1.2 dynamic-slice_bitcast_fusion
  585.5 0.0 reduce-scatter.2.cloned.1.call-done
  585.5 0.0 copy-done.13
  585.5 1.0 copy.42
  (4 shorter events, 0.0 us)
Async XLA Ops:
  7.2 128.3 %copy-start.14 = (s32[8,4]{0,1:T(4,128)S(1)}, s32[8,4]{0,1:T(4,128)}, u32[]{:S(2)}) copy-start(s32[8,4]{0,1:T(4,128)} %param.20) | copy-start | bytes 388
  7.2 128.4 %copy-start.3 = (bf16[2,128,2048]{2,1,0:T(8,128)(2,1)S(1)}, bf16[2,128,2048]{2,1,0:T(8,128)(2,1)}, u32[]{:S(2)}) copy-start(bf16[2,128,2048]{2,1,0:T(8,128)(2,1)} %param.18) | copy-start | bytes 3145732
  7.2 128.4 %copy-start.8 = (bf16[2,128,2048]{2,1,0:T(8,128)(2,1)S(1)}, bf16[2,128,2048]{2,1,0:T(8,128)(2,1)}, u32[]{:S(2)}) copy-start(bf16[2,128,2048]{2,1,0:T(8,128)(2,1)} %param.19) | copy-start | bytes 3145732
  7.2 228.4 %all-gather.2.cloned.1.call-start = ((), (), s32[]{:S(2)}) async-start(), calls=%async_computation.1 | async-start | bytes 9437184 | tf_op jit(solution)/shard_map/all_gather | solution.py:1284
  135.4 450.1 %reduce-scatter.2.cloned.1.call-start = ((), (), s32[]{:S(2)}) async-start(), calls=%async_computation.2 | async-start | bytes 5242880 | tf_op jit(solution)/shard_map/reduce_scatter | solution.py:1301
  135.6 0.9 copy-start.12
  211.5 1.0 copy-start.5
  212.5 1.0 copy-start.6
  213.5 1.0 copy-start.7
  214.4 0.7 copy-start.10
  215.1 0.7 copy-start.11
  215.7 19.8 %copy-start.9 = (f32[16,2048]{1,0:T(8,128)}, f32[16,2048]{1,0:T(8,128)S(1)}, u32[]{:S(2)}) copy-start(f32[16,2048]{1,0:T(8,128)S(1)} %get-tuple-element.70.table.refs_15_) | copy-start | bytes 393220
  215.7 19.8 %copy-start.15 = (s32[8]{0:T(128)S(1)}, s32[8]{0:T(128)}, u32[]{:S(2)}) copy-start(s32[8]{0:T(128)} %param.21) | copy-start | bytes 100
  215.7 19.8 %copy-start.2 = (f32[256,2048]{1,0:T(8,128)S(1)}, f32[256,2048]{1,0:T(8,128)}, u32[]{:S(2)}) copy-start(f32[256,2048]{1,0:T(8,128)} %get-tuple-element.69.refs_8_) | copy-start | bytes 6291460
  233.6 2.0 copy-start
  250.7 2.2 copy-start.4
  255.0 2.1 copy-start.1
  561.3 24.2 %copy-start.13 = (bf16[256,2048]{1,0:T(8,128)(2,1)S(1)}, bf16[256,2048]{1,0:T(8,128)(2,1)}, u32[]{:S(2)}) copy-start(bf16[256,2048]{1,0:T(8,128)(2,1)} %get-tuple-element.78) | copy-start | bytes 3145732
Sparse Core Ops, SparseCore 0:
  135.5 81.3 all-gather.1
  250.7 66.5 reduce-scatter.1

commit v7 on v6

--- a/solution.py
+++ b/solution.py
@@ -14,7 +14,7 @@
 BF = jnp.bfloat16
 F32 = jnp.float32
 MESH = pl.DeviceIdType.MESH
-LAG_MID = 2
+LAG_MID = 1
 LAG_OUT = 6
 BUDGET = 8.0
 TILE_COST = 4.0

time: 604 us -> 604 us (level)
  no operation moved by 1% of the time
where the time goes in v7:
time: 604 us; the launch traced here: 594 us
  Pallas kernels  559 us (93%)
  local copies, waits for them, and re-layouts  19.3 us (3%)
  between operations  14.6 us (2%)
    pallas_call x1, Pallas kernels, back_all(): pl.pallas_call(partial(back_kernel, groups, count, subs, plain, sizes, sh...  305 us
    pallas_call x1, Pallas kernels, gather_all(): pl.pallas_call(partial(gather_kernel, groups, count), out_shape=(tall(wq)...  120 us
    pallas_call x1, Pallas kernels, attend(): pl.pallas_call(partial(attend_kernel, groups, count), out_shape=(shape((c...  75 us
    pallas_call x1, Pallas kernels, widen(): pl.pallas_call(partial(widen_kernel, block, size), out_shape=(shape(*down...  22.9 us
    pallas_call x1, Pallas kernels, lift(): pl.pallas_call(lift_kernel, out_shape=(out, out), grid=(hidden // tile,),...  17.8 us
    pallas_call x1, Pallas kernels, finish_rows(): pl.pallas_call(finish_kernel, out_shape=jax.ShapeDtypeStruct((count, leng...  15 us
    unnamed x34, local copies, waits for them, and re-layouts  12.5 us
  transfers between devices with their start and end apart: 2, of which 0 were waited for; matrix products, arithmetic and copies ran while one was open for 0% of the time, Pallas kernels for 71%

profile of v7, /device:TPU:0, one launch (start us, length us, event | category | flops | bytes accessed | tf_op | source)
XLA Modules:
  0.0 594.2 jit_solution(12823428769178487208)
XLA Ops:
  7.2 0.0 copy-start.14
  7.2 0.0 copy-start.3
  7.2 0.0 copy-start.8
  7.2 0.0 all-gather.2.cloned.1.call-start
  7.3 0.9 fusion
  8.2 0.7 pad_bitcast_fusion.9
  8.8 2.3 cut.1.upc
  11.1 0.7 pad_bitcast_fusion.2
  11.8 0.7 pad_bitcast_fusion.3
  12.5 0.7 pad_bitcast_fusion.5
  13.2 0.7 pad_bitcast_fusion.7
  13.9 0.8 dynamic_update_slice.4
  14.6 1.2 stack.55.small
  15.8 119.5 %gather_all.1 = (bf16[2048,2048]{1,0:T(8,128)(2,1)}, bf16[2048,2048]{1,0:T(8,128)(2,1)}, bf16[2048,256]{1,0:T(8,128)(2,1)}, bf16[512,128]{1,0:T(8,128)(2,1)}, bf16[2048,2048]{1,0:T(8,128)(2,1)}) custom-call(bf16[64,2048]{1,0:T(8,128)(2,1)} %wq.1, bf16[64,2048]{1,0:T(8,128)(2,1)} %wo.1, bf16[64,256]{1,0:T(8,128)(2,1)} %wkv.1, bf16[16,128]{1,0:T(8,128)(2,1)} %stack.55.small, ...), custom_call_target="tpu_custom_call" | custom-call | bytes 100000000 | tf_op jit(solution)/shard_map/gather_all/pallas_call | solution.py:206
  135.4 0.0 all-gather.2.cloned.1.call-update
  135.4 0.0 reduce-scatter.2.cloned.1.call-start
  135.5 0.0 copy-done.14
  135.5 0.1 copy.38.lengths
  135.6 0.0 copy-done.3
  135.6 0.0 copy-done.8
  135.6 0.0 copy-start.12
  135.6 0.9 copy-done.12
  136.5 75.0 %attend.1 = (bf16[1024,2048]{1,0:T(8,128)(2,1)}, bf16[1024,2048]{1,0:T(8,128)(2,1)}, bf16[256,2048]{1,0:T(8,128)(2,1)S(1)}, bf16[256,2048]{1,0:T(8,128)(2,1)S(1)...) custom-call(bf16[256,2048]{1,0:T(8,128)(2,1)S(1)} %bitcast.52, ...), custom_call_target="tpu_custom_call" | custom-call | flops 5000000000 | bytes 100000000 | tf_op jit(solution)/shard_map/attend/pallas_call | solution.py:383
  211.5 0.0 copy-start.5
  211.5 1.0 copy-done.5
  212.5 0.0 copy-start.6
  212.5 1.0 copy-done.6
  213.5 0.0 copy-start.7
  213.5 1.0 copy-done.7
  214.4 0.0 copy-start.10
  214.4 0.7 copy-done.10
  215.1 0.0 copy-start.11
  215.1 0.7 copy-done.11
  215.7 0.0 copy-start.9
  215.7 0.0 copy-start.15
  215.7 0.0 copy-start.2
  215.8 17.8 %lift.1 = (bf16[1024,2048]{1,0:T(8,128)(2,1)S(1)}, bf16[1024,2048]{1,0:T(8,128)(2,1)}) custom-call(bf16[1024,2048]{1,0:T(8,128)(2,1)} %get-tuple-element.64.rows.refs_4_, bf16[2048,2048]{1,0:T(8,128)(2,1)} %get-tuple-element.65.weight.refs_5_, f32[1,2048]{1,0:T(1,128)S(1)} %get-tuple-element.66.bias), custom_call_target="tpu_custom_call" | custom-call | tf_op jit(solution)/shard_map/lift/pallas_call | solution.py:1078
  233.6 0.0 copy-start
  233.6 2.0 copy-done
  235.6 0.0 copy-done.15
  235.6 0.0 all-gather.2.cloned.1.call-done.weight.refs_3_
  235.6 0.0 copy-done.9
  235.6 0.0 copy-done.2
  235.6 15.0 %finish_rows.1 = bf16[8,128,2048]{2,1,0:T(8,128)(2,1)} custom-call(s32[8]{0:T(128)S(1)} %broadcast_subtract_fusion.deal, s32[8,4]{1,0:T(8,128)S(1)} %copy.38.lengths, s32[1]{0:T(128)} %bitcast.place, bf16[8,128,2048]{2,1,0:T(8,128)(2,1)} %bitcast.47, bf16[8,128,2048]{2,1,0:T(8,128)(2,1)} %bitcast.48, ...), custom_call_target="tpu_custom_call" | custom-call | tf_op jit(solution)/shard_map/finish_rows/pallas_call | solution.py:1206
  250.6 0.0 reduce-scatter.2.cloned.1.call-update
  250.6 0.1 select_reduce_fusion.order
  250.7 0.0 copy-start.4
  250.7 2.2 copy-done.4
  252.9 2.1 take_rows.1
  255.0 0.0 copy-start.1
  255.0 2.1 copy-done.1
  257.1 304.7 %back_all.1 = (bf16[2,4,256,2048]{3,2,1,0:T(8,128)(2,1)}, bf16[2,4,256,2048]{3,2,1,0:T(8,128)(2,1)}, bf16[2,1,256,2048]{3,2,1,0:T(8,128)(2,1)}, bf16[2,1,256,204...) custom-call(bf16[1024,2048]{1,0:T(8,128)(2,1)} %copy-done, ...), custom_call_target="tpu_custom_call" | custom-call | bytes 200000000 | tf_op jit(solution)/shard_map/back_all/pallas_call | solution.py:1049
  561.8 0.0 copy-start.13
  561.8 22.9 %widen.1 = (f32[2048,2048]{1,0:T(8,128)}, f32[512,8192]{1,0:T(8,128)}, f32[512,2048]{1,0:T(8,128)}, f32[512,2048]{1,0:T(8,128)}, f32[512,256]{1,0:T(8,128)}, /*i...) custom-call(bf16[2048,2048]{1,0:T(8,128)(2,1)} %bitcast.56, ...), custom_call_target="tpu_custom_call" | custom-call | tf_op jit(solution)/shard_map/widen/pallas_call | solution.py:1124
  584.7 1.2 dynamic-slice_bitcast_fusion
  586.0 0.0 reduce-scatter.2.cloned.1.call-done
  586.0 0.0 copy-done.13
  586.0 1.0 copy.42
  (4 shorter events, 0.0 us)
Async XLA Ops:
  7.2 128.3 %copy-start.14 = (s32[8,4]{0,1:T(4,128)S(1)}, s32[8,4]{0,1:T(4,128)}, u32[]{:S(2)}) copy-start(s32[8,4]{0,1:T(4,128)} %param.20) | copy-start | bytes 388
  7.2 128.4 %copy-start.3 = (bf16[2,128,2048]{2,1,0:T(8,128)(2,1)S(1)}, bf16[2,128,2048]{2,1,0:T(8,128)(2,1)}, u32[]{:S(2)}) copy-start(bf16[2,128,2048]{2,1,0:T(8,128)(2,1)} %param.18) | copy-start | bytes 3145732
  7.2 128.4 %copy-start.8 = (bf16[2,128,2048]{2,1,0:T(8,128)(2,1)S(1)}, bf16[2,128,2048]{2,1,0:T(8,128)(2,1)}, u32[]{:S(2)}) copy-start(bf16[2,128,2048]{2,1,0:T(8,128)(2,1)} %param.19) | copy-start | bytes 3145732
  7.2 228.4 %all-gather.2.cloned.1.call-start = ((), (), s32[]{:S(2)}) async-start(), calls=%async_computation.1 | async-start | bytes 9437184 | tf_op jit(solution)/shard_map/all_gather | solution.py:1284
  135.4 450.6 %reduce-scatter.2.cloned.1.call-start = ((), (), s32[]{:S(2)}) async-start(), calls=%async_computation.2 | async-start | bytes 5242880 | tf_op jit(solution)/shard_map/reduce_scatter | solution.py:1301
  135.6 0.9 copy-start.12
  211.5 1.0 copy-start.5
  212.5 1.0 copy-start.6
  213.5 1.0 copy-start.7
  214.4 0.7 copy-start.10
  215.1 0.7 copy-start.11
  215.7 19.8 %copy-start.9 = (f32[16,2048]{1,0:T(8,128)}, f32[16,2048]{1,0:T(8,128)S(1)}, u32[]{:S(2)}) copy-start(f32[16,2048]{1,0:T(8,128)S(1)} %get-tuple-element.70.table.refs_15_) | copy-start | bytes 393220
  215.7 19.8 %copy-start.15 = (s32[8]{0:T(128)S(1)}, s32[8]{0:T(128)}, u32[]{:S(2)}) copy-start(s32[8]{0:T(128)} %param.21) | copy-start | bytes 100
  215.7 19.8 %copy-start.2 = (f32[256,2048]{1,0:T(8,128)S(1)}, f32[256,2048]{1,0:T(8,128)}, u32[]{:S(2)}) copy-start(f32[256,2048]{1,0:T(8,128)} %get-tuple-element.69.refs_8_) | copy-start | bytes 6291460
  233.6 2.0 copy-start
  250.7 2.2 copy-start.4
  255.0 2.1 copy-start.1
  561.8 24.2 %copy-start.13 = (bf16[256,2048]{1,0:T(8,128)(2,1)S(1)}, bf16[256,2048]{1,0:T(8,128)(2,1)}, u32[]{:S(2)}) copy-start(bf16[256,2048]{1,0:T(8,128)(2,1)} %get-tuple-element.78) | copy-start | bytes 3145732
Sparse Core Ops, SparseCore 0:
  135.5 81.3 all-gather.1
  250.7 66.4 reduce-scatter.1
